TPU v7x, 32 devices: a whole 2x2x4 slice. The times are simulated.
32 devices in a mesh: chain: 2 (over core), energy: 16 (over z, y, x).
Axes of the slice: x: 2, y: 2, z: 4, core: 2. Of those that a mesh axis runs over, the one named last changes fastest.
Arguments:
- retarded: float32 [16, 4, 2, 256, 256], P('energy', 'chain'), may hold values from -0.625 to 0.625
- lesser_sigma: float32 [16, 4, 2, 256, 256], P('energy', 'chain'), may hold values from -6 to 6
- coupling: float32 [4, 2, 256, 256], P('chain'), may hold values from -1 to 1
- coupling_pattern: int32 [4, 4, 4], P('chain'), may hold values from 0 to 1, as said below
- kept_blocks: int32 [4], replicated, may hold values from 0 to 15, as said below
- lead_lesser: float32 [16, 2, 256, 256], P('energy'), may hold values from -8 to 8
Outputs:
- polarization: float32 [16, 2, 65536], P(None, None, ('chain', 'energy'))
Inputs may be any that keep to these rules, and one draw needn't show every extreme that they name: `coupling_pattern`: 0/1 entries; each cell's coupling has exactly 4 ones. `kept_blocks`: distinct block numbers.
All inputs are finite; a program needn't handle non-finite values.
Results may differ from a plain program's by a relative error of at most 0.0001.
Values sent between devices are 32-bit elements; how exact they have to be, the bound alone decides.
No kernel may reach another device: no remote copies, remote signals or barrier semaphores. Data moves between devices by JAX's collectives and lax.ppermute only.
A program may use at most 832 MiB of HBM per device.

v0:
```python
import jax
import jax.numpy as jnp
from jax import lax
from jax.sharding import PartitionSpec as P

M = 256
BLOCK = 64
NBLK = 4
KEEP = 4
LAGS = 16


def passed_along(value, axis, steps):
    count = lax.axis_size(axis)
    leading, last = (max(0, -steps), min(count, count - steps))
    return lax.ppermute(value, axis, [(source, source + steps) for source in range(leading, last)])


def times_plain(left, right):
    return jnp.einsum("...ij,...jk->...ik", left, right, precision=lax.Precision.HIGHEST)


def times_transposed(left, right):
    return jnp.einsum("...ij,...kj->...ik", left, right, precision=lax.Precision.HIGHEST)


def complex_product(left, right):
    left_re, left_im = (left[..., 0, :, :], left[..., 1, :, :])
    right_re, right_im = (right[..., 0, :, :], right[..., 1, :, :])
    first = times_plain(left_re, right_re)
    second = times_plain(left_im, right_im)
    mixed = times_plain(left_re + left_im, right_re + right_im)
    return jnp.stack([first - second, mixed - first - second], axis=-3)


def product_adjoint(left, right):
    left_re, left_im = (left[..., 0, :, :], left[..., 1, :, :])
    right_re, right_im = (right[..., 0, :, :], right[..., 1, :, :])
    first = times_transposed(left_re, right_re)
    second = times_transposed(left_im, right_im)
    mixed = times_transposed(left_re + left_im, right_re - right_im)
    return jnp.stack([first + second, mixed - first + second], axis=-3)


def expand_pattern(pattern):
    return jnp.repeat(jnp.repeat(pattern.astype(jnp.float32), BLOCK, axis=-2), BLOCK, axis=-1)


def pick_blocks(matrix, kept_blocks):
    lead_shape = matrix.shape[:-2]
    tiles = matrix.reshape(lead_shape + (NBLK, BLOCK, NBLK, BLOCK))
    tiles = jnp.swapaxes(tiles, -3, -2)
    tiles = tiles.reshape(lead_shape + (NBLK * NBLK, BLOCK * BLOCK))
    return jnp.take(tiles, kept_blocks, axis=-2)


def per_device(retarded, lesser_sigma, coupling, coupling_pattern, kept_blocks, lead_lesser):
    energies_here = retarded.shape[0]
    cell_count = retarded.shape[1]
    span_width = cell_count * KEEP * BLOCK * BLOCK
    coupling_full = coupling * expand_pattern(coupling_pattern)[:, None]
    joined_all = complex_product(retarded, coupling_full[None])
    fresh_all = product_adjoint(complex_product(retarded, lesser_sigma), retarded)
    position = lax.axis_index("chain")
    length = lax.axis_size("chain")

    def advance(state_in, per_group):
        pieces = []
        for cell_index in range(cell_count):
            bridge = joined_all[:, cell_index]
            state_in = fresh_all[:, cell_index] + product_adjoint(
                complex_product(bridge, state_in), bridge
            )
            pieces.append(pick_blocks(state_in, kept_blocks))
        stacked = jnp.stack(pieces, axis=2)
        return (state_in, stacked.reshape(per_group, 2, span_width))

    def send_whole(leaving):
        return passed_along(leaving, "chain", 1)

    per_group = energies_here // 1
    tick_total = 1 + length - 1
    buffer = jnp.zeros((energies_here, 2, span_width), jnp.float32)

    def tick(tick_index, state):
        incoming, buffer = state
        micro_batch = tick_index - position
        active = jnp.logical_and(micro_batch >= 0, micro_batch < 1)
        batch_slot = jnp.clip(micro_batch, 0, 1 - 1)
        offset = batch_slot * per_group
        entering = jnp.where(position == 0, lead_lesser, incoming)

        def working(operands):
            entering_now, buffer_now = operands
            leaving, retained = advance(entering_now, per_group)
            return (leaving, lax.dynamic_update_slice_in_dim(buffer_now, retained, offset, 0))

        def waiting(operands):
            entering_now, buffer_now = operands
            return (jnp.zeros_like(entering_now), buffer_now)

        leaving, buffer = lax.cond(active, working, waiting, (entering, buffer))
        return (send_whole(leaving), buffer)

    initial = (jnp.zeros((per_group, 2, M, M), jnp.float32), buffer)
    _, buffer = lax.fori_loop(0, tick_total, tick, initial)
    retained = buffer
    owners = lax.all_to_all(retained, "energy", split_axis=2, concat_axis=0, tiled=True)
    energy_total = owners.shape[0]
    results = []
    for lag_index in range(LAGS):
        shifted = owners[lag_index:]
        earlier = owners[: energy_total - lag_index]
        real_part = jnp.sum(shifted[:, 0] * earlier[:, 0] + shifted[:, 1] * earlier[:, 1], axis=0)
        imag_part = jnp.sum(shifted[:, 1] * earlier[:, 0] - shifted[:, 0] * earlier[:, 1], axis=0)
        results.append(jnp.stack([real_part, imag_part], axis=0))
    return jnp.stack(results, axis=0) / jnp.float32(energy_total)


def solution(mesh):
    return jax.shard_map(
        per_device,
        mesh=mesh,
        in_specs=(
            P("energy", "chain", None, None, None),
            P("energy", "chain", None, None, None),
            P("chain", None, None, None),
            P("chain", None, None),
            P(),
            P("energy", None, None, None),
        ),
        out_specs=P(None, None, ("chain", "energy")),
        check_vma=False,
    )
```

profile of v0, /device:TPU:1, one launch (start us, length us, event | category | flops | bytes accessed | tf_op | source)
XLA Modules:
  0.0 344.7 jit_solution(7181016075374133400)
XLA Ops:
  0.0 1.9 fusion.78
  1.9 1.9 fusion.71
  3.8 2.2 fusion.70
  6.1 1.7 fusion.82
  7.8 1.7 fusion.74
  9.5 2.0 fusion.69
  12.5 1.6 copy.76
  15.6 1.5 fusion.67
  19.4 1.3 copy.80
  20.9 75.2 %while.19 = (s32[]{:T(128)}, f32[1,2,256,256]{3,2,1,0:T(8,128)S(1)}, f32[1,2,32768]{2,1,0:T(2,128)S(1)}, s32[]{:T(128)}, f32[1,2,2,256,256]{4,3,2,1,0:T(8,128)S(...) while((s32[]{:T(128)}, ...), condition=%wide.region_3.0_spmd, body=%wide.region_0.4_spmd.sunk | while | flops 2418672640 | bytes 42996096 | solution.py:106
  23.3 29.4 %collective-permute-done = f32[1,2,256,256]{3,2,1,0:T(8,128)S(1)} collective-permute-done((f32[1,2,256,256]{3,2,1,0:T(8,128)}, f32[1,2,256,256]{3,2,1,0:T(8,128)S(1)}, u32[]{:S(2)}, u32[]{:S(2)}) %collective-permute-start) | collective-permute-done | bytes 524320 | tf_op jit(solution)/shard_map/while/body/eval_jaxpr/ppermute | solution.py:16
  52.7 27.6 %conditional.2 = (f32[1,2,256,256]{3,2,1,0:T(8,128)}, f32[1,2,32768]{2,1,0:T(2,128)S(1)}) conditional(s32[]{:T(128)} %convert_element_type.13, f32[1,2,32768]{2,1,0:T(2,128)S(1)} %get-tuple-element.393, (f32[1,2,2,256,256]{4,3,2,1,0:T(8,128)S(1)}, pred[]{:T(512)}, f32[1,2,256,256]{3,2,1,0:T(8,128)}, f32[1,2,256,256]{3,2,1,0:T(8,128)S(1)}, ...), branch_computations={%region_1.1_spmd, %region_2.3_spmd} | conditional | flops 2418672640 | bytes 40898708 | solution.py:102
  61.4 1.9 copy.64
  64.3 1.9 copy.63
  69.7 1.4 fusion.4
  75.7 1.5 squeeze.13
  77.2 1.4 fusion.5
  81.6 2.7 collective-permute-done
  96.0 23.9 %copy.81 = f32[1,2,32768]{1,0,2:T(1,128)} copy(f32[1,2,32768]{2,1,0:T(2,128)S(1)} %get-tuple-element.218) | data formatting | bytes 524288 | tf_op jit(solution)/shard_map/while | solution.py:106
  120.4 146.5 %reduce.30 = f32[32768,2]{1,0:T(8,128)} reduce(f32[32768,1,2]{2,1,0:T(1,128)} %bitcast.396, f32[]{:T(128)} %broadcast.60), dimensions={1}, to_apply=%bitcast.355.reduce_sub_computation | reduce | bytes 524292
  266.9 13.7 %reshape.719 = f32[16,1,4096]{2,1,0:T(1,128)S(1)} reshape(f32[32768,2]{1,0:T(8,128)} %reduce.30) | data formatting | bytes 524288
  280.7 16.7 %all_to_all.18 = f32[16,1,4096]{2,1,0:T(1,128)S(1)} all-to-all(f32[16,1,4096]{2,1,0:T(1,128)S(1)} %reshape.719), channel_id=1, replica_groups=mesh['chain'=2,'energy'=16] {'energy'}, dimensions={0} | all-to-all | bytes 524288 | tf_op jit(solution)/shard_map/all_to_all | solution.py:108
  298.6 29.3 %reshape.720 = f32[32768,1,2]{2,1,0:T(1,128)} reshape(f32[16,4096]{1,0:T(8,128)S(1)} %reduce.31) | data formatting | bytes 524288
  328.0 10.2 %copy.82 = f32[1,2,16,2048]{3,1,0,2:T(2,128)S(1)} copy(f32[1,2,16,2048]{1,3,2,0:T(8,128)} %bitcast.397) | data formatting | bytes 524288 | tf_op jit(solution)/shard_map/all_to_all | solution.py:108
  (124 shorter events, 36.2 us)
Async XLA Ops:
  0.0 14.3 %copy-start.1 = (f32[1,2,2,256,256]{4,3,2,1,0:T(8,128)S(1)}, f32[1,2,2,256,256]{4,3,2,1,0:T(8,128)}, u32[]{:S(2)}) copy-start(f32[1,2,2,256,256]{4,3,2,1,0:T(8,128)} %param.12) | copy-start | bytes 3145732
  3.8 17.1 %copy-start.2 = (s32[4]{0:T(128)S(1)}, s32[4]{0:T(128)}, u32[]{:S(2)}) copy-start(s32[4]{0:T(128)} %param.16) | copy-start | bytes 52
  22.0 30.7 %collective-permute-start = (f32[1,2,256,256]{3,2,1,0:T(8,128)}, f32[1,2,256,256]{3,2,1,0:T(8,128)S(1)}, u32[]{:S(2)}, u32[]{:S(2)}) collective-permute-start(f32[1,2,256,256]{3,2,1,0:T(8,128)} %get-tuple-element.374), channel_id=1, source_target_pairs={{0,16},{1,17},{2,18},{3,19},{4,20},{5,21},{6,22},{7,23},{8,24},{9,... | collective-permute-start | bytes 1572872 | tf_op jit(solution)/shard_map/while/body/eval_jaxpr/ppermute | solution.py:16
  66.8 2.4 copy-start
  80.3 4.0 %collective-permute-start = (f32[1,2,256,256]{3,2,1,0:T(8,128)}, f32[1,2,256,256]{3,2,1,0:T(8,128)S(1)}, u32[]{:S(2)}, u32[]{:S(2)}) collective-permute-start(f32[1,2,256,256]{3,2,1,0:T(8,128)} %get-tuple-element.374), channel_id=1, source_target_pairs={{0,16},{1,17},{2,18},{3,19},{4,20},{5,21},{6,22},{7,23},{8,24},{9,... | collective-permute-start | bytes 1572872 | tf_op jit(solution)/shard_map/while/body/eval_jaxpr/ppermute | solution.py:16
where the time goes:
time: 347 us; the launch traced here: 345 us
  other arithmetic  161 us (46%)
  local copies, waits for them, and re-layouts  98.2 us (28%)
  waiting for transfers between devices  32.2 us (9%)
  matrix products  21.4 us (6%)
  blocking collectives  16.7 us (5%)
  loops' own time  12.2 us (4%)
    unnamed x16, other arithmetic  147 us
    unnamed x8, local copies, waits for them, and re-layouts  45.2 us
    ppermute x2, waiting for transfers between devices, passed_along(): lax.ppermute(value, axis, [(source, source + steps) for source in range(l...  32.2 us
    while x3, local copies, waits for them, and re-layouts, per_device(): _, buffer = lax.fori_loop(0, tick_total, tick, initial)  25.3 us
    all_to_all x1, blocking collectives, per_device(): lax.all_to_all(retained, 'energy', split_axis=2, concat_axis=0, tiled=True)  16.7 us
    dot_general x12, matrix products, times_plain(): jnp.einsum('...ij,...jk->...ik', left, right, precision=lax.Precision.HIG...  12.4 us
    another operation x1, loops' own time, per_device(): _, buffer = lax.fori_loop(0, tick_total, tick, initial)  12 us
    all_to_all x1, local copies, waits for them, and re-layouts, per_device(): lax.all_to_all(retained, 'energy', split_axis=2, concat_axis=0, tiled=True)  10.2 us
  transfers between devices with their start and end apart: 2, of which 2 were waited for; matrix products, arithmetic and copies ran while one was open for 0% of the time, Pallas kernels for 0%

commit v1 on v0

v1 whole, which is shorter than its diff:
```python
import functools

import jax
import jax.numpy as jnp
from jax import lax
from jax.experimental import pallas as pl
from jax.experimental.pallas import tpu as pltpu
from jax.sharding import PartitionSpec as P

BLOCK = 64
LAGS = 16
LANES = 128
F32 = jnp.float32
BF16 = jnp.bfloat16


def two_parts(value):
    high = value.astype(BF16)
    return high, (value - high.astype(F32)).astype(BF16)


def as_left(stacked):
    high, low = stacked
    return jnp.concatenate([high, high, low], axis=1)


def combined(product, conjugate):
    m, n = product.shape[0] // 2, product.shape[1] // 2
    rr, ri = product[:m, :n], product[:m, n:]
    ir, ii = product[m:, :n], product[m:, n:]
    if conjugate:
        return rr + ii, ir - ri
    return rr - ii, ri + ir


def complex_product(left, right):
    high, low = right
    wide = jnp.concatenate([high, low, high], axis=0)
    product = lax.dot_general(as_left(left), wide, (((1,), (0,)), ((), ())), preferred_element_type=F32)
    return combined(product, False)


def product_adjoint(left, right):
    high, low = right
    tall = jnp.concatenate([high, low, high], axis=1)
    product = lax.dot_general(as_left(left), tall, (((1,), (1,)), ((), ())), preferred_element_type=F32)
    return combined(product, True)


def above(pair):
    return two_parts(jnp.concatenate(pair, axis=0))


def beside(pair):
    return two_parts(jnp.concatenate(pair, axis=1))


def beside_of(stacked):
    m = stacked[0].shape[0] // 2
    return tuple(jnp.concatenate([part[:m], part[m:]], axis=1) for part in stacked)


def put_state(state_ref, pair):
    for part in range(2):
        for group in range(state_ref.shape[1]):
            state_ref[part, group] = pair[part][:, group * LANES:(group + 1) * LANES]


def get_state(state_ref):
    groups = range(state_ref.shape[1])
    return tuple(jnp.concatenate([state_ref[part, group] for group in groups], axis=1) for part in range(2))


def block_mask(pattern_ref, cell, size):
    nblk = size // BLOCK
    column = lax.broadcasted_iota(jnp.int32, (BLOCK, size), 1) // BLOCK
    rows = []
    for r in range(nblk):
        row = jnp.zeros((BLOCK, size), F32)
        for c in range(nblk):
            row = jnp.where(column == c, pattern_ref[cell, r, c].astype(F32), row)
        rows.append(row)
    return jnp.concatenate(rows, axis=0)


def pick_into(send_ref, e, cell, matrix_ref, kept_ref, keep, share_rows):
    nblk = matrix_ref.shape[-2] // BLOCK
    half = BLOCK // 2
    lane = lax.broadcasted_iota(jnp.int32, (half, LANES), 1)
    piece = min(half, share_rows)
    for k in range(keep):
        number = kept_ref[k]
        top = (number // nblk) * BLOCK
        across = (number % nblk) * BLOCK
        window = across // LANES
        in_upper = jnp.full((half, LANES), across % LANES, jnp.int32) > 0
        for part in range(2):
            even = matrix_ref[part, window, pl.ds(top, half, 2), :]
            odd = matrix_ref[part, window, pl.ds(top + 1, half, 2), :]
            left = jnp.where(in_upper, pltpu.roll(even, BLOCK, 1), even)
            right = jnp.where(in_upper, odd, pltpu.roll(odd, BLOCK, 1))
            flat = jnp.where(lane < BLOCK, left, right)
            first = (cell * keep + k) * half
            for s in range(0, half, piece):
                owner, inside = divmod(first + s, share_rows)
                send_ref[e, owner, pl.ds(part * share_rows + inside, piece), :] = flat[s:s + piece]


def head_kernel(keep, share_rows, g_hbm, s_hbm, b_hbm, pattern_ref, kept_ref, lead_hbm,
                leaving_hbm, send_hbm, joined_hbm, fresh_hbm,
                g_ref, s_ref, b_ref, lead_ref, state_ref, send_ref, joined_ref, fresh_ref, in_sems, out_sems):
    energies, cells, _, size, _ = g_ref.shape
    position = lax.axis_index("chain")

    def fetch(slot, source, target):
        return pltpu.make_async_copy(source, target, in_sems.at[slot])

    lead_copy = fetch(0, lead_hbm, lead_ref)
    b_copies = [fetch(1 + i, b_hbm.at[i], b_ref.at[i]) for i in range(cells)]
    g_copies = [fetch(1 + cells + i, g_hbm.at[:, i], g_ref.at[:, i]) for i in range(cells)]
    s_copies = [fetch(1 + 2 * cells + i, s_hbm.at[:, i], s_ref.at[:, i]) for i in range(cells)]

    @pl.when(position == 0)
    def _():
        lead_copy.start()

    for i in range(cells):
        b_copies[i].start()
        g_copies[i].start()
        s_copies[i].start()

    def masked(i):
        mask = block_mask(pattern_ref, i, size)
        return b_ref[i, 0] * mask, b_ref[i, 1] * mask

    @pl.when(position == 0)
    def _():
        lead_copy.wait()
        for i in range(cells):
            b_copies[i].wait()
            bridge = above(masked(i))
            for e in range(energies):
                if i == 0:
                    state = (lead_ref[e, 0], lead_ref[e, 1])
                else:
                    state = get_state(state_ref.at[e])
                re, im = product_adjoint(above(complex_product(bridge, beside(state))), bridge)
                if e == 0:
                    s_copies[i].wait()
                    g_copies[i].wait()
                inner = beside((s_ref[e, i, 0] + re, s_ref[e, i, 1] + im))
                green = above((g_ref[e, i, 0], g_ref[e, i, 1]))
                re, im = product_adjoint(above(complex_product(green, inner)), green)
                put_state(state_ref.at[e], (re, im))
                if i == cells - 1 and e == energies - 1:
                    pltpu.make_async_copy(state_ref, leaving_hbm, out_sems.at[0]).start()
                pick_into(send_ref, e, i, state_ref.at[e], kept_ref, keep, share_rows)
        send_copy = pltpu.make_async_copy(send_ref, send_hbm, out_sems.at[1])
        send_copy.start()
        pltpu.make_async_copy(state_ref, leaving_hbm, out_sems.at[0]).wait()
        send_copy.wait()

    @pl.when(position > 0)
    def _():
        copies = []
        for i in range(cells):
            b_copies[i].wait()
            bridge = beside(masked(i))
            g_copies[i].wait()
            s_copies[i].wait()
            for e in range(energies):
                green = above((g_ref[e, i, 0], g_ref[e, i, 1]))
                joined = above(complex_product(green, bridge))
                joined_ref[e, i, 0] = joined[0]
                joined_ref[e, i, 1] = joined[1]
                inner = beside((s_ref[e, i, 0], s_ref[e, i, 1]))
                re, im = product_adjoint(above(complex_product(green, inner)), green)
                fresh_ref[e, i, 0] = re
                fresh_ref[e, i, 1] = im
            for out, (source, target) in enumerate(((joined_ref, joined_hbm), (fresh_ref, fresh_hbm))):
                copy = pltpu.make_async_copy(source.at[:, i], target.at[:, i], out_sems.at[2 + 2 * i + out])
                copy.start()
                copies.append(copy)
        for copy in copies:
            copy.wait()


def head(keep, share_rows, owners, retarded, lesser_sigma, coupling, pattern, kept_blocks, lead):
    energies, cells, _, size, _ = retarded.shape
    hbm = pl.BlockSpec(memory_space=pltpu.HBM)
    smem = pl.BlockSpec(memory_space=pltpu.SMEM)
    state_shape = (energies, 2, size // LANES, size, LANES)
    send_shape = (energies, owners, 2 * share_rows, LANES)
    joined_shape = (energies, cells, 2, 2 * size, size)
    fresh_shape = (energies, cells, 2, size, size)
    return pl.pallas_call(
        functools.partial(head_kernel, keep, share_rows),
        out_shape=(
            jax.ShapeDtypeStruct(state_shape, F32),
            jax.ShapeDtypeStruct(send_shape, F32),
            jax.ShapeDtypeStruct(joined_shape, BF16),
            jax.ShapeDtypeStruct(fresh_shape, F32),
        ),
        in_specs=[hbm, hbm, hbm, smem, smem, hbm],
        out_specs=(hbm, hbm, hbm, hbm),
        scratch_shapes=[
            pltpu.VMEM(retarded.shape, F32),
            pltpu.VMEM(lesser_sigma.shape, F32),
            pltpu.VMEM(coupling.shape, F32),
            pltpu.VMEM(lead.shape, F32),
            pltpu.VMEM(state_shape, F32),
            pltpu.VMEM(send_shape, F32),
            pltpu.VMEM(joined_shape, BF16),
            pltpu.VMEM(fresh_shape, F32),
            pltpu.SemaphoreType.DMA((1 + 3 * cells,)),
            pltpu.SemaphoreType.DMA((2 + 2 * cells,)),
        ],
        compiler_params=pltpu.CompilerParams(vmem_limit_bytes=32 << 20),
        name="head_cells",
    )(retarded, lesser_sigma, coupling, pattern, kept_blocks, lead)


def tail_kernel(keep, share_rows, hop, incoming_hbm, joined_hbm, fresh_hbm, kept_ref, leaving_in, send_in,
                leaving_hbm, send_hbm, state_ref, joined_ref, fresh_ref, send_ref, in_sems, out_sems):
    energies, cells, _, size, _ = fresh_ref.shape

    @pl.when(lax.axis_index("chain") == hop + 1)
    def _():
        state_copy = pltpu.make_async_copy(incoming_hbm, state_ref, in_sems.at[0])
        state_copy.start()
        copies = []
        for i in range(cells):
            pair = (
                pltpu.make_async_copy(joined_hbm.at[:, i], joined_ref.at[:, i], in_sems.at[1 + 2 * i]),
                pltpu.make_async_copy(fresh_hbm.at[:, i], fresh_ref.at[:, i], in_sems.at[2 + 2 * i]),
            )
            for copy in pair:
                copy.start()
            copies.append(pair)
        state_copy.wait()
        for i in range(cells):
            for copy in copies[i]:
                copy.wait()
            for e in range(energies):
                joined = (joined_ref[e, i, 0], joined_ref[e, i, 1])
                state = beside(get_state(state_ref.at[e]))
                re, im = product_adjoint(above(complex_product(joined, state)), joined)
                put_state(state_ref.at[e], (fresh_ref[e, i, 0] + re, fresh_ref[e, i, 1] + im))
                pick_into(send_ref, e, i, state_ref.at[e], kept_ref, keep, share_rows)
        send_copy = pltpu.make_async_copy(send_ref, send_hbm, out_sems.at[0])
        send_copy.start()
        leaving_copy = pltpu.make_async_copy(state_ref, leaving_hbm, out_sems.at[1])
        leaving_copy.start()
        send_copy.wait()
        leaving_copy.wait()


def tail(keep, share_rows, hop, incoming, joined, fresh, kept_blocks, leaving, send):
    cells = fresh.shape[1]
    hbm = pl.BlockSpec(memory_space=pltpu.HBM)
    smem = pl.BlockSpec(memory_space=pltpu.SMEM)
    return pl.pallas_call(
        functools.partial(tail_kernel, keep, share_rows, hop),
        out_shape=(
            jax.ShapeDtypeStruct(leaving.shape, F32),
            jax.ShapeDtypeStruct(send.shape, F32),
        ),
        in_specs=[hbm, hbm, hbm, smem, hbm, hbm],
        out_specs=(hbm, hbm),
        input_output_aliases={4: 0, 5: 1},
        scratch_shapes=[
            pltpu.VMEM(incoming.shape, F32),
            pltpu.VMEM(joined.shape, BF16),
            pltpu.VMEM(fresh.shape, F32),
            pltpu.VMEM(send.shape, F32),
            pltpu.SemaphoreType.DMA((1 + 2 * cells,)),
            pltpu.SemaphoreType.DMA((2,)),
        ],
        compiler_params=pltpu.CompilerParams(vmem_limit_bytes=32 << 20),
        name="tail_cells",
    )(incoming, joined, fresh, kept_blocks, leaving, send)


def lag_kernel(in_ref, out_ref):
    energies, double_rows, _ = in_ref.shape
    rows = double_rows // 2
    step = min(8, rows)
    scale = 1.0 / energies
    for first in range(0, rows, step):
        re = [in_ref[e, first:first + step] for e in range(energies)]
        im = [in_ref[e, rows + first:rows + first + step] for e in range(energies)]
        for lag in range(LAGS):
            real_sum = jnp.zeros((step, LANES), F32)
            imag_sum = jnp.zeros((step, LANES), F32)
            for e in range(energies - lag):
                real_sum += re[e + lag] * re[e] + im[e + lag] * im[e]
                imag_sum += im[e + lag] * re[e] - re[e + lag] * im[e]
            out_ref[lag, pl.ds(2 * first, step, 2), :] = real_sum * scale
            out_ref[lag, pl.ds(2 * first + 1, step, 2), :] = imag_sum * scale


def lag_sums(owned):
    energies, double_rows, lanes = owned.shape
    rows = double_rows // 2
    sums = pl.pallas_call(
        lag_kernel,
        out_shape=jax.ShapeDtypeStruct((LAGS, double_rows, lanes), F32),
        name="lag_sums",
    )(owned)
    sums = sums.reshape(LAGS, rows, 2, lanes)
    return jnp.swapaxes(sums, 1, 2).reshape(LAGS, 2, rows * lanes)


def per_device(retarded, lesser_sigma, coupling, coupling_pattern, kept_blocks, lead_lesser):
    energies_here, cells = retarded.shape[:2]
    keep = kept_blocks.shape[0]
    owners = lax.axis_size("energy")
    length = lax.axis_size("chain")
    share_rows = cells * keep * BLOCK * BLOCK // (owners * LANES)
    leaving, send, joined, fresh = head(
        keep, share_rows, owners, retarded, lesser_sigma, coupling, coupling_pattern, kept_blocks, lead_lesser
    )
    for hop in range(length - 1):
        incoming = lax.ppermute(leaving, "chain", [(hop, hop + 1)])
        leaving, send = tail(keep, share_rows, hop, incoming, joined, fresh, kept_blocks, leaving, send)
    owned = lax.all_to_all(send, "energy", split_axis=1, concat_axis=0, tiled=True)
    return lag_sums(owned.reshape((-1,) + owned.shape[2:]))


def solution(mesh):
    return jax.shard_map(
        per_device,
        mesh=mesh,
        in_specs=(
            P("energy", "chain", None, None, None),
            P("energy", "chain", None, None, None),
            P("chain", None, None, None),
            P("chain", None, None),
            P(),
            P("energy", None, None, None),
        ),
        out_specs=P(None, None, ("chain", "energy")),
        check_vma=False,
    )
```

time: 347 us -> 39.9 us (0.11)
  other arithmetic: 161 us -> 0 us
  local copies, waits for them, and re-layouts: 98.2 us -> 6.05 us
  waiting for transfers between devices: 32.2 us -> 5.07 us
  matrix products: 21.4 us -> 0 us
  loops' own time: 12.2 us -> 0 us
  Pallas kernels: 0 us -> 11.7 us
    unnamed x16 -> x0, other arithmetic: 147 us -> none
    unnamed x8 -> x12, local copies, waits for them, and re-layouts: 45.2 us -> 6.05 us
    ppermute x2 -> x1, waiting for transfers between devices: 32.2 us -> 5.07 us  [per_device(): incoming = lax.ppermute(leaving, 'chain', [(hop, hop + 1)])]
    while x3 -> x0, local copies, waits for them, and re-layouts: 25.3 us -> none  [per_device(): _, buffer = lax.fori_loop(0, tick_total, tick, initial)]
    dot_general x21 -> x0, matrix products: 21.4 us -> none  [the longest x12 12.4 us: times_plain(): jnp.einsum('...ij,...jk->...ik', left, right, precision=lax.Precision.HIG...]
    another operation x3 -> x0, loops' own time: 12.2 us -> none  [the longest x1 12 us: per_device(): _, buffer = lax.fori_loop(0, tick_total, tick, initial)]
    pallas_call x0 -> x3, Pallas kernels: none -> 11.7 us  [the longest x1 5.02 us: head(): pl.pallas_call(functools.partial(head_kernel, keep, share_rows), out_shap...]
    all_to_all x1 -> x0, local copies, waits for them, and re-layouts: 10.2 us -> none  [per_device(): lax.all_to_all(retained, 'energy', split_axis=2, concat_axis=0, tiled=True)]
  transfers between devices with their start and end apart: 2 -> 1, of which waited for: 2 -> 1; matrix products, arithmetic and copies ran while one was open for 0% -> 0% of each run, Pallas kernels for 0% -> 0%
where the time goes in v1:
time: 39.9 us; the launch traced here: 39.5 us
  blocking collectives  15.3 us (38%)
  Pallas kernels  11.7 us (29%)
  local copies, waits for them, and re-layouts  6.05 us (15%)
  waiting for transfers between devices  5.07 us (13%)
  starting transfers between devices  1.29 us (3%)
    all_to_all x1, blocking collectives, per_device(): lax.all_to_all(send, 'energy', split_axis=1, concat_axis=0, tiled=True)  15.3 us
    unnamed x12, local copies, waits for them, and re-layouts  6.05 us
    ppermute x1, waiting for transfers between devices, per_device(): incoming = lax.ppermute(leaving, 'chain', [(hop, hop + 1)])  5.07 us
    pallas_call x1, Pallas kernels, head(): pl.pallas_call(functools.partial(head_kernel, keep, share_rows), out_shap...  5.02 us
    pallas_call x1, Pallas kernels, tail(): pl.pallas_call(functools.partial(tail_kernel, keep, share_rows, hop), out...  4.78 us
    pallas_call x1, Pallas kernels, lag_sums(): pl.pallas_call(lag_kernel, out_shape=jax.ShapeDtypeStruct((LAGS, double_r...  1.94 us
    ppermute x1, starting transfers between devices, per_device(): incoming = lax.ppermute(leaving, 'chain', [(hop, hop + 1)])  1.29 us
  transfers between devices with their start and end apart: 1, of which 1 were waited for; matrix products, arithmetic and copies ran while one was open for 0% of the time, Pallas kernels for 0%

profile of v1, /device:TPU:1, one launch (start us, length us, event | category | flops | bytes accessed | tf_op | source)
XLA Modules:
  0.0 39.5 jit_solution(4755279138518149549)
XLA Ops:
  0.0 0.0 copy-start
  0.0 1.2 %copy-done = f32[1,2,2,256,256]{4,3,2,1,0:T(8,128)S(1)} copy-done((f32[1,2,2,256,256]{4,3,2,1,0:T(8,128)S(1)}, f32[1,2,2,256,256]{4,3,2,1,0:T(8,128)}, u32[]{:S(2)}) %copy-start) | copy-done | bytes 1048600
  1.2 0.0 copy-start.1
  1.2 1.2 %copy-done.1 = f32[1,2,2,256,256]{4,3,2,1,0:T(8,128)S(1)} copy-done((f32[1,2,2,256,256]{4,3,2,1,0:T(8,128)S(1)}, f32[1,2,2,256,256]{4,3,2,1,0:T(8,128)}, u32[]{:S(2)}) %copy-start.1) | copy-done | bytes 1048600
  2.5 0.0 copy-start.2
  2.5 1.2 %copy-done.2 = f32[2,2,256,256]{3,2,1,0:T(8,128)S(1)} copy-done((f32[2,2,256,256]{3,2,1,0:T(8,128)S(1)}, f32[2,2,256,256]{3,2,1,0:T(8,128)}, u32[]{:S(2)}) %copy-start.2) | copy-done | bytes 1048600
  3.7 0.0 copy-start.3
  3.7 1.0 %copy-done.3 = f32[1,2,256,256]{3,2,1,0:T(8,128)S(1)} copy-done((f32[1,2,256,256]{3,2,1,0:T(8,128)S(1)}, f32[1,2,256,256]{3,2,1,0:T(8,128)}, u32[]{:S(2)}) %copy-start.3) | copy-done | bytes 524312
  4.7 0.0 copy-start.4
  4.7 0.7 %copy-done.4 = s32[2,4,4]{2,1,0:T(4,128)S(1)} copy-done((s32[2,4,4]{2,1,0:T(4,128)S(1)}, s32[2,4,4]{2,1,0:T(4,128)}, u32[]{:S(2)}) %copy-start.4) | copy-done | bytes 152
  5.4 0.0 copy-start.5
  5.4 0.7 %copy-done.5 = s32[4]{0:T(128)S(1)} copy-done((s32[4]{0:T(128)S(1)}, s32[4]{0:T(128)}, u32[]{:S(2)}) %copy-start.5) | copy-done | bytes 40
  6.1 5.0 %head_cells.1 = (f32[1,2,2,256,128]{4,3,2,1,0:T(8,128)S(1)}, f32[1,16,32,128]{3,2,1,0:T(8,128)S(1)}, bf16[1,2,2,512,256]{4,3,2,1,0:T(8,128)(2,1)S(1)}, f32[1,2,2,256,256]{4,3,2,1,0:T(8,128)S(1)}) custom-call(f32[1,2,2,256,256]{4,3,2,1,0:T(8,128)S(1)} %copy-done, f32[1,2,2,256,256]{4,3,2,1,0:T(8,128)S(1)} %copy-done.1, f32[2,2,256,256]{3,2,1,0:T(8,128)S(1)} %copy-done.2, ...), custom_call_target="tpu_custom_call" | custom-call | tf_op jit(solution)/shard_map/head_cells/pallas_call | solution.py:196
  11.1 1.3 %collective-permute-start = (f32[1,2,2,256,128]{4,3,2,1,0:T(8,128)S(1)}, f32[1,2,2,256,128]{4,3,2,1,0:T(8,128)S(1)}, u32[]{:S(2)}, u32[]{:S(2)}) collective-permute-start(f32[1,2,2,256,128]{4,3,2,1,0:T(8,128)S(1)} %get-tuple-element.10.leaving_in), channel_id=1, source_target_pairs={{0,16},{1,17},{2,18},{3,19},{4,20},{5,21},{6,22},{7,23},{8,24},{9,... | collective-permute-start | bytes 1572872 | tf_op jit(solution)/shard_map/ppermute | solution.py:324
  12.4 5.1 %collective-permute-done.incoming_hbm = f32[1,2,2,256,128]{4,3,2,1,0:T(8,128)S(1)} collective-permute-done((f32[1,2,2,256,128]{4,3,2,1,0:T(8,128)S(1)}, f32[1,2,2,256,128]{4,3,2,1,0:T(8,128)S(1)}, u32[]{:S(2)}, u32[]{:S(2)}) %collective-permute-start) | collective-permute-done | bytes 524320 | tf_op jit(solution)/shard_map/ppermute | solution.py:324
  17.5 4.8 %tail_cells.1 = (f32[1,2,2,256,128]{4,3,2,1,0:T(8,128)S(1)}, f32[1,16,32,128]{3,2,1,0:T(8,128)S(1)}) custom-call(f32[1,2,2,256,128]{4,3,2,1,0:T(8,128)S(1)} %collective-permute-done.incoming_hbm, bf16[1,2,2,512,256]{4,3,2,1,0:T(8,128)(2,1)S(1)} %get-tuple-element.11.joined_hbm, ...), custom_call_target="tpu_custom_call", output_to_operand_aliasing={{0}: (4, {}), {1}: (5, {})} | custom-call | tf_op jit(solution)/shard_map/tail_cells/pallas_call | solution.py:262
  22.2 15.3 %all_to_all.4 = f32[1,16,32,128]{3,2,0,1:T(8,128)} all-to-all(f32[1,16,32,128]{3,2,0,1:T(8,128)S(1)} %bitcast.7), channel_id=1, replica_groups=mesh['chain'=2,'energy'=16] {'energy'}, dimensions={1} | all-to-all | bytes 524288 | tf_op jit(solution)/shard_map/all_to_all | solution.py:326
  37.5 1.9 %lag_sums.1 = f32[16,32,128]{2,1,0:T(8,128)} custom-call(f32[16,32,128]{2,1,0:T(8,128)} %bitcast.8), custom_call_target="tpu_custom_call" | custom-call | tf_op jit(solution)/shard_map/lag_sums/pallas_call | solution.py:305
Async XLA Ops:
  0.0 1.2 %copy-start = (f32[1,2,2,256,256]{4,3,2,1,0:T(8,128)S(1)}, f32[1,2,2,256,256]{4,3,2,1,0:T(8,128)}, u32[]{:S(2)}) copy-start(f32[1,2,2,256,256]{4,3,2,1,0:T(8,128)} %g_hbm.1) | copy-start | bytes 3145732
  1.2 1.2 %copy-start.1 = (f32[1,2,2,256,256]{4,3,2,1,0:T(8,128)S(1)}, f32[1,2,2,256,256]{4,3,2,1,0:T(8,128)}, u32[]{:S(2)}) copy-start(f32[1,2,2,256,256]{4,3,2,1,0:T(8,128)} %s_hbm.1) | copy-start | bytes 3145732
  2.5 1.2 %copy-start.2 = (f32[2,2,256,256]{3,2,1,0:T(8,128)S(1)}, f32[2,2,256,256]{3,2,1,0:T(8,128)}, u32[]{:S(2)}) copy-start(f32[2,2,256,256]{3,2,1,0:T(8,128)} %b_hbm.1) | copy-start | bytes 3145732
  3.7 1.0 %copy-start.3 = (f32[1,2,256,256]{3,2,1,0:T(8,128)S(1)}, f32[1,2,256,256]{3,2,1,0:T(8,128)}, u32[]{:S(2)}) copy-start(f32[1,2,256,256]{3,2,1,0:T(8,128)} %lead_hbm.1) | copy-start | bytes 1572868
  4.7 0.7 %copy-start.4 = (s32[2,4,4]{2,1,0:T(4,128)S(1)}, s32[2,4,4]{2,1,0:T(4,128)}, u32[]{:S(2)}) copy-start(s32[2,4,4]{2,1,0:T(4,128)} %pattern_ref.1) | copy-start | bytes 388
  5.4 0.7 %copy-start.5 = (s32[4]{0:T(128)S(1)}, s32[4]{0:T(128)}, u32[]{:S(2)}) copy-start(s32[4]{0:T(128)} %kept_ref.3) | copy-start | bytes 52
  11.1 6.4 %collective-permute-start = (f32[1,2,2,256,128]{4,3,2,1,0:T(8,128)S(1)}, f32[1,2,2,256,128]{4,3,2,1,0:T(8,128)S(1)}, u32[]{:S(2)}, u32[]{:S(2)}) collective-permute-start(f32[1,2,2,256,128]{4,3,2,1,0:T(8,128)S(1)} %get-tuple-element.10.leaving_in), channel_id=1, source_target_pairs={{0,16},{1,17},{2,18},{3,19},{4,20},{5,21},{6,22},{7,23},{8,24},{9,... | collective-permute-start | bytes 1572872 | tf_op jit(solution)/shard_map/ppermute | solution.py:324

commit v2 on v1

--- a/solution.py
+++ b/solution.py
@@ -83,8 +83,23 @@
     return jnp.concatenate(rows, axis=0)
 
 
+def split_owners(owners):
+    inner = 1
+    while inner * inner < owners:
+        inner *= 2
+    if owners % inner:
+        inner = 1
+    return inner, owners // inner
+
+
+def place(owner, owners):
+    inner, outer = split_owners(owners)
+    return owner % inner * outer + owner // inner
+
+
 def pick_into(send_ref, e, cell, matrix_ref, kept_ref, keep, share_rows):
     nblk = matrix_ref.shape[-2] // BLOCK
+    owners = send_ref.shape[1]
     half = BLOCK // 2
     lane = lax.broadcasted_iota(jnp.int32, (half, LANES), 1)
     piece = min(half, share_rows)
@@ -103,12 +118,12 @@
             first = (cell * keep + k) * half
             for s in range(0, half, piece):
                 owner, inside = divmod(first + s, share_rows)
-                send_ref[e, owner, pl.ds(part * share_rows + inside, piece), :] = flat[s:s + piece]
-
-
-def head_kernel(keep, share_rows, g_hbm, s_hbm, b_hbm, pattern_ref, kept_ref, lead_hbm,
+                send_ref[e, place(owner, owners), pl.ds(part * share_rows + inside, piece), :] = flat[s:s + piece]
+
+
+def head_kernel(keep, share_rows, g_hbm, s_hbm, b_hbm, pattern_hbm, kept_hbm, lead_hbm,
                 leaving_hbm, send_hbm, joined_hbm, fresh_hbm,
-                g_ref, s_ref, b_ref, lead_ref, state_ref, send_ref, joined_ref, fresh_ref, in_sems, out_sems):
+                pattern_ref, kept_ref, g_ref, s_ref, b_ref, lead_ref, state_ref, send_ref, joined_ref, fresh_ref, in_sems, out_sems):
     energies, cells, _, size, _ = g_ref.shape
     position = lax.axis_index("chain")
 
@@ -120,6 +135,11 @@
     g_copies = [fetch(1 + cells + i, g_hbm.at[:, i], g_ref.at[:, i]) for i in range(cells)]
     s_copies = [fetch(1 + 2 * cells + i, s_hbm.at[:, i], s_ref.at[:, i]) for i in range(cells)]
 
+    pattern_copy = fetch(1 + 3 * cells, pattern_hbm, pattern_ref)
+    kept_copy = fetch(2 + 3 * cells, kept_hbm, kept_ref)
+    pattern_copy.start()
+    kept_copy.start()
+
     @pl.when(position == 0)
     def _():
         lead_copy.start()
@@ -128,6 +148,9 @@
         b_copies[i].start()
         g_copies[i].start()
         s_copies[i].start()
+
+    pattern_copy.wait()
+    kept_copy.wait()
 
     def masked(i):
         mask = block_mask(pattern_ref, i, size)
@@ -185,10 +208,13 @@
             copy.wait()
 
 
+def in_hbm(value):
+    return pltpu.with_memory_space_constraint(value, pltpu.HBM)
+
+
 def head(keep, share_rows, owners, retarded, lesser_sigma, coupling, pattern, kept_blocks, lead):
     energies, cells, _, size, _ = retarded.shape
     hbm = pl.BlockSpec(memory_space=pltpu.HBM)
-    smem = pl.BlockSpec(memory_space=pltpu.SMEM)
     state_shape = (energies, 2, size // LANES, size, LANES)
     send_shape = (energies, owners, 2 * share_rows, LANES)
     joined_shape = (energies, cells, 2, 2 * size, size)
@@ -201,9 +227,11 @@
             jax.ShapeDtypeStruct(joined_shape, BF16),
             jax.ShapeDtypeStruct(fresh_shape, F32),
         ),
-        in_specs=[hbm, hbm, hbm, smem, smem, hbm],
+        in_specs=[hbm] * 6,
         out_specs=(hbm, hbm, hbm, hbm),
         scratch_shapes=[
+            pltpu.SMEM(pattern.shape, jnp.int32),
+            pltpu.SMEM(kept_blocks.shape, jnp.int32),
             pltpu.VMEM(retarded.shape, F32),
             pltpu.VMEM(lesser_sigma.shape, F32),
             pltpu.VMEM(coupling.shape, F32),
@@ -212,20 +240,26 @@
             pltpu.VMEM(send_shape, F32),
             pltpu.VMEM(joined_shape, BF16),
             pltpu.VMEM(fresh_shape, F32),
-            pltpu.SemaphoreType.DMA((1 + 3 * cells,)),
+            pltpu.SemaphoreType.DMA((3 + 3 * cells,)),
             pltpu.SemaphoreType.DMA((2 + 2 * cells,)),
         ],
         compiler_params=pltpu.CompilerParams(vmem_limit_bytes=32 << 20),
         name="head_cells",
-    )(retarded, lesser_sigma, coupling, pattern, kept_blocks, lead)
-
-
-def tail_kernel(keep, share_rows, hop, incoming_hbm, joined_hbm, fresh_hbm, kept_ref, leaving_in, send_in,
-                leaving_hbm, send_hbm, state_ref, joined_ref, fresh_ref, send_ref, in_sems, out_sems):
+    )(*(in_hbm(x) for x in (retarded, lesser_sigma, coupling, pattern, kept_blocks, lead)))
+
+
+def tail_kernel(keep, share_rows, hop, last, incoming_hbm, joined_hbm, fresh_hbm, kept_hbm, *refs):
+    if last:
+        (_, send_hbm), refs = refs[:2], refs[2:]
+    else:
+        (_, _, leaving_hbm, send_hbm), refs = refs[:4], refs[4:]
+    kept_ref, state_ref, joined_ref, fresh_ref, send_ref, in_sems, out_sems = refs
     energies, cells, _, size, _ = fresh_ref.shape
 
     @pl.when(lax.axis_index("chain") == hop + 1)
     def _():
+        kept_copy = pltpu.make_async_copy(kept_hbm, kept_ref, in_sems.at[1 + 2 * cells])
+        kept_copy.start()
         state_copy = pltpu.make_async_copy(incoming_hbm, state_ref, in_sems.at[0])
         state_copy.start()
         copies = []
@@ -246,39 +280,41 @@
                 state = beside(get_state(state_ref.at[e]))
                 re, im = product_adjoint(above(complex_product(joined, state)), joined)
                 put_state(state_ref.at[e], (fresh_ref[e, i, 0] + re, fresh_ref[e, i, 1] + im))
+                if i == 0 and e == 0:
+                    kept_copy.wait()
                 pick_into(send_ref, e, i, state_ref.at[e], kept_ref, keep, share_rows)
-        send_copy = pltpu.make_async_copy(send_ref, send_hbm, out_sems.at[0])
-        send_copy.start()
-        leaving_copy = pltpu.make_async_copy(state_ref, leaving_hbm, out_sems.at[1])
-        leaving_copy.start()
-        send_copy.wait()
-        leaving_copy.wait()
-
-
-def tail(keep, share_rows, hop, incoming, joined, fresh, kept_blocks, leaving, send):
+        outs = [pltpu.make_async_copy(send_ref, send_hbm, out_sems.at[0])]
+        if not last:
+            outs.append(pltpu.make_async_copy(state_ref, leaving_hbm, out_sems.at[1]))
+        for copy in outs:
+            copy.start()
+        for copy in outs:
+            copy.wait()
+
+
+def tail(keep, share_rows, hop, last, incoming, joined, fresh, kept_blocks, leaving, send):
     cells = fresh.shape[1]
     hbm = pl.BlockSpec(memory_space=pltpu.HBM)
-    smem = pl.BlockSpec(memory_space=pltpu.SMEM)
-    return pl.pallas_call(
-        functools.partial(tail_kernel, keep, share_rows, hop),
-        out_shape=(
-            jax.ShapeDtypeStruct(leaving.shape, F32),
-            jax.ShapeDtypeStruct(send.shape, F32),
-        ),
-        in_specs=[hbm, hbm, hbm, smem, hbm, hbm],
-        out_specs=(hbm, hbm),
-        input_output_aliases={4: 0, 5: 1},
+    carried = (send,) if last else (leaving, send)
+    result = pl.pallas_call(
+        functools.partial(tail_kernel, keep, share_rows, hop, last),
+        out_shape=tuple(jax.ShapeDtypeStruct(value.shape, F32) for value in carried),
+        in_specs=[hbm] * (4 + len(carried)),
+        out_specs=(hbm,) * len(carried),
+        input_output_aliases={4 + i: i for i in range(len(carried))},
         scratch_shapes=[
+            pltpu.SMEM(kept_blocks.shape, jnp.int32),
             pltpu.VMEM(incoming.shape, F32),
             pltpu.VMEM(joined.shape, BF16),
             pltpu.VMEM(fresh.shape, F32),
             pltpu.VMEM(send.shape, F32),
-            pltpu.SemaphoreType.DMA((1 + 2 * cells,)),
+            pltpu.SemaphoreType.DMA((2 + 2 * cells,)),
             pltpu.SemaphoreType.DMA((2,)),
         ],
         compiler_params=pltpu.CompilerParams(vmem_limit_bytes=32 << 20),
         name="tail_cells",
-    )(incoming, joined, fresh, kept_blocks, leaving, send)
+    )(incoming, joined, fresh, in_hbm(kept_blocks), *carried)
+    return (leaving, result[0]) if last else result
 
 
 def lag_kernel(in_ref, out_ref):
@@ -311,6 +347,20 @@
     return jnp.swapaxes(sums, 1, 2).reshape(LAGS, 2, rows * lanes)
 
 
+def exchange(send):
+    energies, owners = send.shape[:2]
+    inner, outer = split_owners(owners)
+    near = [[o * inner + i for i in range(inner)] for o in range(outer)]
+    far = [[o * inner + i for o in range(outer)] for i in range(inner)]
+    tail = send.shape[2:]
+    send = send.reshape((energies, inner, outer) + tail)
+    send = lax.all_to_all(send, "energy", split_axis=1, concat_axis=1, axis_index_groups=near, tiled=True)
+    send = jnp.swapaxes(send, 1, 2)
+    send = lax.all_to_all(send, "energy", split_axis=1, concat_axis=0, axis_index_groups=far, tiled=True)
+    send = send.reshape((outer, energies, inner) + tail)
+    return jnp.swapaxes(send, 1, 2).reshape((-1,) + tail)
+
+
 def per_device(retarded, lesser_sigma, coupling, coupling_pattern, kept_blocks, lead_lesser):
     energies_here, cells = retarded.shape[:2]
     keep = kept_blocks.shape[0]
@@ -322,9 +372,9 @@
     )
     for hop in range(length - 1):
         incoming = lax.ppermute(leaving, "chain", [(hop, hop + 1)])
-        leaving, send = tail(keep, share_rows, hop, incoming, joined, fresh, kept_blocks, leaving, send)
-    owned = lax.all_to_all(send, "energy", split_axis=1, concat_axis=0, tiled=True)
-    return lag_sums(owned.reshape((-1,) + owned.shape[2:]))
+        last = hop == length - 2
+        leaving, send = tail(keep, share_rows, hop, last, incoming, joined, fresh, kept_blocks, leaving, send)
+    return lag_sums(exchange(send))
 
 
 def solution(mesh):

time: 39.9 us -> 39.3 us (0.985)
  local copies, waits for them, and re-layouts: 6.05 us -> 0.02 us
  blocking collectives: 15.3 us -> 21 us
    unnamed x12 -> x0, local copies, waits for them, and re-layouts: 6.05 us -> none
    all_to_all x1 -> x2, blocking collectives: 15.3 us -> 21 us  [the longest x1 11.8 us: exchange(): lax.all_to_all(send, 'energy', split_axis=1, concat_axis=0, axis_index_gr...]
    pallas_call x1, Pallas kernels: 4.78 us -> 4.23 us  [tail(): pl.pallas_call(functools.partial(tail_kernel, keep, share_rows, hop, last...]
    pallas_call x1, Pallas kernels: 5.02 us -> 5.44 us  [head(): pl.pallas_call(functools.partial(head_kernel, keep, share_rows), out_shap...]
where the time goes in v2:
time: 39.3 us; the launch traced here: 39 us
  blocking collectives  21 us (53%)
  Pallas kernels  11.6 us (30%)
  waiting for transfers between devices  4.99 us (13%)
  starting transfers between devices  1.29 us (3%)
    all_to_all x1, blocking collectives, exchange(): lax.all_to_all(send, 'energy', split_axis=1, concat_axis=0, axis_index_gr...  11.8 us
    all_to_all x1, blocking collectives, exchange(): lax.all_to_all(send, 'energy', split_axis=1, concat_axis=1, axis_index_gr...  9.26 us
    pallas_call x1, Pallas kernels, head(): pl.pallas_call(functools.partial(head_kernel, keep, share_rows), out_shap...  5.44 us
    ppermute x1, waiting for transfers between devices, per_device(): incoming = lax.ppermute(leaving, 'chain', [(hop, hop + 1)])  4.99 us
    pallas_call x1, Pallas kernels, tail(): pl.pallas_call(functools.partial(tail_kernel, keep, share_rows, hop, last...  4.23 us
    pallas_call x1, Pallas kernels, lag_sums(): pl.pallas_call(lag_kernel, out_shape=jax.ShapeDtypeStruct((LAGS, double_r...  1.94 us
    ppermute x1, starting transfers between devices, per_device(): incoming = lax.ppermute(leaving, 'chain', [(hop, hop + 1)])  1.29 us
  transfers between devices with their start and end apart: 1, of which 1 were waited for; matrix products, arithmetic and copies ran while one was open for 0% of the time, Pallas kernels for 0%

profile of v2, /device:TPU:1, one launch (start us, length us, event | category | flops | bytes accessed | tf_op | source)
XLA Modules:
  0.0 39.0 jit_solution(3277773636049923858)
XLA Ops:
  0.0 5.4 %head_cells.1 = (f32[1,2,2,256,128]{4,3,2,1,0:T(8,128)S(1)}, f32[1,16,32,128]{3,2,1,0:T(8,128)S(1)}, bf16[1,2,2,512,256]{4,3,2,1,0:T(8,128)(2,1)S(1)}, f32[1,2,2,256,256]{4,3,2,1,0:T(8,128)S(1)}) custom-call(f32[1,2,2,256,256]{4,3,2,1,0:T(8,128)} %g_hbm.1, f32[1,2,2,256,256]{4,3,2,1,0:T(8,128)} %s_hbm.1, f32[2,2,256,256]{3,2,1,0:T(8,128)} %b_hbm.1, ...), custom_call_target="tpu_custom_call" | custom-call | tf_op jit(solution)/shard_map/head_cells/pallas_call | solution.py:222
  5.5 1.3 %collective-permute-start = (f32[1,2,2,256,128]{4,3,2,1,0:T(8,128)S(1)}, f32[1,2,2,256,128]{4,3,2,1,0:T(8,128)S(1)}, u32[]{:S(2)}, u32[]{:S(2)}) collective-permute-start(f32[1,2,2,256,128]{4,3,2,1,0:T(8,128)S(1)} %get-tuple-element.9), channel_id=1, source_target_pairs={{0,16},{1,17},{2,18},{3,19},{4,20},{5,21},{6,22},{7,23},{8,24},{9,... | collective-permute-start | bytes 1572872 | tf_op jit(solution)/shard_map/ppermute | solution.py:374
  6.8 5.0 %collective-permute-done.incoming_hbm = f32[1,2,2,256,128]{4,3,2,1,0:T(8,128)S(1)} collective-permute-done((f32[1,2,2,256,128]{4,3,2,1,0:T(8,128)S(1)}, f32[1,2,2,256,128]{4,3,2,1,0:T(8,128)S(1)}, u32[]{:S(2)}, u32[]{:S(2)}) %collective-permute-start) | collective-permute-done | bytes 524320 | tf_op jit(solution)/shard_map/ppermute | solution.py:374
  11.7 4.2 %tail_cells.1 = f32[1,16,32,128]{3,2,1,0:T(8,128)S(1)} custom-call(f32[1,2,2,256,128]{4,3,2,1,0:T(8,128)S(1)} %collective-permute-done.incoming_hbm, bf16[1,2,2,512,256]{4,3,2,1,0:T(8,128)(2,1)S(1)} %get-tuple-element.10.joined_hbm, f32[1,2,2,256,256]{4,3,2,1,0:T(8,128)S(1)} %get-tuple-element.11.fresh_hbm, ...), custom_call_target="tpu_custom_call", output_to_operand_aliasing={{}: (4, {})} | custom-call | tf_op jit(solution)/shard_map/tail_cells/pallas_call | solution.py:299
  16.0 9.3 %all_to_all.14 = f32[1,4,4,32,128]{4,3,2,0,1:T(8,128)S(1)} all-to-all(f32[1,4,4,32,128]{4,3,2,0,1:T(8,128)S(1)} %bitcast.10), channel_id=1, replica_groups={{0,1,2,3},{4,5,6,7},{8,9,10,11},{12,13,14,15},{16,17,18,19},{20,21,22,2..., dimensions={1} | all-to-all | bytes 524288 | tf_op jit(solution)/shard_map/all_to_all | solution.py:357
  25.3 11.8 %all_to_all.15 = f32[1,4,4,32,128]{4,3,2,0,1:T(8,128)} all-to-all(f32[1,4,4,32,128]{4,3,2,0,1:T(8,128)S(1)} %copy.11), channel_id=1, replica_groups={{0,4,8,12},{1,5,9,13},{2,6,10,14},{3,7,11,15},{16,20,24,28},{17,21,25,2..., dimensions={1} | all-to-all | bytes 524288 | tf_op jit(solution)/shard_map/all_to_all | solution.py:359
  37.0 1.9 %lag_sums.1 = f32[16,32,128]{2,1,0:T(8,128)} custom-call(f32[16,32,128]{2,1,0:T(8,128)} %bitcast.12), custom_call_target="tpu_custom_call" | custom-call | tf_op jit(solution)/shard_map/lag_sums/pallas_call | solution.py:341
  (1 shorter events, 0.0 us)
Async XLA Ops:
  5.5 6.3 %collective-permute-start = (f32[1,2,2,256,128]{4,3,2,1,0:T(8,128)S(1)}, f32[1,2,2,256,128]{4,3,2,1,0:T(8,128)S(1)}, u32[]{:S(2)}, u32[]{:S(2)}) collective-permute-start(f32[1,2,2,256,128]{4,3,2,1,0:T(8,128)S(1)} %get-tuple-element.9), channel_id=1, source_target_pairs={{0,16},{1,17},{2,18},{3,19},{4,20},{5,21},{6,22},{7,23},{8,24},{9,... | collective-permute-start | bytes 1572872 | tf_op jit(solution)/shard_map/ppermute | solution.py:374

commit v3 on v2

--- a/solution.py
+++ b/solution.py
@@ -83,23 +83,9 @@
     return jnp.concatenate(rows, axis=0)
 
 
-def split_owners(owners):
-    inner = 1
-    while inner * inner < owners:
-        inner *= 2
-    if owners % inner:
-        inner = 1
-    return inner, owners // inner
-
-
-def place(owner, owners):
-    inner, outer = split_owners(owners)
-    return owner % inner * outer + owner // inner
-
-
 def pick_into(send_ref, e, cell, matrix_ref, kept_ref, keep, share_rows):
     nblk = matrix_ref.shape[-2] // BLOCK
-    owners = send_ref.shape[1]
+    me = lax.axis_index("energy")
     half = BLOCK // 2
     lane = lax.broadcasted_iota(jnp.int32, (half, LANES), 1)
     piece = min(half, share_rows)
@@ -118,7 +104,7 @@
             first = (cell * keep + k) * half
             for s in range(0, half, piece):
                 owner, inside = divmod(first + s, share_rows)
-                send_ref[e, place(owner, owners), pl.ds(part * share_rows + inside, piece), :] = flat[s:s + piece]
+                send_ref[owner ^ me, e, pl.ds(part * share_rows + inside, piece), :] = flat[s:s + piece]
 
 
 def head_kernel(keep, share_rows, g_hbm, s_hbm, b_hbm, pattern_hbm, kept_hbm, lead_hbm,
@@ -216,7 +202,7 @@
     energies, cells, _, size, _ = retarded.shape
     hbm = pl.BlockSpec(memory_space=pltpu.HBM)
     state_shape = (energies, 2, size // LANES, size, LANES)
-    send_shape = (energies, owners, 2 * share_rows, LANES)
+    send_shape = (owners, energies, 2 * share_rows, LANES)
     joined_shape = (energies, cells, 2, 2 * size, size)
     fresh_shape = (energies, cells, 2, size, size)
     return pl.pallas_call(
@@ -317,14 +303,19 @@
     return (leaving, result[0]) if last else result
 
 
-def lag_kernel(in_ref, out_ref):
-    energies, double_rows, _ = in_ref.shape
+def lag_kernel(places, *refs):
+    *in_refs, out_ref, all_ref = refs
+    energies, double_rows, _ = all_ref.shape
+    here = energies // len(places)
     rows = double_rows // 2
     step = min(8, rows)
     scale = 1.0 / energies
+    me = lax.axis_index("energy")
+    for r, (bundle, i) in enumerate(places):
+        all_ref[pl.ds((me ^ r) * here, here)] = in_refs[bundle][i]
     for first in range(0, rows, step):
-        re = [in_ref[e, first:first + step] for e in range(energies)]
-        im = [in_ref[e, rows + first:rows + first + step] for e in range(energies)]
+        re = [all_ref[e, first:first + step] for e in range(energies)]
+        im = [all_ref[e, rows + first:rows + first + step] for e in range(energies)]
         for lag in range(LAGS):
             real_sum = jnp.zeros((step, LANES), F32)
             imag_sum = jnp.zeros((step, LANES), F32)
@@ -335,30 +326,50 @@
             out_ref[lag, pl.ds(2 * first + 1, step, 2), :] = imag_sum * scale
 
 
-def lag_sums(owned):
-    energies, double_rows, lanes = owned.shape
+def lag_sums(slots):
+    bundles, places = [], []
+    for bundle, i in slots:
+        known = [n for n, other in enumerate(bundles) if other is bundle]
+        if not known:
+            known = [len(bundles)]
+            bundles.append(bundle)
+        places.append((known[0], i))
+    _, here, double_rows, lanes = bundles[0].shape
     rows = double_rows // 2
     sums = pl.pallas_call(
-        lag_kernel,
+        functools.partial(lag_kernel, places),
         out_shape=jax.ShapeDtypeStruct((LAGS, double_rows, lanes), F32),
+        scratch_shapes=[pltpu.VMEM((here * len(places), double_rows, lanes), F32)],
         name="lag_sums",
-    )(owned)
+    )(*bundles)
     sums = sums.reshape(LAGS, rows, 2, lanes)
     return jnp.swapaxes(sums, 1, 2).reshape(LAGS, 2, rows * lanes)
 
 
+def digits_of(owners):
+    bits = owners.bit_length() - 1
+    groups = []
+    while bits:
+        width = 2 if bits >= 2 else 1
+        bits -= width
+        groups.append((bits, 1 << width))
+    return groups
+
+
 def exchange(send):
-    energies, owners = send.shape[:2]
-    inner, outer = split_owners(owners)
-    near = [[o * inner + i for i in range(inner)] for o in range(outer)]
-    far = [[o * inner + i for o in range(outer)] for i in range(inner)]
-    tail = send.shape[2:]
-    send = send.reshape((energies, inner, outer) + tail)
-    send = lax.all_to_all(send, "energy", split_axis=1, concat_axis=1, axis_index_groups=near, tiled=True)
-    send = jnp.swapaxes(send, 1, 2)
-    send = lax.all_to_all(send, "energy", split_axis=1, concat_axis=0, axis_index_groups=far, tiled=True)
-    send = send.reshape((outer, energies, inner) + tail)
-    return jnp.swapaxes(send, 1, 2).reshape((-1,) + tail)
+    owners = send.shape[0]
+    slots = [(send, r) for r in range(owners)]
+    for shift, values in digits_of(owners):
+        arrived = []
+        for value in range(1, values):
+            moving = [r for r in range(owners) if (r >> shift) % values == value]
+            bundle = jnp.stack([slots[r][0][slots[r][1]] for r in moving])
+            pairs = [(d, d ^ (value << shift)) for d in range(owners)]
+            arrived.append((moving, lax.ppermute(bundle, "energy", pairs)))
+        for moving, bundle in arrived:
+            for i, r in enumerate(moving):
+                slots[r] = (bundle, i)
+    return slots
 
 
 def per_device(retarded, lesser_sigma, coupling, coupling_pattern, kept_blocks, lead_lesser):

time: 39.3 us -> 36.9 us (0.939)
  blocking collectives: 21 us -> 0 us
  waiting for transfers between devices: 4.99 us -> 14.1 us
  starting transfers between devices: 1.29 us -> 9.12 us
  local copies, waits for them, and re-layouts: 0.02 us -> 1.26 us
    all_to_all x2 -> x0, blocking collectives: 21 us -> none  [the longest x1 11.8 us: exchange(): lax.all_to_all(send, 'energy', split_axis=1, concat_axis=0, axis_index_gr...]
    ppermute x0 -> x6, waiting for transfers between devices: none -> 9.1 us  [exchange(): arrived.append((moving, lax.ppermute(bundle, 'energy', pairs)))]
    ppermute x0 -> x6, starting transfers between devices: none -> 7.83 us  [exchange(): arrived.append((moving, lax.ppermute(bundle, 'energy', pairs)))]
    unnamed x0 -> x14, local copies, waits for them, and re-layouts: none -> 1.23 us
  transfers between devices with their start and end apart: 1 -> 7, of which waited for: 1 -> 6; matrix products, arithmetic and copies ran while one was open for 0% -> 0% of each run, Pallas kernels for 0% -> 0%
where the time goes in v3:
time: 36.9 us; the launch traced here: 36.3 us
  waiting for transfers between devices  14.1 us (38%)
  Pallas kernels  11.8 us (32%)
  starting transfers between devices  9.12 us (25%)
  local copies, waits for them, and re-layouts  1.26 us (3%)
    ppermute x6, waiting for transfers between devices, exchange(): arrived.append((moving, lax.ppermute(bundle, 'energy', pairs)))  9.1 us
    ppermute x6, starting transfers between devices, exchange(): arrived.append((moving, lax.ppermute(bundle, 'energy', pairs)))  7.83 us
    pallas_call x1, Pallas kernels, head(): pl.pallas_call(functools.partial(head_kernel, keep, share_rows), out_shap...  5.44 us
    ppermute x1, waiting for transfers between devices, per_device(): incoming = lax.ppermute(leaving, 'chain', [(hop, hop + 1)])  4.99 us
    pallas_call x1, Pallas kernels, tail(): pl.pallas_call(functools.partial(tail_kernel, keep, share_rows, hop, last...  4.23 us
    pallas_call x1, Pallas kernels, lag_sums(): pl.pallas_call(functools.partial(lag_kernel, places), out_shape=jax.Shape...  2.09 us
    ppermute x1, starting transfers between devices, per_device(): incoming = lax.ppermute(leaving, 'chain', [(hop, hop + 1)])  1.29 us
    unnamed x14, local copies, waits for them, and re-layouts  1.23 us
  transfers between devices with their start and end apart: 7, of which 6 were waited for; matrix products, arithmetic and copies ran while one was open for 0% of the time, Pallas kernels for 0%

profile of v3, /device:TPU:1, one launch (start us, length us, event | category | flops | bytes accessed | tf_op | source)
XLA Modules:
  0.0 36.3 jit_solution(11780153837802177843)
XLA Ops:
  0.0 5.4 %head_cells.1 = (f32[1,2,2,256,128]{4,3,2,1,0:T(8,128)S(1)}, f32[16,1,32,128]{3,2,1,0:T(8,128)S(1)}, bf16[1,2,2,512,256]{4,3,2,1,0:T(8,128)(2,1)S(1)}, f32[1,2,2,256,256]{4,3,2,1,0:T(8,128)S(1)}) custom-call(f32[1,2,2,256,256]{4,3,2,1,0:T(8,128)} %g_hbm.1, f32[1,2,2,256,256]{4,3,2,1,0:T(8,128)} %s_hbm.1, f32[2,2,256,256]{3,2,1,0:T(8,128)} %b_hbm.1, ...), custom_call_target="tpu_custom_call" | custom-call | tf_op jit(solution)/shard_map/head_cells/pallas_call | solution.py:208
  5.5 1.3 %collective-permute-start = (f32[1,2,2,256,128]{4,3,2,1,0:T(8,128)S(1)}, f32[1,2,2,256,128]{4,3,2,1,0:T(8,128)S(1)}, u32[]{:S(2)}, u32[]{:S(2)}) collective-permute-start(f32[1,2,2,256,128]{4,3,2,1,0:T(8,128)S(1)} %get-tuple-element.9), channel_id=1, source_target_pairs={{0,16},{1,17},{2,18},{3,19},{4,20},{5,21},{6,22},{7,23},{8,24},{9,... | collective-permute-start | bytes 1572872 | tf_op jit(solution)/shard_map/ppermute | solution.py:385
  6.8 5.0 %collective-permute-done.incoming_hbm = f32[1,2,2,256,128]{4,3,2,1,0:T(8,128)S(1)} collective-permute-done((f32[1,2,2,256,128]{4,3,2,1,0:T(8,128)S(1)}, f32[1,2,2,256,128]{4,3,2,1,0:T(8,128)S(1)}, u32[]{:S(2)}, u32[]{:S(2)}) %collective-permute-start) | collective-permute-done | bytes 524320 | tf_op jit(solution)/shard_map/ppermute | solution.py:385
  11.7 4.2 %tail_cells.1.refs_0_ = f32[16,1,32,128]{3,2,1,0:T(8,128)S(1)} custom-call(f32[1,2,2,256,128]{4,3,2,1,0:T(8,128)S(1)} %collective-permute-done.incoming_hbm, bf16[1,2,2,512,256]{4,3,2,1,0:T(8,128)(2,1)S(1)} %get-tuple-element.10.joined_hbm, f32[1,2,2,256,256]{4,3,2,1,0:T(8,128)S(1)} %get-tuple-element.11.fresh_hbm, ...), custom_call_target="tpu_custom_call", output_to_operand_aliasing={{}: (4, {})} | custom-call | tf_op jit(solution)/shard_map/tail_cells/pallas_call | solution.py:285
  16.0 0.0 copy-start
  16.0 2.8 %collective-permute-start.1 = (f32[4,1,32,128]{3,2,1,0:T(8,128)S(1)}, f32[4,1,32,128]{3,2,1,0:T(8,128)S(1)}, u32[]{:S(2)}, u32[]{:S(2)}) collective-permute-start(f32[4,1,32,128]{3,2,1,0:T(8,128)S(1)} %get-tuple-element.16), channel_id=1, source_target_pairs={{0,4},{1,5},{2,6},{3,7},{4,0},{5,1},{6,2},{7,3},{8,12},{9,13},{10,... | collective-permute-start | bytes 196616 | tf_op jit(solution)/shard_map/ppermute | solution.py:368
  18.8 2.2 %collective-permute-start.3 = (f32[4,1,32,128]{3,2,1,0:T(8,128)S(1)}, f32[4,1,32,128]{3,2,1,0:T(8,128)S(1)}, u32[]{:S(2)}, u32[]{:S(2)}) collective-permute-start(f32[4,1,32,128]{3,2,1,0:T(8,128)S(1)} %get-tuple-element.17), channel_id=1, source_target_pairs={{0,12},{1,13},{2,14},{3,15},{4,8},{5,9},{6,10},{7,11},{8,4},{9,5},... | collective-permute-start | bytes 196616 | tf_op jit(solution)/shard_map/ppermute | solution.py:368
  21.0 0.2 collective-permute-start.2
  21.2 0.0 collective-permute-done.1.refs_4_
  21.2 0.0 copy-done
  21.2 2.6 %collective-permute-done.3.refs_6_ = f32[4,1,32,128]{3,2,1,0:T(8,128)S(1)} collective-permute-done((f32[4,1,32,128]{3,2,1,0:T(8,128)S(1)}, f32[4,1,32,128]{3,2,1,0:T(8,128)S(1)}, u32[]{:S(2)}, u32[]{:S(2)}) %collective-permute-start.3) | collective-permute-done | bytes 65568 | tf_op jit(solution)/shard_map/ppermute | solution.py:368
  23.8 0.0 copy-done.1
  23.9 1.9 %collective-permute-done.2.refs_5_ = f32[4,1,32,128]{3,2,1,0:T(8,128)S(1)} collective-permute-done((f32[4,1,32,128]{3,2,1,0:T(8,128)S(1)}, f32[4,1,32,128]{3,2,1,0:T(8,128)S(1)}, u32[]{:S(2)}, u32[]{:S(2)}) %collective-permute-start.2) | collective-permute-done | bytes 65568 | tf_op jit(solution)/shard_map/ppermute | solution.py:368
  25.7 0.0 copy-done.2
  25.8 0.6 %copy-done.3 = f32[4,1,32,128]{3,2,1,0:T(8,128)} copy-done((f32[4,1,32,128]{3,2,1,0:T(8,128)}, f32[4,1,32,128]{3,2,1,0:T(8,128)S(1)}, u32[]{:S(2)}) %copy-start.3) | copy-done | bytes 65560
  26.4 1.2 %collective-permute-start.4 = (f32[4,1,32,128]{3,2,1,0:T(8,128)S(1)}, f32[4,1,32,128]{3,2,1,0:T(8,128)S(1)}, u32[]{:S(2)}, u32[]{:S(2)}) collective-permute-start(f32[4,1,32,128]{3,2,1,0:T(8,128)S(1)} %pad_maximum_fusion), channel_id=1, source_target_pairs={{0,1},{1,0},{2,3},{3,2},{4,5},{5,4},{6,7},{7,6},{8,9},{9,8},{10,11... | collective-permute-start | bytes 196616 | tf_op jit(solution)/shard_map/ppermute | solution.py:368
  27.6 1.2 %collective-permute-start.5 = (f32[4,1,32,128]{3,2,1,0:T(8,128)S(1)}, f32[4,1,32,128]{3,2,1,0:T(8,128)S(1)}, u32[]{:S(2)}, u32[]{:S(2)}) collective-permute-start(f32[4,1,32,128]{3,2,1,0:T(8,128)S(1)} %pad_maximum_fusion.1), channel_id=1, source_target_pairs={{0,2},{1,3},{2,0},{3,1},{4,6},{5,7},{6,4},{7,5},{8,10},{9,11},{10,... | collective-permute-start | bytes 196616 | tf_op jit(solution)/shard_map/ppermute | solution.py:368
  28.8 0.2 collective-permute-start.6
  29.0 0.5 %collective-permute-done.4.refs_1_ = f32[4,1,32,128]{3,2,1,0:T(8,128)S(1)} collective-permute-done((f32[4,1,32,128]{3,2,1,0:T(8,128)S(1)}, f32[4,1,32,128]{3,2,1,0:T(8,128)S(1)}, u32[]{:S(2)}, u32[]{:S(2)}) %collective-permute-start.4) | collective-permute-done | bytes 65568 | tf_op jit(solution)/shard_map/ppermute | solution.py:368
  29.5 1.5 %collective-permute-done.5.refs_2_ = f32[4,1,32,128]{3,2,1,0:T(8,128)S(1)} collective-permute-done((f32[4,1,32,128]{3,2,1,0:T(8,128)S(1)}, f32[4,1,32,128]{3,2,1,0:T(8,128)S(1)}, u32[]{:S(2)}, u32[]{:S(2)}) %collective-permute-start.5) | collective-permute-done | bytes 65568 | tf_op jit(solution)/shard_map/ppermute | solution.py:368
  31.0 2.6 %collective-permute-done.6.refs_3_ = f32[4,1,32,128]{3,2,1,0:T(8,128)S(1)} collective-permute-done((f32[4,1,32,128]{3,2,1,0:T(8,128)S(1)}, f32[4,1,32,128]{3,2,1,0:T(8,128)S(1)}, u32[]{:S(2)}, u32[]{:S(2)}) %collective-permute-start.6) | collective-permute-done | bytes 65568 | tf_op jit(solution)/shard_map/ppermute | solution.py:368
  33.6 0.0 copy-done.4
  33.6 0.6 %copy-done.6 = f32[4,1,32,128]{3,2,1,0:T(8,128)} copy-done((f32[4,1,32,128]{3,2,1,0:T(8,128)}, f32[4,1,32,128]{3,2,1,0:T(8,128)S(1)}, u32[]{:S(2)}) %copy-start.6) | copy-done | bytes 65560
  34.2 2.1 %lag_sums.1 = f32[16,32,128]{2,1,0:T(8,128)} custom-call(f32[16,1,32,128]{3,2,1,0:T(8,128)} %copy-done, f32[4,1,32,128]{3,2,1,0:T(8,128)} %copy-done.4, f32[4,1,32,128]{3,2,1,0:T(8,128)} %copy-done.5, f32[4,1,32,128]{3,2,1,0:T(8,128)} %copy-done.6, f32[4,1,32,128]{3,2,1,0:T(8,128)} %copy-done.1, f32[4,1,32,128]{3,2,1,0:T(8,128)} %copy-done.3, ...), custom_call_target="tpu_custom_call" | custom-call | tf_op jit(solution)/shard_map/lag_sums/pallas_call | solution.py:339
  (15 shorter events, 0.1 us)
Async XLA Ops:
  5.5 6.3 %collective-permute-start = (f32[1,2,2,256,128]{4,3,2,1,0:T(8,128)S(1)}, f32[1,2,2,256,128]{4,3,2,1,0:T(8,128)S(1)}, u32[]{:S(2)}, u32[]{:S(2)}) collective-permute-start(f32[1,2,2,256,128]{4,3,2,1,0:T(8,128)S(1)} %get-tuple-element.9), channel_id=1, source_target_pairs={{0,16},{1,17},{2,18},{3,19},{4,20},{5,21},{6,22},{7,23},{8,24},{9,... | collective-permute-start | bytes 1572872 | tf_op jit(solution)/shard_map/ppermute | solution.py:385
  16.0 5.2 %copy-start = (f32[16,1,32,128]{3,2,1,0:T(8,128)}, f32[16,1,32,128]{3,2,1,0:T(8,128)S(1)}, u32[]{:S(2)}) copy-start(f32[16,1,32,128]{3,2,1,0:T(8,128)S(1)} %tail_cells.1.refs_0_) | copy-start | bytes 786436
  16.0 5.2 %collective-permute-start.1 = (f32[4,1,32,128]{3,2,1,0:T(8,128)S(1)}, f32[4,1,32,128]{3,2,1,0:T(8,128)S(1)}, u32[]{:S(2)}, u32[]{:S(2)}) collective-permute-start(f32[4,1,32,128]{3,2,1,0:T(8,128)S(1)} %get-tuple-element.16), channel_id=1, source_target_pairs={{0,4},{1,5},{2,6},{3,7},{4,0},{5,1},{6,2},{7,3},{8,12},{9,13},{10,... | collective-permute-start | bytes 196616 | tf_op jit(solution)/shard_map/ppermute | solution.py:368
  18.8 5.0 %collective-permute-start.3 = (f32[4,1,32,128]{3,2,1,0:T(8,128)S(1)}, f32[4,1,32,128]{3,2,1,0:T(8,128)S(1)}, u32[]{:S(2)}, u32[]{:S(2)}) collective-permute-start(f32[4,1,32,128]{3,2,1,0:T(8,128)S(1)} %get-tuple-element.17), channel_id=1, source_target_pairs={{0,12},{1,13},{2,14},{3,15},{4,8},{5,9},{6,10},{7,11},{8,4},{9,5},... | collective-permute-start | bytes 196616 | tf_op jit(solution)/shard_map/ppermute | solution.py:368
  21.0 4.7 %collective-permute-start.2 = (f32[4,1,32,128]{3,2,1,0:T(8,128)S(1)}, f32[4,1,32,128]{3,2,1,0:T(8,128)S(1)}, u32[]{:S(2)}, u32[]{:S(2)}) collective-permute-start(f32[4,1,32,128]{3,2,1,0:T(8,128)S(1)} %get-tuple-element.18), channel_id=1, source_target_pairs={{0,8},{1,9},{2,10},{3,11},{4,12},{5,13},{6,14},{7,15},{8,0},{9,1},... | collective-permute-start | bytes 196616 | tf_op jit(solution)/shard_map/ppermute | solution.py:368
  21.2 2.6 %copy-start.1 = (f32[4,1,32,128]{3,2,1,0:T(8,128)}, f32[4,1,32,128]{3,2,1,0:T(8,128)S(1)}, u32[]{:S(2)}) copy-start(f32[4,1,32,128]{3,2,1,0:T(8,128)S(1)} %collective-permute-done.1.refs_4_) | copy-start | bytes 196612
  23.8 1.9 %copy-start.2 = (f32[4,1,32,128]{3,2,1,0:T(8,128)}, f32[4,1,32,128]{3,2,1,0:T(8,128)S(1)}, u32[]{:S(2)}) copy-start(f32[4,1,32,128]{3,2,1,0:T(8,128)S(1)} %collective-permute-done.3.refs_6_) | copy-start | bytes 196612
  25.7 0.6 %copy-start.3 = (f32[4,1,32,128]{3,2,1,0:T(8,128)}, f32[4,1,32,128]{3,2,1,0:T(8,128)S(1)}, u32[]{:S(2)}) copy-start(f32[4,1,32,128]{3,2,1,0:T(8,128)S(1)} %collective-permute-done.2.refs_5_) | copy-start | bytes 196612
  26.4 3.2 %collective-permute-start.4 = (f32[4,1,32,128]{3,2,1,0:T(8,128)S(1)}, f32[4,1,32,128]{3,2,1,0:T(8,128)S(1)}, u32[]{:S(2)}, u32[]{:S(2)}) collective-permute-start(f32[4,1,32,128]{3,2,1,0:T(8,128)S(1)} %pad_maximum_fusion), channel_id=1, source_target_pairs={{0,1},{1,0},{2,3},{3,2},{4,5},{5,4},{6,7},{7,6},{8,9},{9,8},{10,11... | collective-permute-start | bytes 196616 | tf_op jit(solution)/shard_map/ppermute | solution.py:368
  27.6 3.4 %collective-permute-start.5 = (f32[4,1,32,128]{3,2,1,0:T(8,128)S(1)}, f32[4,1,32,128]{3,2,1,0:T(8,128)S(1)}, u32[]{:S(2)}, u32[]{:S(2)}) collective-permute-start(f32[4,1,32,128]{3,2,1,0:T(8,128)S(1)} %pad_maximum_fusion.1), channel_id=1, source_target_pairs={{0,2},{1,3},{2,0},{3,1},{4,6},{5,7},{6,4},{7,5},{8,10},{9,11},{10,... | collective-permute-start | bytes 196616 | tf_op jit(solution)/shard_map/ppermute | solution.py:368
  28.8 4.8 %collective-permute-start.6 = (f32[4,1,32,128]{3,2,1,0:T(8,128)S(1)}, f32[4,1,32,128]{3,2,1,0:T(8,128)S(1)}, u32[]{:S(2)}, u32[]{:S(2)}) collective-permute-start(f32[4,1,32,128]{3,2,1,0:T(8,128)S(1)} %pad_maximum_fusion.2), channel_id=1, source_target_pairs={{0,3},{1,2},{2,1},{3,0},{4,7},{5,6},{6,5},{7,4},{8,11},{9,10},{10,... | collective-permute-start | bytes 196616 | tf_op jit(solution)/shard_map/ppermute | solution.py:368
  29.5 4.1 %copy-start.4 = (f32[4,1,32,128]{3,2,1,0:T(8,128)}, f32[4,1,32,128]{3,2,1,0:T(8,128)S(1)}, u32[]{:S(2)}) copy-start(f32[4,1,32,128]{3,2,1,0:T(8,128)S(1)} %collective-permute-done.4.refs_1_) | copy-start | bytes 196612
  31.0 2.6 %copy-start.5 = (f32[4,1,32,128]{3,2,1,0:T(8,128)}, f32[4,1,32,128]{3,2,1,0:T(8,128)S(1)}, u32[]{:S(2)}) copy-start(f32[4,1,32,128]{3,2,1,0:T(8,128)S(1)} %collective-permute-done.5.refs_2_) | copy-start | bytes 196612
  33.6 0.6 %copy-start.6 = (f32[4,1,32,128]{3,2,1,0:T(8,128)}, f32[4,1,32,128]{3,2,1,0:T(8,128)S(1)}, u32[]{:S(2)}) copy-start(f32[4,1,32,128]{3,2,1,0:T(8,128)S(1)} %collective-permute-done.6.refs_3_) | copy-start | bytes 196612

commit v4 on v2

v4 whole, which is shorter than its diff:
```python
import functools

import jax
import jax.numpy as jnp
from jax import lax
from jax.experimental import pallas as pl
from jax.experimental.pallas import tpu as pltpu
from jax.sharding import PartitionSpec as P

BLOCK = 64
LAGS = 16
LANES = 128
F32 = jnp.float32
BF16 = jnp.bfloat16


def two_parts(value):
    high = value.astype(BF16)
    return high, (value - high.astype(F32)).astype(BF16)


def dot(left, right):
    return lax.dot_general(left, right, (((1,), (0,)), ((), ())), preferred_element_type=F32)


def left_parts(pair):
    return two_parts(jnp.concatenate(pair, axis=1))


def right_parts(pair):
    both = []
    for re, im in zip(two_parts(pair[0]), two_parts(pair[1])):
        both.append(jnp.concatenate([jnp.concatenate([re, im], axis=1), jnp.concatenate([-im, re], axis=1)], axis=0))
    return tuple(both)


def adjoint(pair):
    return pair[0].T, -pair[1].T


def product(left, right):
    wide = jnp.concatenate([left[0], left[0], left[1]], axis=1)
    tall = jnp.concatenate([right[0], right[1], right[0]], axis=0)
    both = dot(wide, tall)
    half = both.shape[1] // 2
    return both[:, :half], both[:, half:]


def plus(one, other):
    return one[0] + other[0], one[1] + other[1]


def put_state(state_ref, pair):
    for part in range(2):
        for group in range(state_ref.shape[1]):
            state_ref[part, group] = pair[part][:, group * LANES:(group + 1) * LANES]


def get_state(state_ref):
    groups = range(state_ref.shape[1])
    return tuple(jnp.concatenate([state_ref[part, group] for group in groups], axis=1) for part in range(2))


def block_mask(pattern_ref, cell, size):
    nblk = size // BLOCK
    column = lax.broadcasted_iota(jnp.int32, (BLOCK, size), 1) // BLOCK
    rows = []
    for r in range(nblk):
        row = jnp.zeros((BLOCK, size), F32)
        for c in range(nblk):
            row = jnp.where(column == c, pattern_ref[cell, r, c].astype(F32), row)
        rows.append(row)
    return jnp.concatenate(rows, axis=0)


def pick_into(send_ref, e, cell, matrix_ref, kept_ref, keep, share_rows):
    nblk = matrix_ref.shape[-2] // BLOCK
    half = BLOCK // 2
    lane = lax.broadcasted_iota(jnp.int32, (half, LANES), 1)
    piece = min(half, share_rows)
    for k in range(keep):
        number = kept_ref[k]
        top = (number // nblk) * BLOCK
        across = (number % nblk) * BLOCK
        window = across // LANES
        in_upper = jnp.full((half, LANES), across % LANES, jnp.int32) > 0
        for part in range(2):
            even = matrix_ref[part, window, pl.ds(top, half, 2), :]
            odd = matrix_ref[part, window, pl.ds(top + 1, half, 2), :]
            left = jnp.where(in_upper, pltpu.roll(even, BLOCK, 1), even)
            right = jnp.where(in_upper, odd, pltpu.roll(odd, BLOCK, 1))
            flat = jnp.where(lane < BLOCK, left, right)
            first = (cell * keep + k) * half
            for s in range(0, half, piece):
                owner, inside = divmod(first + s, share_rows)
                send_ref[e, owner, pl.ds(part * share_rows + inside, piece), :] = flat[s:s + piece]


def head_kernel(keep, share_rows, g_hbm, s_hbm, b_hbm, pattern_hbm, kept_hbm, lead_hbm,
                leaving_ref, send_ref, left_ref, right_ref, fresh_ref,
                pattern_ref, kept_ref, g_ref, s_ref, b_ref, lead_ref, state_ref, sems):
    energies, cells, _, size, _ = g_ref.shape
    position = lax.axis_index("chain")

    def fetch(slot, source, target):
        return pltpu.make_async_copy(source, target, sems.at[slot])

    lead_copy = fetch(0, lead_hbm, lead_ref)
    b_copies = [fetch(1 + i, b_hbm.at[i], b_ref.at[i]) for i in range(cells)]
    g_copies = [fetch(1 + cells + i, g_hbm.at[:, i], g_ref.at[:, i]) for i in range(cells)]
    s_copies = [fetch(1 + 2 * cells + i, s_hbm.at[:, i], s_ref.at[:, i]) for i in range(cells)]
    pattern_copy = fetch(1 + 3 * cells, pattern_hbm, pattern_ref)
    kept_copy = fetch(2 + 3 * cells, kept_hbm, kept_ref)
    pattern_copy.start()
    kept_copy.start()

    @pl.when(position == 0)
    def _():
        lead_copy.start()

    for i in range(cells):
        b_copies[i].start()
        g_copies[i].start()
        s_copies[i].start()
    pattern_copy.wait()
    kept_copy.wait()

    def bridge_of(i):
        mask = block_mask(pattern_ref, i, size)
        return b_ref[i, 0] * mask, b_ref[i, 1] * mask

    def matrix(ref, e, i):
        return ref[e, i, 0], ref[e, i, 1]

    @pl.when(position == 0)
    def _():
        lead_copy.wait()
        states = [(lead_ref[e, 0], lead_ref[e, 1]) for e in range(energies)]
        for i in range(cells):
            b_copies[i].wait()
            bridge = bridge_of(i)
            bridge_left, bridge_right = left_parts(bridge), right_parts(adjoint(bridge))
            for e in range(energies):
                entered = product(left_parts(product(bridge_left, right_parts(states[e]))), bridge_right)
                if e == 0:
                    g_copies[i].wait()
                    s_copies[i].wait()
                green = matrix(g_ref, e, i)
                green_left, green_right = left_parts(green), right_parts(adjoint(green))
                inner = right_parts(plus(matrix(s_ref, e, i), entered))
                states[e] = product(left_parts(product(green_left, inner)), green_right)
                out_ref = leaving_ref.at[e] if i == cells - 1 else state_ref.at[e, i]
                put_state(out_ref, states[e])
                pick_into(send_ref, e, i, out_ref, kept_ref, keep, share_rows)

    @pl.when(position > 0)
    def _():
        states, joined = [None] * energies, [None] * energies
        for i in range(cells):
            b_copies[i].wait()
            g_copies[i].wait()
            s_copies[i].wait()
            bridge = bridge_of(i)
            for e in range(energies):
                green = matrix(g_ref, e, i)
                green_left, green_right = left_parts(green), right_parts(adjoint(green))
                inner = matrix(s_ref, e, i)
                if i == 0:
                    joined[e] = product(green_left, right_parts(bridge))
                else:
                    bridge_left, bridge_right = left_parts(bridge), right_parts(adjoint(bridge))
                    half = left_parts(product(bridge_left, right_parts(states[e])))
                    across = right_parts(product(bridge_left, right_parts(joined[e])))
                    inner = plus(inner, product(half, bridge_right))
                    joined[e] = product(green_left, across)
                states[e] = product(left_parts(product(green_left, right_parts(inner))), green_right)
                left_ref[e, i, 0], left_ref[e, i, 1] = left_parts(joined[e])
                right_ref[e, i, 0], right_ref[e, i, 1] = right_parts(adjoint(joined[e]))
                fresh_ref[e, i, 0], fresh_ref[e, i, 1] = states[e]


def in_hbm(value):
    return pltpu.with_memory_space_constraint(value, pltpu.HBM)


def head(keep, share_rows, owners, retarded, lesser_sigma, coupling, pattern, kept_blocks, lead):
    energies, cells, _, size, _ = retarded.shape
    hbm = pl.BlockSpec(memory_space=pltpu.HBM)
    vmem = pl.BlockSpec(memory_space=pltpu.VMEM)
    state_shape = (2, size // LANES, size, LANES)
    return pl.pallas_call(
        functools.partial(head_kernel, keep, share_rows),
        out_shape=(
            jax.ShapeDtypeStruct((energies,) + state_shape, F32),
            jax.ShapeDtypeStruct((energies, owners, 2 * share_rows, LANES), F32),
            jax.ShapeDtypeStruct((energies, cells, 2, size, 2 * size), BF16),
            jax.ShapeDtypeStruct((energies, cells, 2, 2 * size, 2 * size), BF16),
            jax.ShapeDtypeStruct((energies, cells, 2, size, size), F32),
        ),
        in_specs=[hbm] * 6,
        out_specs=(vmem,) * 5,
        scratch_shapes=[
            pltpu.SMEM(pattern.shape, jnp.int32),
            pltpu.SMEM(kept_blocks.shape, jnp.int32),
            pltpu.VMEM(retarded.shape, F32),
            pltpu.VMEM(lesser_sigma.shape, F32),
            pltpu.VMEM(coupling.shape, F32),
            pltpu.VMEM(lead.shape, F32),
            pltpu.VMEM((energies, cells) + state_shape, F32),
            pltpu.SemaphoreType.DMA((3 + 3 * cells,)),
        ],
        compiler_params=pltpu.CompilerParams(vmem_limit_bytes=32 << 20),
        name="head_cells",
    )(*(in_hbm(x) for x in (retarded, lesser_sigma, coupling, pattern, kept_blocks, lead)))


def tail_kernel(keep, share_rows, hop, last, incoming_ref, left_ref, right_ref, fresh_ref, kept_hbm, *refs):
    if last:
        (_, send_ref), refs = refs[:2], refs[2:]
        leaving_ref = None
    else:
        (_, _, leaving_ref, send_ref), refs = refs[:4], refs[4:]
    kept_ref, state_ref, sem = refs
    energies, cells, _, size, _ = fresh_ref.shape

    @pl.when(lax.axis_index("chain") == hop + 1)
    def _():
        kept_copy = pltpu.make_async_copy(kept_hbm, kept_ref, sem)
        kept_copy.start()
        for e in range(energies):
            state = right_parts(get_state(incoming_ref.at[e]))
            halves = []
            for i in range(cells):
                halves.append(left_parts(product((left_ref[e, i, 0], left_ref[e, i, 1]), state)))
            for i in range(cells):
                grown = product(halves[i], (right_ref[e, i, 0], right_ref[e, i, 1]))
                put_state(state_ref.at[e, i], plus((fresh_ref[e, i, 0], fresh_ref[e, i, 1]), grown))
                if i == 0 and e == 0:
                    kept_copy.wait()
                pick_into(send_ref, e, i, state_ref.at[e, i], kept_ref, keep, share_rows)
            if not last:
                leaving_ref[e] = state_ref[e, cells - 1]


def tail(keep, share_rows, hop, last, incoming, left, right, fresh, kept_blocks, leaving, send):
    energies, cells = fresh.shape[:2]
    hbm = pl.BlockSpec(memory_space=pltpu.HBM)
    vmem = pl.BlockSpec(memory_space=pltpu.VMEM)
    carried = (send,) if last else (leaving, send)
    result = pl.pallas_call(
        functools.partial(tail_kernel, keep, share_rows, hop, last),
        out_shape=tuple(jax.ShapeDtypeStruct(value.shape, F32) for value in carried),
        in_specs=[vmem] * 4 + [hbm] + [vmem] * len(carried),
        out_specs=(vmem,) * len(carried),
        input_output_aliases={5 + i: i for i in range(len(carried))},
        scratch_shapes=[
            pltpu.SMEM(kept_blocks.shape, jnp.int32),
            pltpu.VMEM((energies, cells) + incoming.shape[1:], F32),
            pltpu.SemaphoreType.DMA,
        ],
        compiler_params=pltpu.CompilerParams(vmem_limit_bytes=32 << 20),
        name="tail_cells",
    )(incoming, left, right, fresh, in_hbm(kept_blocks), *carried)
    return (leaving, result[0]) if last else result


def lag_kernel(in_ref, out_ref):
    energies, double_rows, _ = in_ref.shape
    rows = double_rows // 2
    step = min(8, rows)
    scale = 1.0 / energies
    for first in range(0, rows, step):
        re = [in_ref[e, first:first + step] for e in range(energies)]
        im = [in_ref[e, rows + first:rows + first + step] for e in range(energies)]
        for lag in range(LAGS):
            real_sum = jnp.zeros((step, LANES), F32)
            imag_sum = jnp.zeros((step, LANES), F32)
            for e in range(energies - lag):
                real_sum += re[e + lag] * re[e] + im[e + lag] * im[e]
                imag_sum += im[e + lag] * re[e] - re[e + lag] * im[e]
            out_ref[lag, pl.ds(2 * first, step, 2), :] = real_sum * scale
            out_ref[lag, pl.ds(2 * first + 1, step, 2), :] = imag_sum * scale


def lag_sums(owned):
    energies, double_rows, lanes = owned.shape
    rows = double_rows // 2
    vmem = pl.BlockSpec(memory_space=pltpu.VMEM)
    sums = pl.pallas_call(
        lag_kernel,
        out_shape=jax.ShapeDtypeStruct((LAGS, double_rows, lanes), F32),
        in_specs=[vmem],
        out_specs=vmem,
        name="lag_sums",
    )(owned)
    sums = sums.reshape(LAGS, rows, 2, lanes)
    return jnp.swapaxes(sums, 1, 2).reshape(LAGS, 2, rows * lanes)


def per_device(retarded, lesser_sigma, coupling, coupling_pattern, kept_blocks, lead_lesser):
    cells = retarded.shape[1]
    keep = kept_blocks.shape[0]
    owners = lax.axis_size("energy")
    length = lax.axis_size("chain")
    share_rows = cells * keep * BLOCK * BLOCK // (owners * LANES)
    leaving, send, left, right, fresh = head(
        keep, share_rows, owners, retarded, lesser_sigma, coupling, coupling_pattern, kept_blocks, lead_lesser
    )
    for hop in range(length - 1):
        incoming = lax.ppermute(leaving, "chain", [(i, (i + 1) % length) for i in range(length)])
        last = hop == length - 2
        leaving, send = tail(keep, share_rows, hop, last, incoming, left, right, fresh, kept_blocks, leaving, send)
    owned = lax.all_to_all(send, "energy", split_axis=1, concat_axis=0, tiled=True)
    return lag_sums(owned.reshape((-1,) + owned.shape[2:]))


def solution(mesh):
    return jax.shard_map(
        per_device,
        mesh=mesh,
        in_specs=(
            P("energy", "chain", None, None, None),
            P("energy", "chain", None, None, None),
            P("chain", None, None, None),
            P("chain", None, None),
            P(),
            P("energy", None, None, None),
        ),
        out_specs=P(None, None, ("chain", "energy")),
        check_vma=False,
    )
```

time: 39.3 us -> 28.9 us (0.74)
  blocking collectives: 21 us -> 16.9 us
  waiting for transfers between devices: 4.99 us -> 1.68 us
  Pallas kernels: 11.6 us -> 9.76 us
  starting transfers between devices: 1.29 us -> 0.29 us
    all_to_all x2 -> x1, blocking collectives: 21 us -> 16.9 us  [per_device(): lax.all_to_all(send, 'energy', split_axis=1, concat_axis=0, tiled=True)]
    ppermute x1, waiting for transfers between devices: 4.99 us -> 1.68 us  [per_device(): lax.ppermute(leaving, 'chain', [(i, (i + 1) % length) for i in range(leng...]
    pallas_call x1, Pallas kernels: 4.23 us -> 2.12 us  [tail(): pl.pallas_call(functools.partial(tail_kernel, keep, share_rows, hop, last...]
    ppermute x1, starting transfers between devices: 1.29 us -> 0.29 us  [per_device(): lax.ppermute(leaving, 'chain', [(i, (i + 1) % length) for i in range(leng...]
where the time goes in v4:
time: 28.9 us; the launch traced here: 28.7 us
  blocking collectives  16.9 us (58%)
  Pallas kernels  9.76 us (34%)
  waiting for transfers between devices  1.68 us (6%)
  starting transfers between devices  0.29 us (1%)
    all_to_all x1, blocking collectives, per_device(): lax.all_to_all(send, 'energy', split_axis=1, concat_axis=0, tiled=True)  16.9 us
    pallas_call x1, Pallas kernels, head(): pl.pallas_call(functools.partial(head_kernel, keep, share_rows), out_shap...  5.7 us
    pallas_call x1, Pallas kernels, tail(): pl.pallas_call(functools.partial(tail_kernel, keep, share_rows, hop, last...  2.12 us
    pallas_call x1, Pallas kernels, lag_sums(): pl.pallas_call(lag_kernel, out_shape=jax.ShapeDtypeStruct((LAGS, double_r...  1.94 us
    ppermute x1, waiting for transfers between devices, per_device(): lax.ppermute(leaving, 'chain', [(i, (i + 1) % length) for i in range(leng...  1.68 us
  transfers between devices with their start and end apart: 1, of which 1 were waited for; matrix products, arithmetic and copies ran while one was open for 0% of the time, Pallas kernels for 0%

profile of v4, /device:TPU:1, one launch (start us, length us, event | category | flops | bytes accessed | tf_op | source)
XLA Modules:
  0.0 28.7 jit_solution(12728565024167140839)
XLA Ops:
  0.0 5.7 %head_cells.1 = (f32[1,2,2,256,128]{4,3,2,1,0:T(8,128)S(1)}, f32[1,16,32,128]{3,2,1,0:T(8,128)S(1)}, bf16[1,2,2,256,512]{4,3,2,1,0:T(8,128)(2,1)S(1)}, bf16[1,2,...) custom-call(f32[1,2,2,256,256]{4,3,2,1,0:T(8,128)} %g_hbm.1, f32[1,2,2,256,256]{4,3,2,1,0:T(8,128)} %s_hbm.1, ...), custom_call_target="tpu_custom_call" | custom-call | tf_op jit(solution)/shard_map/head_cells/pallas_call | solution.py:191
  5.7 0.3 %collective-permute-start = (f32[1,2,2,256,128]{4,3,2,1,0:T(8,128)S(1)}, f32[1,2,2,256,128]{4,3,2,1,0:T(8,128)S(1)}, u32[]{:S(2)}, u32[]{:S(2)}) collective-permute-start(f32[1,2,2,256,128]{4,3,2,1,0:T(8,128)S(1)} %get-tuple-element.10), channel_id=1, source_target_pairs={{0,16},{16,0},{1,17},{17,1},{2,18},{18,2},{3,19},{19,3},{4,20},{20... | collective-permute-start | bytes 1572872 | tf_op jit(solution)/shard_map/ppermute | solution.py:310
  6.0 1.7 %collective-permute-done.incoming_ref = f32[1,2,2,256,128]{4,3,2,1,0:T(8,128)S(1)} collective-permute-done((f32[1,2,2,256,128]{4,3,2,1,0:T(8,128)S(1)}, f32[1,2,2,256,128]{4,3,2,1,0:T(8,128)S(1)}, u32[]{:S(2)}, u32[]{:S(2)}) %collective-permute-start) | collective-permute-done | bytes 524320 | tf_op jit(solution)/shard_map/ppermute | solution.py:310
  7.7 2.1 %tail_cells.1 = f32[1,16,32,128]{3,2,1,0:T(8,128)S(1)} custom-call(f32[1,2,2,256,128]{4,3,2,1,0:T(8,128)S(1)} %collective-permute-done.incoming_ref, bf16[1,2,2,256,512]{4,3,2,1,0:T(8,128)(2,1)S(1)} %get-tuple-element.11.left_ref, bf16[1,2,2,512,512]{4,3,2,1,0:T(8,128)(2,1)S(1)} %get-tuple-element.12.right_ref, ...), custom_call_target="tpu_custom_call", output_to_operand_aliasing={{}: (5, {})} | custom-call | tf_op jit(solution)/shard_map/tail_cells/pallas_call | solution.py:250
  9.8 16.9 %all_to_all.4 = f32[1,16,32,128]{3,2,0,1:T(8,128)} all-to-all(f32[1,16,32,128]{3,2,0,1:T(8,128)S(1)} %bitcast.7), channel_id=1, replica_groups=mesh['chain'=2,'energy'=16] {'energy'}, dimensions={1} | all-to-all | bytes 524288 | tf_op jit(solution)/shard_map/all_to_all | solution.py:313
  26.8 1.9 %lag_sums.1 = f32[16,32,128]{2,1,0:T(8,128)} custom-call(f32[16,32,128]{2,1,0:T(8,128)} %bitcast.8), custom_call_target="tpu_custom_call" | custom-call | tf_op jit(solution)/shard_map/lag_sums/pallas_call | solution.py:289
Async XLA Ops:
  5.7 2.0 %collective-permute-start = (f32[1,2,2,256,128]{4,3,2,1,0:T(8,128)S(1)}, f32[1,2,2,256,128]{4,3,2,1,0:T(8,128)S(1)}, u32[]{:S(2)}, u32[]{:S(2)}) collective-permute-start(f32[1,2,2,256,128]{4,3,2,1,0:T(8,128)S(1)} %get-tuple-element.10), channel_id=1, source_target_pairs={{0,16},{16,0},{1,17},{17,1},{2,18},{18,2},{3,19},{19,3},{4,20},{20... | collective-permute-start | bytes 1572872 | tf_op jit(solution)/shard_map/ppermute | solution.py:310

commit v5 on v4

--- a/solution.py
+++ b/solution.py
@@ -93,7 +93,7 @@
             first = (cell * keep + k) * half
             for s in range(0, half, piece):
                 owner, inside = divmod(first + s, share_rows)
-                send_ref[e, owner, pl.ds(part * share_rows + inside, piece), :] = flat[s:s + piece]
+                send_ref[e, send_ref.shape[1] - 1 - owner, pl.ds(part * share_rows + inside, piece), :] = flat[s:s + piece]
 
 
 def head_kernel(keep, share_rows, g_hbm, s_hbm, b_hbm, pattern_hbm, kept_hbm, lead_hbm,
@@ -264,33 +264,50 @@
     return (leaving, result[0]) if last else result
 
 
-def lag_kernel(in_ref, out_ref):
+def lag_kernel(here, in_ref, out_hbm, out_ref, sems):
     energies, double_rows, _ = in_ref.shape
     rows = double_rows // 2
     step = min(8, rows)
     scale = 1.0 / energies
-    for first in range(0, rows, step):
-        re = [in_ref[e, first:first + step] for e in range(energies)]
-        im = [in_ref[e, rows + first:rows + first + step] for e in range(energies)]
-        for lag in range(LAGS):
-            real_sum = jnp.zeros((step, LANES), F32)
-            imag_sum = jnp.zeros((step, LANES), F32)
-            for e in range(energies - lag):
-                real_sum += re[e + lag] * re[e] + im[e + lag] * im[e]
-                imag_sum += im[e + lag] * re[e] - re[e + lag] * im[e]
-            out_ref[lag, pl.ds(2 * first, step, 2), :] = real_sum * scale
-            out_ref[lag, pl.ds(2 * first + 1, step, 2), :] = imag_sum * scale
-
-
-def lag_sums(owned):
+    groups = sems.shape[0]
+    width = LAGS // groups
+
+    def at(e, first):
+        place = (energies // here - 1 - e // here) * here + e % here
+        return in_ref[place, first:first + step]
+
+    copies = []
+    for group in range(groups):
+        for lag in range(group * width, (group + 1) * width):
+            for first in range(0, rows, step):
+                real_sum = jnp.zeros((step, LANES), F32)
+                imag_sum = jnp.zeros((step, LANES), F32)
+                for e in range(energies - lag):
+                    late_re, late_im = at(e + lag, first), at(e + lag, rows + first)
+                    early_re, early_im = at(e, first), at(e, rows + first)
+                    real_sum += late_re * early_re + late_im * early_im
+                    imag_sum += late_im * early_re - late_re * early_im
+                out_ref[lag, pl.ds(2 * first, step, 2), :] = real_sum * scale
+                out_ref[lag, pl.ds(2 * first + 1, step, 2), :] = imag_sum * scale
+        part = pl.ds(group * width, width)
+        copies.append(pltpu.make_async_copy(out_ref.at[part], out_hbm.at[part], sems.at[group]))
+        copies[-1].start()
+    for copy in copies:
+        copy.wait()
+
+
+def lag_sums(here, owned):
     energies, double_rows, lanes = owned.shape
     rows = double_rows // 2
-    vmem = pl.BlockSpec(memory_space=pltpu.VMEM)
     sums = pl.pallas_call(
-        lag_kernel,
+        functools.partial(lag_kernel, here),
         out_shape=jax.ShapeDtypeStruct((LAGS, double_rows, lanes), F32),
-        in_specs=[vmem],
-        out_specs=vmem,
+        in_specs=[pl.BlockSpec(memory_space=pltpu.VMEM)],
+        out_specs=pl.BlockSpec(memory_space=pltpu.HBM),
+        scratch_shapes=[
+            pltpu.VMEM((LAGS, double_rows, lanes), F32),
+            pltpu.SemaphoreType.DMA((4,)),
+        ],
         name="lag_sums",
     )(owned)
     sums = sums.reshape(LAGS, rows, 2, lanes)
@@ -310,8 +327,9 @@
         incoming = lax.ppermute(leaving, "chain", [(i, (i + 1) % length) for i in range(length)])
         last = hop == length - 2
         leaving, send = tail(keep, share_rows, hop, last, incoming, left, right, fresh, kept_blocks, leaving, send)
-    owned = lax.all_to_all(send, "energy", split_axis=1, concat_axis=0, tiled=True)
-    return lag_sums(owned.reshape((-1,) + owned.shape[2:]))
+    backwards = [list(range(owners))[::-1]]
+    owned = lax.all_to_all(send, "energy", split_axis=1, concat_axis=0, axis_index_groups=backwards, tiled=True)
+    return lag_sums(retarded.shape[0], owned.reshape((-1,) + owned.shape[2:]))
 
 
 def solution(mesh):

time: 28.9 us -> 27.4 us (0.948)
  blocking collectives: 16.9 us -> 15.3 us
    all_to_all x1, blocking collectives: 16.9 us -> 15.3 us  [per_device(): lax.all_to_all(send, 'energy', split_axis=1, concat_axis=0, axis_index_gr...]
where the time goes in v5:
time: 27.4 us; the launch traced here: 27 us
  blocking collectives  15.3 us (56%)
  Pallas kernels  9.73 us (36%)
  waiting for transfers between devices  1.67 us (6%)
  starting transfers between devices  0.31 us (1%)
    all_to_all x1, blocking collectives, per_device(): lax.all_to_all(send, 'energy', split_axis=1, concat_axis=0, axis_index_gr...  15.3 us
    pallas_call x1, Pallas kernels, head(): pl.pallas_call(functools.partial(head_kernel, keep, share_rows), out_shap...  5.7 us
    pallas_call x1, Pallas kernels, tail(): pl.pallas_call(functools.partial(tail_kernel, keep, share_rows, hop, last...  2.12 us
    pallas_call x1, Pallas kernels, lag_sums(): pl.pallas_call(functools.partial(lag_kernel, here), out_shape=jax.ShapeDt...  1.91 us
    ppermute x1, waiting for transfers between devices, per_device(): lax.ppermute(leaving, 'chain', [(i, (i + 1) % length) for i in range(leng...  1.67 us
  transfers between devices with their start and end apart: 1, of which 1 were waited for; matrix products, arithmetic and copies ran while one was open for 0% of the time, Pallas kernels for 0%

profile of v5, /device:TPU:1, one launch (start us, length us, event | category | flops | bytes accessed | tf_op | source)
XLA Modules:
  0.0 27.0 jit_solution(12353500159277372807)
XLA Ops:
  0.0 5.7 %head_cells.1 = (f32[1,2,2,256,128]{4,3,2,1,0:T(8,128)S(1)}, f32[1,16,32,128]{3,2,1,0:T(8,128)S(1)}, bf16[1,2,2,256,512]{4,3,2,1,0:T(8,128)(2,1)S(1)}, bf16[1,2,...) custom-call(f32[1,2,2,256,256]{4,3,2,1,0:T(8,128)} %g_hbm.1, f32[1,2,2,256,256]{4,3,2,1,0:T(8,128)} %s_hbm.1, ...), custom_call_target="tpu_custom_call" | custom-call | tf_op jit(solution)/shard_map/head_cells/pallas_call | solution.py:191
  5.7 0.3 %collective-permute-start = (f32[1,2,2,256,128]{4,3,2,1,0:T(8,128)S(1)}, f32[1,2,2,256,128]{4,3,2,1,0:T(8,128)S(1)}, u32[]{:S(2)}, u32[]{:S(2)}) collective-permute-start(f32[1,2,2,256,128]{4,3,2,1,0:T(8,128)S(1)} %get-tuple-element.10), channel_id=1, source_target_pairs={{0,16},{16,0},{1,17},{17,1},{2,18},{18,2},{3,19},{19,3},{4,20},{20... | collective-permute-start | bytes 1572872 | tf_op jit(solution)/shard_map/ppermute | solution.py:327
  6.0 1.7 %collective-permute-done.incoming_ref = f32[1,2,2,256,128]{4,3,2,1,0:T(8,128)S(1)} collective-permute-done((f32[1,2,2,256,128]{4,3,2,1,0:T(8,128)S(1)}, f32[1,2,2,256,128]{4,3,2,1,0:T(8,128)S(1)}, u32[]{:S(2)}, u32[]{:S(2)}) %collective-permute-start) | collective-permute-done | bytes 524320 | tf_op jit(solution)/shard_map/ppermute | solution.py:327
  7.7 2.1 %tail_cells.1 = f32[1,16,32,128]{3,2,1,0:T(8,128)S(1)} custom-call(f32[1,2,2,256,128]{4,3,2,1,0:T(8,128)S(1)} %collective-permute-done.incoming_ref, bf16[1,2,2,256,512]{4,3,2,1,0:T(8,128)(2,1)S(1)} %get-tuple-element.11.left_ref, bf16[1,2,2,512,512]{4,3,2,1,0:T(8,128)(2,1)S(1)} %get-tuple-element.12.right_ref, ...), custom_call_target="tpu_custom_call", output_to_operand_aliasing={{}: (5, {})} | custom-call | tf_op jit(solution)/shard_map/tail_cells/pallas_call | solution.py:250
  9.8 15.3 %all_to_all.4 = f32[1,16,32,128]{3,2,0,1:T(8,128)} all-to-all(f32[1,16,32,128]{3,2,0,1:T(8,128)S(1)} %bitcast.7), channel_id=1, replica_groups={{15,14,13,12,11,10,9,8,7,6,5,4,3,2,1,0},{31,30,29,28,27,26,25,24,23,22,..., dimensions={1} | all-to-all | bytes 524288 | tf_op jit(solution)/shard_map/all_to_all | solution.py:331
  25.1 1.9 %lag_sums.1 = f32[16,32,128]{2,1,0:T(8,128)} custom-call(f32[16,32,128]{2,1,0:T(8,128)} %bitcast.8), custom_call_target="tpu_custom_call" | custom-call | tf_op jit(solution)/shard_map/lag_sums/pallas_call | solution.py:302
Async XLA Ops:
  5.7 2.0 %collective-permute-start = (f32[1,2,2,256,128]{4,3,2,1,0:T(8,128)S(1)}, f32[1,2,2,256,128]{4,3,2,1,0:T(8,128)S(1)}, u32[]{:S(2)}, u32[]{:S(2)}) collective-permute-start(f32[1,2,2,256,128]{4,3,2,1,0:T(8,128)S(1)} %get-tuple-element.10), channel_id=1, source_target_pairs={{0,16},{16,0},{1,17},{17,1},{2,18},{18,2},{3,19},{19,3},{4,20},{20... | collective-permute-start | bytes 1572872 | tf_op jit(solution)/shard_map/ppermute | solution.py:327

commit v6 on v5

--- a/solution.py
+++ b/solution.py
@@ -73,7 +73,17 @@
     return jnp.concatenate(rows, axis=0)
 
 
+def sending_order(owners):
+    half = [0]
+    while len(half) * 2 < owners:
+        half = [2 * n for n in half] + [2 * n + 1 for n in half]
+    if len(half) * 2 != owners:
+        return list(range(owners))[::-1]
+    return [n for near in half for n in (owners - 1 - near, near)]
+
+
 def pick_into(send_ref, e, cell, matrix_ref, kept_ref, keep, share_rows):
+    order = sending_order(send_ref.shape[1])
     nblk = matrix_ref.shape[-2] // BLOCK
     half = BLOCK // 2
     lane = lax.broadcasted_iota(jnp.int32, (half, LANES), 1)
@@ -93,7 +103,7 @@
             first = (cell * keep + k) * half
             for s in range(0, half, piece):
                 owner, inside = divmod(first + s, share_rows)
-                send_ref[e, send_ref.shape[1] - 1 - owner, pl.ds(part * share_rows + inside, piece), :] = flat[s:s + piece]
+                send_ref[e, order.index(owner), pl.ds(part * share_rows + inside, piece), :] = flat[s:s + piece]
 
 
 def head_kernel(keep, share_rows, g_hbm, s_hbm, b_hbm, pattern_hbm, kept_hbm, lead_hbm,
@@ -272,23 +282,32 @@
     groups = sems.shape[0]
     width = LAGS // groups
 
-    def at(e, first):
-        place = (energies // here - 1 - e // here) * here + e % here
-        return in_ref[place, first:first + step]
+    order = sending_order(energies // here)
+
+    def at(e, part):
+        place = order.index(e // here) * here + e % here
+        start = part * rows
+        return [in_ref[place, start + first:start + first + step] for first in range(0, rows, step)]
 
     copies = []
     for group in range(groups):
-        for lag in range(group * width, (group + 1) * width):
-            for first in range(0, rows, step):
-                real_sum = jnp.zeros((step, LANES), F32)
-                imag_sum = jnp.zeros((step, LANES), F32)
-                for e in range(energies - lag):
-                    late_re, late_im = at(e + lag, first), at(e + lag, rows + first)
-                    early_re, early_im = at(e, first), at(e, rows + first)
-                    real_sum += late_re * early_re + late_im * early_im
-                    imag_sum += late_im * early_re - late_re * early_im
-                out_ref[lag, pl.ds(2 * first, step, 2), :] = real_sum * scale
-                out_ref[lag, pl.ds(2 * first + 1, step, 2), :] = imag_sum * scale
+        lags = range(group * width, (group + 1) * width)
+        sums = {}
+        for e in range(energies):
+            early_re, early_im = at(e, 0), at(e, 1)
+            for lag in lags:
+                if e + lag >= energies:
+                    continue
+                late_re, late_im = at(e + lag, 0), at(e + lag, 1)
+                for n in range(rows // step):
+                    re = late_re[n] * early_re[n] + late_im[n] * early_im[n]
+                    im = late_im[n] * early_re[n] - late_re[n] * early_im[n]
+                    if (lag, n) in sums:
+                        re, im = sums[lag, n][0] + re, sums[lag, n][1] + im
+                    sums[lag, n] = re, im
+        for (lag, n), (re, im) in sums.items():
+            out_ref[lag, pl.ds(2 * n * step, step, 2), :] = re * scale
+            out_ref[lag, pl.ds(2 * n * step + 1, step, 2), :] = im * scale
         part = pl.ds(group * width, width)
         copies.append(pltpu.make_async_copy(out_ref.at[part], out_hbm.at[part], sems.at[group]))
         copies[-1].start()
@@ -327,8 +346,8 @@
         incoming = lax.ppermute(leaving, "chain", [(i, (i + 1) % length) for i in range(length)])
         last = hop == length - 2
         leaving, send = tail(keep, share_rows, hop, last, incoming, left, right, fresh, kept_blocks, leaving, send)
-    backwards = [list(range(owners))[::-1]]
-    owned = lax.all_to_all(send, "energy", split_axis=1, concat_axis=0, axis_index_groups=backwards, tiled=True)
+    groups = [sending_order(owners)]
+    owned = lax.all_to_all(send, "energy", split_axis=1, concat_axis=0, axis_index_groups=groups, tiled=True)
     return lag_sums(retarded.shape[0], owned.reshape((-1,) + owned.shape[2:]))
 
 

time: 27.4 us -> 27.8 us (1.015)
  no operation moved by 1% of the time
where the time goes in v6:
time: 27.8 us; the launch traced here: 27.2 us
  blocking collectives  15.5 us (56%)
  Pallas kernels  9.73 us (35%)
  waiting for transfers between devices  1.68 us (6%)
  starting transfers between devices  0.29 us (1%)
    all_to_all x1, blocking collectives, per_device(): lax.all_to_all(send, 'energy', split_axis=1, concat_axis=0, axis_index_gr...  15.5 us
    pallas_call x1, Pallas kernels, head(): pl.pallas_call(functools.partial(head_kernel, keep, share_rows), out_shap...  5.7 us
    pallas_call x1, Pallas kernels, tail(): pl.pallas_call(functools.partial(tail_kernel, keep, share_rows, hop, last...  2.12 us
    pallas_call x1, Pallas kernels, lag_sums(): pl.pallas_call(functools.partial(lag_kernel, here), out_shape=jax.ShapeDt...  1.91 us
    ppermute x1, waiting for transfers between devices, per_device(): lax.ppermute(leaving, 'chain', [(i, (i + 1) % length) for i in range(leng...  1.68 us
  transfers between devices with their start and end apart: 1, of which 1 were waited for; matrix products, arithmetic and copies ran while one was open for 0% of the time, Pallas kernels for 0%

profile of v6, /device:TPU:1, one launch (start us, length us, event | category | flops | bytes accessed | tf_op | source)
XLA Modules:
  0.0 27.2 jit_solution(11739212635951914524)
XLA Ops:
  0.0 5.7 %head_cells.1 = (f32[1,2,2,256,128]{4,3,2,1,0:T(8,128)S(1)}, f32[1,16,32,128]{3,2,1,0:T(8,128)S(1)}, bf16[1,2,2,256,512]{4,3,2,1,0:T(8,128)(2,1)S(1)}, bf16[1,2,...) custom-call(f32[1,2,2,256,256]{4,3,2,1,0:T(8,128)} %g_hbm.1, f32[1,2,2,256,256]{4,3,2,1,0:T(8,128)} %s_hbm.1, ...), custom_call_target="tpu_custom_call" | custom-call | tf_op jit(solution)/shard_map/head_cells/pallas_call | solution.py:201
  5.7 0.3 %collective-permute-start = (f32[1,2,2,256,128]{4,3,2,1,0:T(8,128)S(1)}, f32[1,2,2,256,128]{4,3,2,1,0:T(8,128)S(1)}, u32[]{:S(2)}, u32[]{:S(2)}) collective-permute-start(f32[1,2,2,256,128]{4,3,2,1,0:T(8,128)S(1)} %get-tuple-element.10), channel_id=1, source_target_pairs={{0,16},{16,0},{1,17},{17,1},{2,18},{18,2},{3,19},{19,3},{4,20},{20... | collective-permute-start | bytes 1572872 | tf_op jit(solution)/shard_map/ppermute | solution.py:346
  6.0 1.7 %collective-permute-done.incoming_ref = f32[1,2,2,256,128]{4,3,2,1,0:T(8,128)S(1)} collective-permute-done((f32[1,2,2,256,128]{4,3,2,1,0:T(8,128)S(1)}, f32[1,2,2,256,128]{4,3,2,1,0:T(8,128)S(1)}, u32[]{:S(2)}, u32[]{:S(2)}) %collective-permute-start) | collective-permute-done | bytes 524320 | tf_op jit(solution)/shard_map/ppermute | solution.py:346
  7.7 2.1 %tail_cells.1 = f32[1,16,32,128]{3,2,1,0:T(8,128)S(1)} custom-call(f32[1,2,2,256,128]{4,3,2,1,0:T(8,128)S(1)} %collective-permute-done.incoming_ref, bf16[1,2,2,256,512]{4,3,2,1,0:T(8,128)(2,1)S(1)} %get-tuple-element.11.left_ref, bf16[1,2,2,512,512]{4,3,2,1,0:T(8,128)(2,1)S(1)} %get-tuple-element.12.right_ref, ...), custom_call_target="tpu_custom_call", output_to_operand_aliasing={{}: (5, {})} | custom-call | tf_op jit(solution)/shard_map/tail_cells/pallas_call | solution.py:260
  9.8 15.5 %all_to_all.4 = f32[1,16,32,128]{3,2,0,1:T(8,128)} all-to-all(f32[1,16,32,128]{3,2,0,1:T(8,128)S(1)} %bitcast.7), channel_id=1, replica_groups={{15,0,11,4,13,2,9,6,14,1,10,5,12,3,8,7},{31,16,27,20,29,18,25,22,30,17,..., dimensions={1} | all-to-all | bytes 524288 | tf_op jit(solution)/shard_map/all_to_all | solution.py:350
  25.3 1.9 %lag_sums.1 = f32[16,32,128]{2,1,0:T(8,128)} custom-call(f32[16,32,128]{2,1,0:T(8,128)} %bitcast.8), custom_call_target="tpu_custom_call" | custom-call | tf_op jit(solution)/shard_map/lag_sums/pallas_call | solution.py:321
Async XLA Ops:
  5.7 2.0 %collective-permute-start = (f32[1,2,2,256,128]{4,3,2,1,0:T(8,128)S(1)}, f32[1,2,2,256,128]{4,3,2,1,0:T(8,128)S(1)}, u32[]{:S(2)}, u32[]{:S(2)}) collective-permute-start(f32[1,2,2,256,128]{4,3,2,1,0:T(8,128)S(1)} %get-tuple-element.10), channel_id=1, source_target_pairs={{0,16},{16,0},{1,17},{17,1},{2,18},{18,2},{3,19},{19,3},{4,20},{20... | collective-permute-start | bytes 1572872 | tf_op jit(solution)/shard_map/ppermute | solution.py:346

commit v7 on v5

v7 whole, which is shorter than its diff:
```python
import functools

import jax
import jax.numpy as jnp
from jax import lax
from jax.experimental import pallas as pl
from jax.experimental.pallas import tpu as pltpu
from jax.sharding import PartitionSpec as P

BLOCK = 64
LAGS = 16
LANES = 128
F32 = jnp.float32
BF16 = jnp.bfloat16


def two_parts(value):
    high = value.astype(BF16)
    return high, (value - high.astype(F32)).astype(BF16)


def dot(left, right):
    return lax.dot_general(left, right, (((1,), (0,)), ((), ())), preferred_element_type=F32)


def left_parts(pair):
    return two_parts(jnp.concatenate(pair, axis=1))


def right_parts(pair):
    both = []
    for re, im in zip(two_parts(pair[0]), two_parts(pair[1])):
        both.append(jnp.concatenate([jnp.concatenate([re, im], axis=1), jnp.concatenate([-im, re], axis=1)], axis=0))
    return tuple(both)


def adjoint(pair):
    return pair[0].T, -pair[1].T


def product(left, right):
    wide = jnp.concatenate([left[0], left[0], left[1]], axis=1)
    tall = jnp.concatenate([right[0], right[1], right[0]], axis=0)
    both = dot(wide, tall)
    half = both.shape[1] // 2
    return both[:, :half], both[:, half:]


def plus(one, other):
    return one[0] + other[0], one[1] + other[1]


def put_state(state_ref, pair):
    for part in range(2):
        for group in range(state_ref.shape[1]):
            state_ref[part, group] = pair[part][:, group * LANES:(group + 1) * LANES]


def get_state(state_ref):
    groups = range(state_ref.shape[1])
    return tuple(jnp.concatenate([state_ref[part, group] for group in groups], axis=1) for part in range(2))


def block_mask(size, value_of):
    nblk = size // BLOCK
    column = lax.broadcasted_iota(jnp.int32, (BLOCK, size), 1) // BLOCK
    rows = []
    for r in range(nblk):
        row = jnp.zeros((BLOCK, size), F32)
        for c in range(nblk):
            row = jnp.where(column == c, value_of(r, c).astype(F32), row)
        rows.append(row)
    return jnp.concatenate(rows, axis=0)


def pick_into(send_ref, e, cell, matrix_ref, kept_ref, keep, share_rows):
    nblk = matrix_ref.shape[-2] // BLOCK
    owners = send_ref.shape[1]
    half = BLOCK // 2
    lane = lax.broadcasted_iota(jnp.int32, (half, LANES), 1)
    piece = min(half, share_rows)
    per_share = share_rows // piece
    for k in range(keep):
        number = kept_ref[k]
        top = (number // nblk) * BLOCK
        across = (number % nblk) * BLOCK
        window = across // LANES
        in_upper = jnp.full((half, LANES), across % LANES, jnp.int32) > 0
        for part in range(2):
            even = matrix_ref[part, window, pl.ds(top, half, 2), :]
            odd = matrix_ref[part, window, pl.ds(top + 1, half, 2), :]
            left = jnp.where(in_upper, pltpu.roll(even, BLOCK, 1), even)
            right = jnp.where(in_upper, odd, pltpu.roll(odd, BLOCK, 1))
            flat = jnp.where(lane < BLOCK, left, right)
            for s in range(half // piece):
                index = (cell * keep + k) * (half // piece) + s
                owner, inside = index, 0
                if per_share > 1:
                    owner, inside = index // per_share, pl.multiple_of(index % per_share * piece, piece)
                rows = pl.ds(part * share_rows + inside, piece)
                send_ref[e, owners - 1 - owner, rows, :] = flat[s * piece:(s + 1) * piece]


def put_parts(ref, parts):
    ref[0], ref[1] = parts


def parts_of(ref):
    return ref[0], ref[1]


def head_kernel(keep, share_rows, g_hbm, s_hbm, b_hbm, pattern_hbm, kept_hbm, lead_hbm,
                leaving_ref, send_ref, left_ref, right_ref, fresh_ref,
                pattern_ref, kept_ref, m_ref, s_ref, lead_ref, m_left, state_right, joined_right, sems, m_sems):
    energies, cells, _, size, _ = s_ref.shape
    position = lax.axis_index("chain")
    is_first = position == 0

    def m_copy(e, k, i, source_hbm):
        source = source_hbm.at[i] if source_hbm is b_hbm else source_hbm.at[e, i]
        return pltpu.make_async_copy(source, m_ref.at[e, k], m_sems.at[e, k])

    lead_copy = pltpu.make_async_copy(lead_hbm, lead_ref, sems.at[0])
    pattern_copy = pltpu.make_async_copy(pattern_hbm, pattern_ref, sems.at[1])
    kept_copy = pltpu.make_async_copy(kept_hbm, kept_ref, sems.at[2])

    def s_copy(i):
        return pltpu.make_async_copy(s_hbm.at[:, i], s_ref.at[:, i], sems.at[3 + i])

    pattern_copy.start()
    kept_copy.start()

    @pl.when(is_first)
    def _():
        lead_copy.start()

    for i in range(cells):
        for e in range(energies):
            m_copy(e, 2 * i, i, b_hbm).start()
        s_copy(i).start()
        for e in range(energies):
            m_copy(e, 2 * i + 1, i, g_hbm).start()
    pattern_copy.wait()
    kept_copy.wait()

    def matrix(ref, e, i):
        return ref[e, i, 0], ref[e, i, 1]

    def masked(e, k):
        bridge = k % 2 == 0
        mask = block_mask(size, lambda r, c: jnp.where(bridge, pattern_ref[k // 2, r, c], 1))
        return m_ref[e, k, 0] * mask, m_ref[e, k, 1] * mask

    @pl.when(is_first)
    def _():
        lead_copy.wait()
        for e in range(energies):
            put_parts(state_right.at[e], right_parts((lead_ref[e, 0], lead_ref[e, 1])))

    @pl.when(jnp.logical_not(is_first))
    def _():
        s_copy(0).wait()
        for e in range(energies):
            m_copy(e, 0, 0, b_hbm).wait()
            put_parts(state_right.at[e], right_parts(matrix(s_ref, e, 0)))
            put_parts(joined_right.at[e], right_parts(masked(e, 0)))

    def step(k, carry):
        cell = k // 2
        done = k % 2 == 1

        @pl.when(jnp.logical_not(done))
        def _():
            s_copy(cell).wait()

        kept_share = (1 - k % 2).astype(F32)
        for e in range(energies):
            m_copy(e, k, 0, b_hbm).wait()
            factor = masked(e, k)
            left = left_parts(factor)
            put_parts(m_left, left)
            half = left_parts(product(left, parts_of(state_right.at[e])))
            grown = product(half, right_parts(adjoint(factor)))
            added = matrix(s_ref, e, cell)
            state = plus(grown, (added[0] * kept_share, added[1] * kept_share))
            put_parts(state_right.at[e], right_parts(state))
            put_state(fresh_ref.at[e, cell], state)

            @pl.when(jnp.logical_not(is_first))
            def _():
                joined = product(parts_of(m_left), parts_of(joined_right.at[e]))
                put_parts(joined_right.at[e], right_parts(joined))

                @pl.when(done)
                def _():
                    put_parts(left_ref.at[e, cell], left_parts(joined))
                    put_parts(right_ref.at[e, cell], right_parts(adjoint(joined)))

            @pl.when(jnp.logical_and(is_first, done))
            def _():
                pick_into(send_ref, e, cell, fresh_ref.at[e, cell], kept_ref, keep, share_rows)

        return carry

    lax.fori_loop(jnp.where(is_first, 0, 1), 2 * cells, step, 0)

    @pl.when(is_first)
    def _():
        for e in range(energies):
            leaving_ref[e] = fresh_ref[e, cells - 1]


def in_hbm(value):
    return pltpu.with_memory_space_constraint(value, pltpu.HBM)


def head(keep, share_rows, owners, retarded, lesser_sigma, coupling, pattern, kept_blocks, lead):
    energies, cells, _, size, _ = retarded.shape
    hbm = pl.BlockSpec(memory_space=pltpu.HBM)
    vmem = pl.BlockSpec(memory_space=pltpu.VMEM)
    state_shape = (2, size // LANES, size, LANES)
    return pl.pallas_call(
        functools.partial(head_kernel, keep, share_rows),
        out_shape=(
            jax.ShapeDtypeStruct((energies,) + state_shape, F32),
            jax.ShapeDtypeStruct((energies, owners, 2 * share_rows, LANES), F32),
            jax.ShapeDtypeStruct((energies, cells, 2, size, 2 * size), BF16),
            jax.ShapeDtypeStruct((energies, cells, 2, 2 * size, 2 * size), BF16),
            jax.ShapeDtypeStruct((energies, cells) + state_shape, F32),
        ),
        in_specs=[hbm] * 6,
        out_specs=(vmem,) * 5,
        scratch_shapes=[
            pltpu.SMEM(pattern.shape, jnp.int32),
            pltpu.SMEM(kept_blocks.shape, jnp.int32),
            pltpu.VMEM((energies, 2 * cells, 2, size, size), F32),
            pltpu.VMEM(lesser_sigma.shape, F32),
            pltpu.VMEM(lead.shape, F32),
            pltpu.VMEM((2, size, 2 * size), BF16),
            pltpu.VMEM((energies, 2, 2 * size, 2 * size), BF16),
            pltpu.VMEM((energies, 2, 2 * size, 2 * size), BF16),
            pltpu.SemaphoreType.DMA((3 + cells,)),
            pltpu.SemaphoreType.DMA((energies, 2 * cells)),
        ],
        compiler_params=pltpu.CompilerParams(vmem_limit_bytes=32 << 20),
        name="head_cells",
    )(*(in_hbm(x) for x in (retarded, lesser_sigma, coupling, pattern, kept_blocks, lead)))


def tail_kernel(keep, share_rows, hop, last, incoming_ref, left_ref, right_ref, fresh_ref, kept_hbm, *refs):
    if last:
        (_, send_ref), refs = refs[:2], refs[2:]
        leaving_ref = None
    else:
        (_, _, leaving_ref, send_ref), refs = refs[:4], refs[4:]
    kept_ref, state_ref, state_right, sem = refs
    energies, cells = fresh_ref.shape[:2]

    @pl.when(lax.axis_index("chain") == hop + 1)
    def _():
        kept_copy = pltpu.make_async_copy(kept_hbm, kept_ref, sem)
        kept_copy.start()
        for e in range(energies):
            put_parts(state_right.at[e], right_parts(get_state(incoming_ref.at[e])))
        kept_copy.wait()

        def step(i, carry):
            for e in range(energies):
                half = left_parts(product(parts_of(left_ref.at[e, i]), parts_of(state_right.at[e])))
                grown = product(half, parts_of(right_ref.at[e, i]))
                put_state(state_ref.at[e], plus(get_state(fresh_ref.at[e, i]), grown))
                pick_into(send_ref, e, i, state_ref.at[e], kept_ref, keep, share_rows)
            return carry

        lax.fori_loop(0, cells, step, 0)
        if not last:
            leaving_ref[...] = state_ref[...]


def tail(keep, share_rows, hop, last, incoming, left, right, fresh, kept_blocks, leaving, send):
    energies = fresh.shape[0]
    hbm = pl.BlockSpec(memory_space=pltpu.HBM)
    vmem = pl.BlockSpec(memory_space=pltpu.VMEM)
    carried = (send,) if last else (leaving, send)
    result = pl.pallas_call(
        functools.partial(tail_kernel, keep, share_rows, hop, last),
        out_shape=tuple(jax.ShapeDtypeStruct(value.shape, F32) for value in carried),
        in_specs=[vmem] * 4 + [hbm] + [vmem] * len(carried),
        out_specs=(vmem,) * len(carried),
        input_output_aliases={5 + i: i for i in range(len(carried))},
        scratch_shapes=[
            pltpu.SMEM(kept_blocks.shape, jnp.int32),
            pltpu.VMEM(incoming.shape, F32),
            pltpu.VMEM((energies,) + right.shape[2:], BF16),
            pltpu.SemaphoreType.DMA,
        ],
        compiler_params=pltpu.CompilerParams(vmem_limit_bytes=32 << 20),
        name="tail_cells",
    )(incoming, left, right, fresh, in_hbm(kept_blocks), *carried)
    return (leaving, result[0]) if last else result


def lag_kernel(here, in_ref, out_hbm, out_ref, all_ref, sems):
    energies, double_rows, _ = in_ref.shape
    rows = double_rows // 2
    step = min(8, rows)
    scale = 1.0 / energies
    for e in range(energies):
        all_ref[e] = in_ref[(energies // here - 1 - e // here) * here + e % here]
    for e in range(energies, all_ref.shape[0]):
        all_ref[e] = jnp.zeros((double_rows, LANES), F32)

    def out_copy(lag):
        return pltpu.make_async_copy(out_ref.at[lag], out_hbm.at[lag], sems.at[lag])

    def one_lag(lag, carry):
        for first in range(0, rows, step):
            sums = [jnp.zeros((step, LANES), F32) for _ in range(4)]
            for e in range(energies):
                early_re, early_im = all_ref[e, pl.ds(first, step)], all_ref[e, pl.ds(rows + first, step)]
                late_re, late_im = all_ref[e + lag, pl.ds(first, step)], all_ref[e + lag, pl.ds(rows + first, step)]
                sums[0] += late_re * early_re
                sums[1] += late_im * early_im
                sums[2] += late_im * early_re
                sums[3] += late_re * early_im
            out_ref[lag, pl.ds(2 * first, step, 2), :] = (sums[0] + sums[1]) * scale
            out_ref[lag, pl.ds(2 * first + 1, step, 2), :] = (sums[2] - sums[3]) * scale
        out_copy(lag).start()
        return carry

    def finish(lag, carry):
        out_copy(lag).wait()
        return carry

    lax.fori_loop(0, LAGS, one_lag, 0)
    lax.fori_loop(0, LAGS, finish, 0)


def lag_sums(here, owned):
    energies, double_rows, lanes = owned.shape
    rows = double_rows // 2
    sums = pl.pallas_call(
        functools.partial(lag_kernel, here),
        out_shape=jax.ShapeDtypeStruct((LAGS, double_rows, lanes), F32),
        in_specs=[pl.BlockSpec(memory_space=pltpu.VMEM)],
        out_specs=pl.BlockSpec(memory_space=pltpu.HBM),
        scratch_shapes=[
            pltpu.VMEM((LAGS, double_rows, lanes), F32),
            pltpu.VMEM((energies + LAGS - 1, double_rows, lanes), F32),
            pltpu.SemaphoreType.DMA((LAGS,)),
        ],
        name="lag_sums",
    )(owned)
    sums = sums.reshape(LAGS, rows, 2, lanes)
    return jnp.swapaxes(sums, 1, 2).reshape(LAGS, 2, rows * lanes)


def per_device(retarded, lesser_sigma, coupling, coupling_pattern, kept_blocks, lead_lesser):
    cells = retarded.shape[1]
    keep = kept_blocks.shape[0]
    owners = lax.axis_size("energy")
    length = lax.axis_size("chain")
    share_rows = cells * keep * BLOCK * BLOCK // (owners * LANES)
    leaving, send, left, right, fresh = head(
        keep, share_rows, owners, retarded, lesser_sigma, coupling, coupling_pattern, kept_blocks, lead_lesser
    )
    for hop in range(length - 1):
        incoming = lax.ppermute(leaving, "chain", [(i, (i + 1) % length) for i in range(length)])
        last = hop == length - 2
        leaving, send = tail(keep, share_rows, hop, last, incoming, left, right, fresh, kept_blocks, leaving, send)
    backwards = [list(range(owners))[::-1]]
    owned = lax.all_to_all(send, "energy", split_axis=1, concat_axis=0, axis_index_groups=backwards, tiled=True)
    return lag_sums(retarded.shape[0], owned.reshape((-1,) + owned.shape[2:]))


def solution(mesh):
    return jax.shard_map(
        per_device,
        mesh=mesh,
        in_specs=(
            P("energy", "chain", None, None, None),
            P("energy", "chain", None, None, None),
            P("chain", None, None, None),
            P("chain", None, None),
            P(),
            P("energy", None, None, None),
        ),
        out_specs=P(None, None, ("chain", "energy")),
        check_vma=False,
    )
```

time: 27.4 us -> 29.2 us (1.066)
  Pallas kernels: 9.73 us -> 13.3 us
  blocking collectives: 15.3 us -> 13.6 us
    pallas_call x1, Pallas kernels: 5.7 us -> 7.77 us  [head(): pl.pallas_call(functools.partial(head_kernel, keep, share_rows), out_shap...]
    all_to_all x1, blocking collectives: 15.3 us -> 13.6 us  [per_device(): lax.all_to_all(send, 'energy', split_axis=1, concat_axis=0, axis_index_gr...]
    pallas_call x1, Pallas kernels: 2.12 us -> 3.05 us  [tail(): pl.pallas_call(functools.partial(tail_kernel, keep, share_rows, hop, last...]
    pallas_call x1, Pallas kernels: 1.91 us -> 2.52 us  [lag_sums(): pl.pallas_call(functools.partial(lag_kernel, here), out_shape=jax.ShapeDt...]
where the time goes in v7:
time: 29.2 us; the launch traced here: 29 us
  blocking collectives  13.6 us (47%)
  Pallas kernels  13.3 us (46%)
  waiting for transfers between devices  1.9 us (7%)
    all_to_all x1, blocking collectives, per_device(): lax.all_to_all(send, 'energy', split_axis=1, concat_axis=0, axis_index_gr...  13.6 us
    pallas_call x1, Pallas kernels, head(): pl.pallas_call(functools.partial(head_kernel, keep, share_rows), out_shap...  7.77 us
    pallas_call x1, Pallas kernels, tail(): pl.pallas_call(functools.partial(tail_kernel, keep, share_rows, hop, last...  3.05 us
    pallas_call x1, Pallas kernels, lag_sums(): pl.pallas_call(functools.partial(lag_kernel, here), out_shape=jax.ShapeDt...  2.52 us
    ppermute x1, waiting for transfers between devices, per_device(): lax.ppermute(leaving, 'chain', [(i, (i + 1) % length) for i in range(leng...  1.9 us
  transfers between devices with their start and end apart: 1, of which 1 were waited for; matrix products, arithmetic and copies ran while one was open for 0% of the time, Pallas kernels for 0%

profile of v7, /device:TPU:1, one launch (start us, length us, event | category | flops | bytes accessed | tf_op | source)
XLA Modules:
  0.0 29.0 jit_solution(9020908199042236985)
XLA Ops:
  0.0 7.8 %head_cells.1 = (f32[1,2,2,256,128]{4,3,2,1,0:T(8,128)S(1)}, f32[1,16,32,128]{3,2,1,0:T(8,128)S(1)}, bf16[1,2,2,256,512]{4,3,2,1,0:T(8,128)(2,1)S(1)}, bf16[1,2,...) custom-call(f32[1,2,2,256,256]{4,3,2,1,0:T(8,128)} %g_hbm.1, f32[1,2,2,256,256]{4,3,2,1,0:T(8,128)} %s_hbm.1, ...), custom_call_target="tpu_custom_call" | custom-call | tf_op jit(solution)/shard_map/head_cells/pallas_call | solution.py:222
  7.8 0.1 collective-permute-start
  7.9 1.9 %collective-permute-done.incoming_ref = f32[1,2,2,256,128]{4,3,2,1,0:T(8,128)S(1)} collective-permute-done((f32[1,2,2,256,128]{4,3,2,1,0:T(8,128)S(1)}, f32[1,2,2,256,128]{4,3,2,1,0:T(8,128)S(1)}, u32[]{:S(2)}, u32[]{:S(2)}) %collective-permute-start) | collective-permute-done | bytes 524320 | tf_op jit(solution)/shard_map/ppermute | solution.py:368
  9.8 3.0 %tail_cells.1 = f32[1,16,32,128]{3,2,1,0:T(8,128)S(1)} custom-call(f32[1,2,2,256,128]{4,3,2,1,0:T(8,128)S(1)} %collective-permute-done.incoming_ref, bf16[1,2,2,256,512]{4,3,2,1,0:T(8,128)(2,1)S(1)} %get-tuple-element.11.left_ref, bf16[1,2,2,512,512]{4,3,2,1,0:T(8,128)(2,1)S(1)} %get-tuple-element.12.right_ref, ...), custom_call_target="tpu_custom_call", output_to_operand_aliasing={{}: (5, {})} | custom-call | tf_op jit(solution)/shard_map/tail_cells/pallas_call | solution.py:285
  12.8 13.6 %all_to_all.4 = f32[1,16,32,128]{3,2,0,1:T(8,128)} all-to-all(f32[1,16,32,128]{3,2,0,1:T(8,128)S(1)} %bitcast.7), channel_id=1, replica_groups={{15,14,13,12,11,10,9,8,7,6,5,4,3,2,1,0},{31,30,29,28,27,26,25,24,23,22,..., dimensions={1} | all-to-all | bytes 524288 | tf_op jit(solution)/shard_map/all_to_all | solution.py:372
  26.5 2.5 %lag_sums.1 = f32[16,32,128]{2,1,0:T(8,128)} custom-call(f32[16,32,128]{2,1,0:T(8,128)} %bitcast.8), custom_call_target="tpu_custom_call" | custom-call | tf_op jit(solution)/shard_map/lag_sums/pallas_call | solution.py:342
Async XLA Ops:
  7.8 2.0 %collective-permute-start = (f32[1,2,2,256,128]{4,3,2,1,0:T(8,128)S(1)}, f32[1,2,2,256,128]{4,3,2,1,0:T(8,128)S(1)}, u32[]{:S(2)}, u32[]{:S(2)}) collective-permute-start(f32[1,2,2,256,128]{4,3,2,1,0:T(8,128)S(1)} %get-tuple-element.10), channel_id=1, source_target_pairs={{0,16},{16,0},{1,17},{17,1},{2,18},{18,2},{3,19},{19,3},{4,20},{20... | collective-permute-start | bytes 1572872 | tf_op jit(solution)/shard_map/ppermute | solution.py:368

commit v8 on v5

--- a/solution.py
+++ b/solution.py
@@ -23,15 +23,8 @@
     return lax.dot_general(left, right, (((1,), (0,)), ((), ())), preferred_element_type=F32)
 
 
-def left_parts(pair):
-    return two_parts(jnp.concatenate(pair, axis=1))
-
-
-def right_parts(pair):
-    both = []
-    for re, im in zip(two_parts(pair[0]), two_parts(pair[1])):
-        both.append(jnp.concatenate([jnp.concatenate([re, im], axis=1), jnp.concatenate([-im, re], axis=1)], axis=0))
-    return tuple(both)
+def parts(pair):
+    return tuple(part for value in (pair[0], pair[1], pair[0] + pair[1]) for part in two_parts(value))
 
 
 def adjoint(pair):
@@ -39,11 +32,21 @@
 
 
 def product(left, right):
-    wide = jnp.concatenate([left[0], left[0], left[1]], axis=1)
-    tall = jnp.concatenate([right[0], right[1], right[0]], axis=0)
-    both = dot(wide, tall)
-    half = both.shape[1] // 2
-    return both[:, :half], both[:, half:]
+    real = []
+    for n in range(0, 6, 2):
+        wide = jnp.concatenate([left[n], left[n], left[n + 1]], axis=1)
+        tall = jnp.concatenate([right[n], right[n + 1], right[n]], axis=0)
+        real.append(dot(wide, tall))
+    return real[0] - real[1], real[2] - real[0] - real[1]
+
+
+def put_parts(ref, values):
+    for n, value in enumerate(values):
+        ref[n] = value
+
+
+def get_parts(ref):
+    return tuple(ref[n] for n in range(6))
 
 
 def plus(one, other):
@@ -139,16 +142,16 @@
         for i in range(cells):
             b_copies[i].wait()
             bridge = bridge_of(i)
-            bridge_left, bridge_right = left_parts(bridge), right_parts(adjoint(bridge))
+            bridge_left, bridge_right = parts(bridge), parts(adjoint(bridge))
             for e in range(energies):
-                entered = product(left_parts(product(bridge_left, right_parts(states[e]))), bridge_right)
+                entered = product(parts(product(bridge_left, parts(states[e]))), bridge_right)
                 if e == 0:
                     g_copies[i].wait()
                     s_copies[i].wait()
                 green = matrix(g_ref, e, i)
-                green_left, green_right = left_parts(green), right_parts(adjoint(green))
-                inner = right_parts(plus(matrix(s_ref, e, i), entered))
-                states[e] = product(left_parts(product(green_left, inner)), green_right)
+                green_left, green_right = parts(green), parts(adjoint(green))
+                inner = parts(plus(matrix(s_ref, e, i), entered))
+                states[e] = product(parts(product(green_left, inner)), green_right)
                 out_ref = leaving_ref.at[e] if i == cells - 1 else state_ref.at[e, i]
                 put_state(out_ref, states[e])
                 pick_into(send_ref, e, i, out_ref, kept_ref, keep, share_rows)
@@ -163,19 +166,19 @@
             bridge = bridge_of(i)
             for e in range(energies):
                 green = matrix(g_ref, e, i)
-                green_left, green_right = left_parts(green), right_parts(adjoint(green))
+                green_left, green_right = parts(green), parts(adjoint(green))
                 inner = matrix(s_ref, e, i)
                 if i == 0:
-                    joined[e] = product(green_left, right_parts(bridge))
+                    joined[e] = product(green_left, parts(bridge))
                 else:
-                    bridge_left, bridge_right = left_parts(bridge), right_parts(adjoint(bridge))
-                    half = left_parts(product(bridge_left, right_parts(states[e])))
-                    across = right_parts(product(bridge_left, right_parts(joined[e])))
+                    bridge_left, bridge_right = parts(bridge), parts(adjoint(bridge))
+                    half = parts(product(bridge_left, parts(states[e])))
+                    across = parts(product(bridge_left, parts(joined[e])))
                     inner = plus(inner, product(half, bridge_right))
                     joined[e] = product(green_left, across)
-                states[e] = product(left_parts(product(green_left, right_parts(inner))), green_right)
-                left_ref[e, i, 0], left_ref[e, i, 1] = left_parts(joined[e])
-                right_ref[e, i, 0], right_ref[e, i, 1] = right_parts(adjoint(joined[e]))
+                states[e] = product(parts(product(green_left, parts(inner))), green_right)
+                put_parts(left_ref.at[e, i], parts(joined[e]))
+                put_parts(right_ref.at[e, i], parts(adjoint(joined[e])))
                 fresh_ref[e, i, 0], fresh_ref[e, i, 1] = states[e]
 
 
@@ -193,8 +196,8 @@
         out_shape=(
             jax.ShapeDtypeStruct((energies,) + state_shape, F32),
             jax.ShapeDtypeStruct((energies, owners, 2 * share_rows, LANES), F32),
-            jax.ShapeDtypeStruct((energies, cells, 2, size, 2 * size), BF16),
-            jax.ShapeDtypeStruct((energies, cells, 2, 2 * size, 2 * size), BF16),
+            jax.ShapeDtypeStruct((energies, cells, 6, size, size), BF16),
+            jax.ShapeDtypeStruct((energies, cells, 6, size, size), BF16),
             jax.ShapeDtypeStruct((energies, cells, 2, size, size), F32),
         ),
         in_specs=[hbm] * 6,
@@ -228,12 +231,12 @@
         kept_copy = pltpu.make_async_copy(kept_hbm, kept_ref, sem)
         kept_copy.start()
         for e in range(energies):
-            state = right_parts(get_state(incoming_ref.at[e]))
+            state = parts(get_state(incoming_ref.at[e]))
             halves = []
             for i in range(cells):
-                halves.append(left_parts(product((left_ref[e, i, 0], left_ref[e, i, 1]), state)))
+                halves.append(parts(product(get_parts(left_ref.at[e, i]), state)))
             for i in range(cells):
-                grown = product(halves[i], (right_ref[e, i, 0], right_ref[e, i, 1]))
+                grown = product(halves[i], get_parts(right_ref.at[e, i]))
                 put_state(state_ref.at[e, i], plus((fresh_ref[e, i, 0], fresh_ref[e, i, 1]), grown))
                 if i == 0 and e == 0:
                     kept_copy.wait()

time: 27.4 us -> 26.8 us (0.978)
  Pallas kernels: 9.73 us -> 8.93 us
    pallas_call x1, Pallas kernels: 5.7 us -> 5.08 us  [head(): pl.pallas_call(functools.partial(head_kernel, keep, share_rows), out_shap...]
where the time goes in v8:
time: 26.8 us; the launch traced here: 26.4 us
  blocking collectives  15.5 us (58%)
  Pallas kernels  8.93 us (33%)
  waiting for transfers between devices  1.67 us (6%)
  starting transfers between devices  0.3 us (1%)
    all_to_all x1, blocking collectives, per_device(): lax.all_to_all(send, 'energy', split_axis=1, concat_axis=0, axis_index_gr...  15.5 us
    pallas_call x1, Pallas kernels, head(): pl.pallas_call(functools.partial(head_kernel, keep, share_rows), out_shap...  5.08 us
    pallas_call x1, Pallas kernels, tail(): pl.pallas_call(functools.partial(tail_kernel, keep, share_rows, hop, last...  1.94 us
    pallas_call x1, Pallas kernels, lag_sums(): pl.pallas_call(functools.partial(lag_kernel, here), out_shape=jax.ShapeDt...  1.91 us
    ppermute x1, waiting for transfers between devices, per_device(): lax.ppermute(leaving, 'chain', [(i, (i + 1) % length) for i in range(leng...  1.67 us
  transfers between devices with their start and end apart: 1, of which 1 were waited for; matrix products, arithmetic and copies ran while one was open for 0% of the time, Pallas kernels for 0%

profile of v8, /device:TPU:1, one launch (start us, length us, event | category | flops | bytes accessed | tf_op | source)
XLA Modules:
  0.0 26.4 jit_solution(18433605708041379644)
XLA Ops:
  0.0 5.1 %head_cells.1 = (f32[1,2,2,256,128]{4,3,2,1,0:T(8,128)S(1)}, f32[1,16,32,128]{3,2,1,0:T(8,128)S(1)}, bf16[1,2,6,256,256]{4,3,2,1,0:T(8,128)(2,1)S(1)}, bf16[1,2,...) custom-call(f32[1,2,2,256,256]{4,3,2,1,0:T(8,128)} %g_hbm.1, f32[1,2,2,256,256]{4,3,2,1,0:T(8,128)} %s_hbm.1, ...), custom_call_target="tpu_custom_call" | custom-call | tf_op jit(solution)/shard_map/head_cells/pallas_call | solution.py:194
  5.1 0.3 %collective-permute-start = (f32[1,2,2,256,128]{4,3,2,1,0:T(8,128)S(1)}, f32[1,2,2,256,128]{4,3,2,1,0:T(8,128)S(1)}, u32[]{:S(2)}, u32[]{:S(2)}) collective-permute-start(f32[1,2,2,256,128]{4,3,2,1,0:T(8,128)S(1)} %get-tuple-element.10), channel_id=1, source_target_pairs={{0,16},{16,0},{1,17},{17,1},{2,18},{18,2},{3,19},{19,3},{4,20},{20... | collective-permute-start | bytes 1572872 | tf_op jit(solution)/shard_map/ppermute | solution.py:330
  5.4 1.7 %collective-permute-done.incoming_ref = f32[1,2,2,256,128]{4,3,2,1,0:T(8,128)S(1)} collective-permute-done((f32[1,2,2,256,128]{4,3,2,1,0:T(8,128)S(1)}, f32[1,2,2,256,128]{4,3,2,1,0:T(8,128)S(1)}, u32[]{:S(2)}, u32[]{:S(2)}) %collective-permute-start) | collective-permute-done | bytes 524320 | tf_op jit(solution)/shard_map/ppermute | solution.py:330
  7.1 1.9 %tail_cells.1 = f32[1,16,32,128]{3,2,1,0:T(8,128)S(1)} custom-call(f32[1,2,2,256,128]{4,3,2,1,0:T(8,128)S(1)} %collective-permute-done.incoming_ref, bf16[1,2,6,256,256]{4,3,2,1,0:T(8,128)(2,1)S(1)} %get-tuple-element.11.left_ref, bf16[1,2,6,256,256]{4,3,2,1,0:T(8,128)(2,1)S(1)} %get-tuple-element.12.right_ref, ...), custom_call_target="tpu_custom_call", output_to_operand_aliasing={{}: (5, {})} | custom-call | tf_op jit(solution)/shard_map/tail_cells/pallas_call | solution.py:253
  9.0 15.5 %all_to_all.4 = f32[1,16,32,128]{3,2,0,1:T(8,128)} all-to-all(f32[1,16,32,128]{3,2,0,1:T(8,128)S(1)} %bitcast.7), channel_id=1, replica_groups={{15,14,13,12,11,10,9,8,7,6,5,4,3,2,1,0},{31,30,29,28,27,26,25,24,23,22,..., dimensions={1} | all-to-all | bytes 524288 | tf_op jit(solution)/shard_map/all_to_all | solution.py:334
  24.5 1.9 %lag_sums.1 = f32[16,32,128]{2,1,0:T(8,128)} custom-call(f32[16,32,128]{2,1,0:T(8,128)} %bitcast.8), custom_call_target="tpu_custom_call" | custom-call | tf_op jit(solution)/shard_map/lag_sums/pallas_call | solution.py:305
Async XLA Ops:
  5.1 2.0 %collective-permute-start = (f32[1,2,2,256,128]{4,3,2,1,0:T(8,128)S(1)}, f32[1,2,2,256,128]{4,3,2,1,0:T(8,128)S(1)}, u32[]{:S(2)}, u32[]{:S(2)}) collective-permute-start(f32[1,2,2,256,128]{4,3,2,1,0:T(8,128)S(1)} %get-tuple-element.10), channel_id=1, source_target_pairs={{0,16},{16,0},{1,17},{17,1},{2,18},{18,2},{3,19},{19,3},{4,20},{20... | collective-permute-start | bytes 1572872 | tf_op jit(solution)/shard_map/ppermute | solution.py:330

commit v9 on v8

--- a/solution.py
+++ b/solution.py
@@ -76,7 +76,15 @@
     return jnp.concatenate(rows, axis=0)
 
 
+def sending_order(owners):
+    codes = [n ^ (n >> 1) for n in range(owners)]
+    if sorted(codes) != list(range(owners)):
+        codes = list(range(owners))
+    return [owners - 1 - code for code in codes]
+
+
 def pick_into(send_ref, e, cell, matrix_ref, kept_ref, keep, share_rows):
+    order = sending_order(send_ref.shape[1])
     nblk = matrix_ref.shape[-2] // BLOCK
     half = BLOCK // 2
     lane = lax.broadcasted_iota(jnp.int32, (half, LANES), 1)
@@ -96,7 +104,7 @@
             first = (cell * keep + k) * half
             for s in range(0, half, piece):
                 owner, inside = divmod(first + s, share_rows)
-                send_ref[e, send_ref.shape[1] - 1 - owner, pl.ds(part * share_rows + inside, piece), :] = flat[s:s + piece]
+                send_ref[e, order.index(owner), pl.ds(part * share_rows + inside, piece), :] = flat[s:s + piece]
 
 
 def head_kernel(keep, share_rows, g_hbm, s_hbm, b_hbm, pattern_hbm, kept_hbm, lead_hbm,
@@ -154,7 +162,8 @@
                 states[e] = product(parts(product(green_left, inner)), green_right)
                 out_ref = leaving_ref.at[e] if i == cells - 1 else state_ref.at[e, i]
                 put_state(out_ref, states[e])
-                pick_into(send_ref, e, i, out_ref, kept_ref, keep, share_rows)
+                if i < cells - 1:
+                    pick_into(send_ref, e, i, out_ref, kept_ref, keep, share_rows)
 
     @pl.when(position > 0)
     def _():
@@ -219,17 +228,25 @@
 
 def tail_kernel(keep, share_rows, hop, last, incoming_ref, left_ref, right_ref, fresh_ref, kept_hbm, *refs):
     if last:
-        (_, send_ref), refs = refs[:2], refs[2:]
+        (left_by, _, send_ref), refs = refs[:3], refs[3:]
         leaving_ref = None
     else:
-        (_, _, leaving_ref, send_ref), refs = refs[:4], refs[4:]
+        (left_by, _, leaving_ref, send_ref), refs = refs[:4], refs[4:]
     kept_ref, state_ref, sem = refs
     energies, cells, _, size, _ = fresh_ref.shape
-
-    @pl.when(lax.axis_index("chain") == hop + 1)
-    def _():
-        kept_copy = pltpu.make_async_copy(kept_hbm, kept_ref, sem)
-        kept_copy.start()
+    position = lax.axis_index("chain")
+    kept_copy = pltpu.make_async_copy(kept_hbm, kept_ref, sem)
+    kept_copy.start()
+
+    if hop == 0:
+        @pl.when(position == 0)
+        def _():
+            kept_copy.wait()
+            for e in range(energies):
+                pick_into(send_ref, e, cells - 1, left_by.at[e], kept_ref, keep, share_rows)
+
+    @pl.when(position == hop + 1)
+    def _():
         for e in range(energies):
             state = parts(get_state(incoming_ref.at[e]))
             halves = []
@@ -244,6 +261,14 @@
             if not last:
                 leaving_ref[e] = state_ref[e, cells - 1]
 
+    waited = position == hop + 1
+    if hop == 0:
+        waited = jnp.logical_or(waited, position == 0)
+
+    @pl.when(jnp.logical_not(waited))
+    def _():
+        kept_copy.wait()
+
 
 def tail(keep, share_rows, hop, last, incoming, left, right, fresh, kept_blocks, leaving, send):
     energies, cells = fresh.shape[:2]
@@ -253,9 +278,9 @@
     result = pl.pallas_call(
         functools.partial(tail_kernel, keep, share_rows, hop, last),
         out_shape=tuple(jax.ShapeDtypeStruct(value.shape, F32) for value in carried),
-        in_specs=[vmem] * 4 + [hbm] + [vmem] * len(carried),
+        in_specs=[vmem] * 4 + [hbm] + [vmem] * 2,
         out_specs=(vmem,) * len(carried),
-        input_output_aliases={5 + i: i for i in range(len(carried))},
+        input_output_aliases={6: 0} if last else {5: 0, 6: 1},
         scratch_shapes=[
             pltpu.SMEM(kept_blocks.shape, jnp.int32),
             pltpu.VMEM((energies, cells) + incoming.shape[1:], F32),
@@ -263,7 +288,7 @@
         ],
         compiler_params=pltpu.CompilerParams(vmem_limit_bytes=32 << 20),
         name="tail_cells",
-    )(incoming, left, right, fresh, in_hbm(kept_blocks), *carried)
+    )(incoming, left, right, fresh, in_hbm(kept_blocks), leaving, send)
     return (leaving, result[0]) if last else result
 
 
@@ -275,8 +300,10 @@
     groups = sems.shape[0]
     width = LAGS // groups
 
+    order = sending_order(energies // here)
+
     def at(e, first):
-        place = (energies // here - 1 - e // here) * here + e % here
+        place = order.index(e // here) * here + e % here
         return in_ref[place, first:first + step]
 
     copies = []
@@ -330,8 +357,8 @@
         incoming = lax.ppermute(leaving, "chain", [(i, (i + 1) % length) for i in range(length)])
         last = hop == length - 2
         leaving, send = tail(keep, share_rows, hop, last, incoming, left, right, fresh, kept_blocks, leaving, send)
-    backwards = [list(range(owners))[::-1]]
-    owned = lax.all_to_all(send, "energy", split_axis=1, concat_axis=0, axis_index_groups=backwards, tiled=True)
+    groups = [sending_order(owners)]
+    owned = lax.all_to_all(send, "energy", split_axis=1, concat_axis=0, axis_index_groups=groups, tiled=True)
     return lag_sums(retarded.shape[0], owned.reshape((-1,) + owned.shape[2:]))
 
 

time: 26.8 us -> 27 us (level)
  blocking collectives: 15.5 us -> 15.8 us
    all_to_all x1, blocking collectives: 15.5 us -> 15.8 us  [per_device(): lax.all_to_all(send, 'energy', split_axis=1, concat_axis=0, axis_index_gr...]
where the time goes in v9:
time: 27 us; the launch traced here: 26.7 us
  blocking collectives  15.8 us (59%)
  Pallas kernels  8.93 us (33%)
  waiting for transfers between devices  1.83 us (7%)
    all_to_all x1, blocking collectives, per_device(): lax.all_to_all(send, 'energy', split_axis=1, concat_axis=0, axis_index_gr...  15.8 us
    pallas_call x1, Pallas kernels, head(): pl.pallas_call(functools.partial(head_kernel, keep, share_rows), out_shap...  5.08 us
    pallas_call x1, Pallas kernels, tail(): pl.pallas_call(functools.partial(tail_kernel, keep, share_rows, hop, last...  1.94 us
    pallas_call x1, Pallas kernels, lag_sums(): pl.pallas_call(functools.partial(lag_kernel, here), out_shape=jax.ShapeDt...  1.91 us
    ppermute x1, waiting for transfers between devices, per_device(): lax.ppermute(leaving, 'chain', [(i, (i + 1) % length) for i in range(leng...  1.83 us
  transfers between devices with their start and end apart: 1, of which 1 were waited for; matrix products, arithmetic and copies ran while one was open for 0% of the time, Pallas kernels for 0%

profile of v9, /device:TPU:1, one launch (start us, length us, event | category | flops | bytes accessed | tf_op | source)
XLA Modules:
  0.0 26.7 jit_solution(2986998250603950400)
XLA Ops:
  0.0 5.1 %head_cells.1 = (f32[1,2,2,256,128]{4,3,2,1,0:T(8,128)S(1)}, f32[1,16,32,128]{3,2,1,0:T(8,128)S(1)}, bf16[1,2,6,256,256]{4,3,2,1,0:T(8,128)(2,1)S(1)}, bf16[1,2,...) custom-call(f32[1,2,2,256,256]{4,3,2,1,0:T(8,128)} %g_hbm.1, f32[1,2,2,256,256]{4,3,2,1,0:T(8,128)} %s_hbm.1, ...), custom_call_target="tpu_custom_call" | custom-call | tf_op jit(solution)/shard_map/head_cells/pallas_call | solution.py:203
  5.1 0.1 collective-permute-start
  5.2 1.8 %collective-permute-done.incoming_ref = f32[1,2,2,256,128]{4,3,2,1,0:T(8,128)S(1)} collective-permute-done((f32[1,2,2,256,128]{4,3,2,1,0:T(8,128)S(1)}, f32[1,2,2,256,128]{4,3,2,1,0:T(8,128)S(1)}, u32[]{:S(2)}, u32[]{:S(2)}) %collective-permute-start) | collective-permute-done | bytes 524320 | tf_op jit(solution)/shard_map/ppermute | solution.py:357
  7.1 1.9 %tail_cells.1 = f32[1,16,32,128]{3,2,1,0:T(8,128)S(1)} custom-call(f32[1,2,2,256,128]{4,3,2,1,0:T(8,128)S(1)} %collective-permute-done.incoming_ref, bf16[1,2,6,256,256]{4,3,2,1,0:T(8,128)(2,1)S(1)} %get-tuple-element.11.left_ref, bf16[1,2,6,256,256]{4,3,2,1,0:T(8,128)(2,1)S(1)} %get-tuple-element.12.right_ref, ...), custom_call_target="tpu_custom_call", output_to_operand_aliasing={{}: (6, {})} | custom-call | tf_op jit(solution)/shard_map/tail_cells/pallas_call | solution.py:278
  9.0 15.8 %all_to_all.4 = f32[1,16,32,128]{3,2,0,1:T(8,128)} all-to-all(f32[1,16,32,128]{3,2,0,1:T(8,128)S(1)} %bitcast.7), channel_id=1, replica_groups={{15,14,12,13,9,8,10,11,3,2,0,1,5,4,6,7},{31,30,28,29,25,24,26,27,19,18,..., dimensions={1} | all-to-all | bytes 524288 | tf_op jit(solution)/shard_map/all_to_all | solution.py:361
  24.8 1.9 %lag_sums.1 = f32[16,32,128]{2,1,0:T(8,128)} custom-call(f32[16,32,128]{2,1,0:T(8,128)} %bitcast.8), custom_call_target="tpu_custom_call" | custom-call | tf_op jit(solution)/shard_map/lag_sums/pallas_call | solution.py:332
Async XLA Ops:
  5.1 2.0 %collective-permute-start = (f32[1,2,2,256,128]{4,3,2,1,0:T(8,128)S(1)}, f32[1,2,2,256,128]{4,3,2,1,0:T(8,128)S(1)}, u32[]{:S(2)}, u32[]{:S(2)}) collective-permute-start(f32[1,2,2,256,128]{4,3,2,1,0:T(8,128)S(1)} %get-tuple-element.10.refs_0_), channel_id=1, source_target_pairs={{0,16},{16,0},{1,17},{17,1},{2,18},{18,2},{3,19},{19,3},{4,20},{20... | collective-permute-start | bytes 1572872 | tf_op jit(solution)/shard_map/ppermute | solution.py:357

commit v10 on v8

--- a/solution.py
+++ b/solution.py
@@ -117,14 +117,29 @@
     pattern_copy.start()
     kept_copy.start()
 
+    later = [copy for i in range(1, cells) for copy in (b_copies[i], g_copies[i], s_copies[i])]
+
     @pl.when(position == 0)
     def _():
         lead_copy.start()
-
-    for i in range(cells):
-        b_copies[i].start()
-        g_copies[i].start()
-        s_copies[i].start()
+        b_copies[0].start()
+        lead_copy.wait()
+        b_copies[0].wait()
+        g_copies[0].start()
+        s_copies[0].start()
+        for copy in later:
+            copy.start()
+
+    @pl.when(position > 0)
+    def _():
+        g_copies[0].start()
+        b_copies[0].start()
+        s_copies[0].start()
+        g_copies[0].wait()
+        b_copies[0].wait()
+        for copy in later:
+            copy.start()
+
     pattern_copy.wait()
     kept_copy.wait()
 
@@ -137,10 +152,10 @@
 
     @pl.when(position == 0)
     def _():
-        lead_copy.wait()
         states = [(lead_ref[e, 0], lead_ref[e, 1]) for e in range(energies)]
         for i in range(cells):
-            b_copies[i].wait()
+            if i > 0:
+                b_copies[i].wait()
             bridge = bridge_of(i)
             bridge_left, bridge_right = parts(bridge), parts(adjoint(bridge))
             for e in range(energies):
@@ -160,8 +175,9 @@
     def _():
         states, joined = [None] * energies, [None] * energies
         for i in range(cells):
-            b_copies[i].wait()
-            g_copies[i].wait()
+            if i > 0:
+                b_copies[i].wait()
+                g_copies[i].wait()
             s_copies[i].wait()
             bridge = bridge_of(i)
             for e in range(energies):

time: 26.8 us -> 27.1 us (1.011)
  starting transfers between devices: 0.3 us -> 0.58 us
    ppermute x1, starting transfers between devices: 0.3 us -> 0.58 us  [per_device(): lax.ppermute(leaving, 'chain', [(i, (i + 1) % length) for i in range(leng...]
where the time goes in v10:
time: 27.1 us; the launch traced here: 26.7 us
  blocking collectives  15.6 us (58%)
  Pallas kernels  8.92 us (33%)
  waiting for transfers between devices  1.54 us (6%)
  starting transfers between devices  0.58 us (2%)
    all_to_all x1, blocking collectives, per_device(): lax.all_to_all(send, 'energy', split_axis=1, concat_axis=0, axis_index_gr...  15.6 us
    pallas_call x1, Pallas kernels, head(): pl.pallas_call(functools.partial(head_kernel, keep, share_rows), out_shap...  5.08 us
    pallas_call x1, Pallas kernels, tail(): pl.pallas_call(functools.partial(tail_kernel, keep, share_rows, hop, last...  1.94 us
    pallas_call x1, Pallas kernels, lag_sums(): pl.pallas_call(functools.partial(lag_kernel, here), out_shape=jax.ShapeDt...  1.91 us
    ppermute x1, waiting for transfers between devices, per_device(): lax.ppermute(leaving, 'chain', [(i, (i + 1) % length) for i in range(leng...  1.54 us
    ppermute x1, starting transfers between devices, per_device(): lax.ppermute(leaving, 'chain', [(i, (i + 1) % length) for i in range(leng...  0.58 us
  transfers between devices with their start and end apart: 1, of which 1 were waited for; matrix products, arithmetic and copies ran while one was open for 0% of the time, Pallas kernels for 0%

profile of v10, /device:TPU:1, one launch (start us, length us, event | category | flops | bytes accessed | tf_op | source)
XLA Modules:
  0.0 26.7 jit_solution(8971190280645422350)
XLA Ops:
  0.0 5.1 %head_cells.1 = (f32[1,2,2,256,128]{4,3,2,1,0:T(8,128)S(1)}, f32[1,16,32,128]{3,2,1,0:T(8,128)S(1)}, bf16[1,2,6,256,256]{4,3,2,1,0:T(8,128)(2,1)S(1)}, bf16[1,2,...) custom-call(f32[1,2,2,256,256]{4,3,2,1,0:T(8,128)} %g_hbm.1, f32[1,2,2,256,256]{4,3,2,1,0:T(8,128)} %s_hbm.1, ...), custom_call_target="tpu_custom_call" | custom-call | tf_op jit(solution)/shard_map/head_cells/pallas_call | solution.py:210
  5.1 0.6 %collective-permute-start = (f32[1,2,2,256,128]{4,3,2,1,0:T(8,128)S(1)}, f32[1,2,2,256,128]{4,3,2,1,0:T(8,128)S(1)}, u32[]{:S(2)}, u32[]{:S(2)}) collective-permute-start(f32[1,2,2,256,128]{4,3,2,1,0:T(8,128)S(1)} %get-tuple-element.10), channel_id=1, source_target_pairs={{0,16},{16,0},{1,17},{17,1},{2,18},{18,2},{3,19},{19,3},{4,20},{20... | collective-permute-start | bytes 1572872 | tf_op jit(solution)/shard_map/ppermute | solution.py:346
  5.7 1.5 %collective-permute-done.incoming_ref = f32[1,2,2,256,128]{4,3,2,1,0:T(8,128)S(1)} collective-permute-done((f32[1,2,2,256,128]{4,3,2,1,0:T(8,128)S(1)}, f32[1,2,2,256,128]{4,3,2,1,0:T(8,128)S(1)}, u32[]{:S(2)}, u32[]{:S(2)}) %collective-permute-start) | collective-permute-done | bytes 524320 | tf_op jit(solution)/shard_map/ppermute | solution.py:346
  7.2 1.9 %tail_cells.1 = f32[1,16,32,128]{3,2,1,0:T(8,128)S(1)} custom-call(f32[1,2,2,256,128]{4,3,2,1,0:T(8,128)S(1)} %collective-permute-done.incoming_ref, bf16[1,2,6,256,256]{4,3,2,1,0:T(8,128)(2,1)S(1)} %get-tuple-element.11.left_ref, bf16[1,2,6,256,256]{4,3,2,1,0:T(8,128)(2,1)S(1)} %get-tuple-element.12.right_ref, ...), custom_call_target="tpu_custom_call", output_to_operand_aliasing={{}: (5, {})} | custom-call | tf_op jit(solution)/shard_map/tail_cells/pallas_call | solution.py:269
  9.2 15.6 %all_to_all.4 = f32[1,16,32,128]{3,2,0,1:T(8,128)} all-to-all(f32[1,16,32,128]{3,2,0,1:T(8,128)S(1)} %bitcast.7), channel_id=1, replica_groups={{15,14,13,12,11,10,9,8,7,6,5,4,3,2,1,0},{31,30,29,28,27,26,25,24,23,22,..., dimensions={1} | all-to-all | bytes 524288 | tf_op jit(solution)/shard_map/all_to_all | solution.py:350
  24.8 1.9 %lag_sums.1 = f32[16,32,128]{2,1,0:T(8,128)} custom-call(f32[16,32,128]{2,1,0:T(8,128)} %bitcast.8), custom_call_target="tpu_custom_call" | custom-call | tf_op jit(solution)/shard_map/lag_sums/pallas_call | solution.py:321
Async XLA Ops:
  5.1 2.1 %collective-permute-start = (f32[1,2,2,256,128]{4,3,2,1,0:T(8,128)S(1)}, f32[1,2,2,256,128]{4,3,2,1,0:T(8,128)S(1)}, u32[]{:S(2)}, u32[]{:S(2)}) collective-permute-start(f32[1,2,2,256,128]{4,3,2,1,0:T(8,128)S(1)} %get-tuple-element.10), channel_id=1, source_target_pairs={{0,16},{16,0},{1,17},{17,1},{2,18},{18,2},{3,19},{19,3},{4,20},{20... | collective-permute-start | bytes 1572872 | tf_op jit(solution)/shard_map/ppermute | solution.py:346

commit v11 on v8

--- a/solution.py
+++ b/solution.py
@@ -99,23 +99,25 @@
                 send_ref[e, send_ref.shape[1] - 1 - owner, pl.ds(part * share_rows + inside, piece), :] = flat[s:s + piece]
 
 
-def head_kernel(keep, share_rows, g_hbm, s_hbm, b_hbm, pattern_hbm, kept_hbm, lead_hbm,
-                leaving_ref, send_ref, left_ref, right_ref, fresh_ref,
-                pattern_ref, kept_ref, g_ref, s_ref, b_ref, lead_ref, state_ref, sems):
-    energies, cells, _, size, _ = g_ref.shape
+def head_kernel(g_hbm, s_hbm, b_hbm, pattern_hbm, lead_hbm,
+                inner_ref, fresh_ref, factor_ref, green_ref, bridge_ref,
+                pattern_ref, g_ref, s_ref, b_ref, lead_ref, sems):
+    energies, cells, _, size, _ = s_ref.shape
     position = lax.axis_index("chain")
+    final = cells - 1
 
     def fetch(slot, source, target):
         return pltpu.make_async_copy(source, target, sems.at[slot])
 
+    def g_place(i):
+        return green_ref if i == final else g_ref.at[:, i]
+
     lead_copy = fetch(0, lead_hbm, lead_ref)
     b_copies = [fetch(1 + i, b_hbm.at[i], b_ref.at[i]) for i in range(cells)]
-    g_copies = [fetch(1 + cells + i, g_hbm.at[:, i], g_ref.at[:, i]) for i in range(cells)]
+    g_copies = [fetch(1 + cells + i, g_hbm.at[:, i], g_place(i)) for i in range(cells)]
     s_copies = [fetch(1 + 2 * cells + i, s_hbm.at[:, i], s_ref.at[:, i]) for i in range(cells)]
     pattern_copy = fetch(1 + 3 * cells, pattern_hbm, pattern_ref)
-    kept_copy = fetch(2 + 3 * cells, kept_hbm, kept_ref)
     pattern_copy.start()
-    kept_copy.start()
 
     @pl.when(position == 0)
     def _():
@@ -126,14 +128,15 @@
         g_copies[i].start()
         s_copies[i].start()
     pattern_copy.wait()
-    kept_copy.wait()
 
     def bridge_of(i):
         mask = block_mask(pattern_ref, i, size)
         return b_ref[i, 0] * mask, b_ref[i, 1] * mask
 
-    def matrix(ref, e, i):
-        return ref[e, i, 0], ref[e, i, 1]
+    def green_of(e, i):
+        if i == final:
+            return green_ref[e, 0], green_ref[e, 1]
+        return g_ref[e, i, 0], g_ref[e, i, 1]
 
     @pl.when(position == 0)
     def _():
@@ -148,73 +151,147 @@
                 if e == 0:
                     g_copies[i].wait()
                     s_copies[i].wait()
-                green = matrix(g_ref, e, i)
-                green_left, green_right = parts(green), parts(adjoint(green))
-                inner = parts(plus(matrix(s_ref, e, i), entered))
-                states[e] = product(parts(product(green_left, inner)), green_right)
-                out_ref = leaving_ref.at[e] if i == cells - 1 else state_ref.at[e, i]
-                put_state(out_ref, states[e])
-                pick_into(send_ref, e, i, out_ref, kept_ref, keep, share_rows)
+                inner = plus((s_ref[e, i, 0], s_ref[e, i, 1]), entered)
+                if i == final:
+                    put_state(inner_ref.at[e], inner)
+                else:
+                    green = green_of(e, i)
+                    states[e] = product(parts(product(parts(green), parts(inner))), parts(adjoint(green)))
+                    put_state(fresh_ref.at[e, i], states[e])
 
     @pl.when(position > 0)
     def _():
-        states, joined = [None] * energies, [None] * energies
+        states = [None] * energies
         for i in range(cells):
             b_copies[i].wait()
             g_copies[i].wait()
             s_copies[i].wait()
             bridge = bridge_of(i)
+            if i == final:
+                bridge_ref[0], bridge_ref[1] = bridge
             for e in range(energies):
-                green = matrix(g_ref, e, i)
+                green = green_of(e, i)
                 green_left, green_right = parts(green), parts(adjoint(green))
-                inner = matrix(s_ref, e, i)
-                if i == 0:
-                    joined[e] = product(green_left, parts(bridge))
-                else:
-                    bridge_left, bridge_right = parts(bridge), parts(adjoint(bridge))
-                    half = parts(product(bridge_left, parts(states[e])))
-                    across = parts(product(bridge_left, parts(joined[e])))
-                    inner = plus(inner, product(half, bridge_right))
-                    joined[e] = product(green_left, across)
+                inner = s_ref[e, i, 0], s_ref[e, i, 1]
+                if i < final:
+                    put_parts(factor_ref.at[e, i], parts(product(green_left, parts(bridge))))
+                if i > 0:
+                    half = parts(product(parts(bridge), parts(states[e])))
+                    inner = plus(inner, product(half, parts(adjoint(bridge))))
                 states[e] = product(parts(product(green_left, parts(inner))), green_right)
-                put_parts(left_ref.at[e, i], parts(joined[e]))
-                put_parts(right_ref.at[e, i], parts(adjoint(joined[e])))
-                fresh_ref[e, i, 0], fresh_ref[e, i, 1] = states[e]
+                put_state(fresh_ref.at[e, i], states[e])
 
 
 def in_hbm(value):
     return pltpu.with_memory_space_constraint(value, pltpu.HBM)
 
 
-def head(keep, share_rows, owners, retarded, lesser_sigma, coupling, pattern, kept_blocks, lead):
+def head(retarded, lesser_sigma, coupling, pattern, lead):
     energies, cells, _, size, _ = retarded.shape
     hbm = pl.BlockSpec(memory_space=pltpu.HBM)
     vmem = pl.BlockSpec(memory_space=pltpu.VMEM)
     state_shape = (2, size // LANES, size, LANES)
+    others = max(cells - 1, 1)
     return pl.pallas_call(
-        functools.partial(head_kernel, keep, share_rows),
+        head_kernel,
         out_shape=(
             jax.ShapeDtypeStruct((energies,) + state_shape, F32),
+            jax.ShapeDtypeStruct((energies, cells) + state_shape, F32),
+            jax.ShapeDtypeStruct((energies, others, 6, size, size), BF16),
+            jax.ShapeDtypeStruct((energies, 2, size, size), F32),
+            jax.ShapeDtypeStruct((2, size, size), F32),
+        ),
+        in_specs=[hbm] * 5,
+        out_specs=(vmem,) * 5,
+        scratch_shapes=[
+            pltpu.SMEM(pattern.shape, jnp.int32),
+            pltpu.VMEM((energies, others, 2, size, size), F32),
+            pltpu.VMEM(lesser_sigma.shape, F32),
+            pltpu.VMEM(coupling.shape, F32),
+            pltpu.VMEM(lead.shape, F32),
+            pltpu.SemaphoreType.DMA((2 + 3 * cells,)),
+        ],
+        compiler_params=pltpu.CompilerParams(vmem_limit_bytes=32 << 20),
+        name="head_cells",
+    )(*(in_hbm(x) for x in (retarded, lesser_sigma, coupling, pattern, lead)))
+
+
+def middle_kernel(keep, share_rows, before_ref, inner_ref, fresh_ref, factor_ref, green_ref, bridge_ref, kept_hbm,
+                  send_ref, left_ref, right_ref, kept_ref, state_ref, sem):
+    energies, cells = fresh_ref.shape[:2]
+    final = cells - 1
+    position = lax.axis_index("chain")
+    kept_copy = pltpu.make_async_copy(kept_hbm, kept_ref, sem)
+    kept_copy.start()
+
+    @pl.when(position == 0)
+    def _():
+        for e in range(energies):
+            green = green_ref[e, 0], green_ref[e, 1]
+            inner = parts(get_state(inner_ref.at[e]))
+            put_state(state_ref.at[e], product(parts(product(parts(green), inner)), parts(adjoint(green))))
+            if e == 0:
+                kept_copy.wait()
+            for i in range(cells):
+                matrix_ref = state_ref.at[e] if i == final else fresh_ref.at[e, i]
+                pick_into(send_ref, e, i, matrix_ref, kept_ref, keep, share_rows)
+
+    def chain_of_factors(with_before):
+        for e in range(energies):
+            last_factor = product(parts((green_ref[e, 0], green_ref[e, 1])), parts((bridge_ref[0], bridge_ref[1])))
+            joined = None
+            if with_before:
+                joined = before_ref[e, final, 0], before_ref[e, final, 1]
+            for i in range(cells):
+                if joined is not None:
+                    factor = parts(last_factor) if i == final else get_parts(factor_ref.at[e, i])
+                    joined = product(factor, parts(joined))
+                    put_parts(left_ref.at[e, i], parts(joined))
+                    put_parts(right_ref.at[e, i], parts(adjoint(joined)))
+                    continue
+                if i == final:
+                    joined = last_factor
+                else:
+                    whole = get_parts(factor_ref.at[e, i])
+                    joined = tuple(whole[n].astype(F32) + whole[n + 1].astype(F32) for n in (0, 2))
+                put_parts(left_ref.at[e, i], parts(joined))
+                put_parts(right_ref.at[e, i], parts(adjoint(joined)))
+
+    @pl.when(position == 1)
+    def _():
+        chain_of_factors(True)
+        kept_copy.wait()
+
+    if lax.axis_size("chain") > 2:
+        @pl.when(position > 1)
+        def _():
+            chain_of_factors(False)
+            kept_copy.wait()
+
+
+def middle(keep, share_rows, owners, before, inner, fresh, factor, green, bridge, kept_blocks):
+    energies, cells = fresh.shape[:2]
+    size = bridge.shape[-1]
+    hbm = pl.BlockSpec(memory_space=pltpu.HBM)
+    vmem = pl.BlockSpec(memory_space=pltpu.VMEM)
+    return pl.pallas_call(
+        functools.partial(middle_kernel, keep, share_rows),
+        out_shape=(
             jax.ShapeDtypeStruct((energies, owners, 2 * share_rows, LANES), F32),
             jax.ShapeDtypeStruct((energies, cells, 6, size, size), BF16),
             jax.ShapeDtypeStruct((energies, cells, 6, size, size), BF16),
-            jax.ShapeDtypeStruct((energies, cells, 2, size, size), F32),
         ),
-        in_specs=[hbm] * 6,
-        out_specs=(vmem,) * 5,
+        in_specs=[vmem] * 6 + [hbm],
+        out_specs=(vmem,) * 3,
         scratch_shapes=[
-            pltpu.SMEM(pattern.shape, jnp.int32),
             pltpu.SMEM(kept_blocks.shape, jnp.int32),
-            pltpu.VMEM(retarded.shape, F32),
-            pltpu.VMEM(lesser_sigma.shape, F32),
-            pltpu.VMEM(coupling.shape, F32),
-            pltpu.VMEM(lead.shape, F32),
-            pltpu.VMEM((energies, cells) + state_shape, F32),
-            pltpu.SemaphoreType.DMA((3 + 3 * cells,)),
+            pltpu.VMEM(inner.shape, F32),
+            pltpu.SemaphoreType.DMA,
         ],
         compiler_params=pltpu.CompilerParams(vmem_limit_bytes=32 << 20),
-        name="head_cells",
-    )(*(in_hbm(x) for x in (retarded, lesser_sigma, coupling, pattern, kept_blocks, lead)))
+        cost_estimate=pl.CostEstimate(flops=12 * 2 * size**3, bytes_accessed=4 * size * size, transcendentals=0),
+        name="middle_cells",
+    )(before, inner, fresh, factor, green, bridge, in_hbm(kept_blocks))
 
 
 def tail_kernel(keep, share_rows, hop, last, incoming_ref, left_ref, right_ref, fresh_ref, kept_hbm, *refs):
@@ -224,7 +301,7 @@
     else:
         (_, _, leaving_ref, send_ref), refs = refs[:4], refs[4:]
     kept_ref, state_ref, sem = refs
-    energies, cells, _, size, _ = fresh_ref.shape
+    energies, cells = fresh_ref.shape[:2]
 
     @pl.when(lax.axis_index("chain") == hop + 1)
     def _():
@@ -237,7 +314,7 @@
                 halves.append(parts(product(get_parts(left_ref.at[e, i]), state)))
             for i in range(cells):
                 grown = product(halves[i], get_parts(right_ref.at[e, i]))
-                put_state(state_ref.at[e, i], plus((fresh_ref[e, i, 0], fresh_ref[e, i, 1]), grown))
+                put_state(state_ref.at[e, i], plus(get_state(fresh_ref.at[e, i]), grown))
                 if i == 0 and e == 0:
                     kept_copy.wait()
                 pick_into(send_ref, e, i, state_ref.at[e, i], kept_ref, keep, share_rows)
@@ -323,11 +400,14 @@
     owners = lax.axis_size("energy")
     length = lax.axis_size("chain")
     share_rows = cells * keep * BLOCK * BLOCK // (owners * LANES)
-    leaving, send, left, right, fresh = head(
-        keep, share_rows, owners, retarded, lesser_sigma, coupling, coupling_pattern, kept_blocks, lead_lesser
-    )
+    ring = [(i, (i + 1) % length) for i in range(length)]
+    before = lax.ppermute(retarded, "chain", ring)
+    leaving, fresh, factor, green, bridge = head(retarded, lesser_sigma, coupling, coupling_pattern, lead_lesser)
+    incoming = lax.ppermute(leaving, "chain", ring)
+    send, left, right = middle(keep, share_rows, owners, before, leaving, fresh, factor, green, bridge, kept_blocks)
     for hop in range(length - 1):
-        incoming = lax.ppermute(leaving, "chain", [(i, (i + 1) % length) for i in range(length)])
+        if hop > 0:
+            incoming = lax.ppermute(leaving, "chain", ring)
         last = hop == length - 2
         leaving, send = tail(keep, share_rows, hop, last, incoming, left, right, fresh, kept_blocks, leaving, send)
     backwards = [list(range(owners))[::-1]]

time: 26.8 us -> 26 us (0.970)
  waiting for transfers between devices: 1.67 us -> 0.32 us
  Pallas kernels: 8.93 us -> 9.73 us
    ppermute x1 -> x2, waiting for transfers between devices: 1.67 us -> 0.32 us  [the longest x1 0.32 us: per_device(): incoming = lax.ppermute(leaving, 'chain', ring)]
    pallas_call x1 -> x2, Pallas kernels: 5.08 us -> 5.88 us  [the longest x1 4.39 us: head(): pl.pallas_call(head_kernel, out_shape=(jax.ShapeDtypeStruct((energies,) +...]
  transfers between devices with their start and end apart: 1 -> 2, of which waited for: 1 -> 1; matrix products, arithmetic and copies ran while one was open for 0% -> 0% of each run, Pallas kernels for 0% -> 23%
where the time goes in v11:
time: 26 us; the launch traced here: 25.6 us
  blocking collectives  15.4 us (59%)
  Pallas kernels  9.73 us (37%)
  waiting for transfers between devices  0.32 us (1%)
    all_to_all x1, blocking collectives, per_device(): lax.all_to_all(send, 'energy', split_axis=1, concat_axis=0, axis_index_gr...  15.4 us
    pallas_call x1, Pallas kernels, head(): pl.pallas_call(head_kernel, out_shape=(jax.ShapeDtypeStruct((energies,) +...  4.39 us
    pallas_call x1, Pallas kernels, tail(): pl.pallas_call(functools.partial(tail_kernel, keep, share_rows, hop, last...  1.94 us
    pallas_call x1, Pallas kernels, lag_sums(): pl.pallas_call(functools.partial(lag_kernel, here), out_shape=jax.ShapeDt...  1.91 us
    pallas_call x1, Pallas kernels, middle(): pl.pallas_call(functools.partial(middle_kernel, keep, share_rows), out_sh...  1.49 us
  transfers between devices with their start and end apart: 2, of which 1 were waited for; matrix products, arithmetic and copies ran while one was open for 0% of the time, Pallas kernels for 23%

profile of v11, /device:TPU:1, one launch (start us, length us, event | category | flops | bytes accessed | tf_op | source)
XLA Modules:
  0.0 25.6 jit_solution(16667144243467488888)
XLA Ops:
  0.0 0.1 collective-permute-start.1
  0.1 4.4 %head_cells.1 = (f32[1,2,2,256,128]{4,3,2,1,0:T(8,128)S(1)}, f32[1,2,2,2,256,128]{5,4,3,2,1,0:T(8,128)S(1)}, bf16[1,1,6,256,256]{4,3,2,1,0:T(8,128)(2,1)S(1)}, f...) custom-call(f32[1,2,2,256,256]{4,3,2,1,0:T(8,128)} %g_hbm.1, f32[1,2,2,256,256]{4,3,2,1,0:T(8,128)} %s_hbm.1, ...), custom_call_target="tpu_custom_call" | custom-call | tf_op jit(solution)/shard_map/head_cells/pallas_call | solution.py:195
  4.5 0.1 collective-permute-start
  4.6 0.0 collective-permute-done.1.before_ref
  4.6 1.5 %middle_cells.1 = (f32[1,16,32,128]{3,2,1,0:T(8,128)S(1)}, bf16[1,2,6,256,256]{4,3,2,1,0:T(8,128)(2,1)S(1)}, bf16[1,2,6,256,256]{4,3,2,1,0:T(8,128)(2,1)S(1)}) custom-call(f32[1,2,2,256,256]{4,3,2,1,0:T(8,128)S(1)} %collective-permute-done.1.before_ref, f32[1,2,2,256,128]{4,3,2,1,0:T(8,128)S(1)} %get-tuple-element.13.inner_ref, ...), custom_call_target="tpu_custom_call" | custom-call | flops 402653184 | bytes 262144 | tf_op jit(solution)/shard_map/middle_cells/pallas_call | solution.py:277
  6.1 0.3 %collective-permute-done.incoming_ref = f32[1,2,2,256,128]{4,3,2,1,0:T(8,128)S(1)} collective-permute-done((f32[1,2,2,256,128]{4,3,2,1,0:T(8,128)S(1)}, f32[1,2,2,256,128]{4,3,2,1,0:T(8,128)S(1)}, u32[]{:S(2)}, u32[]{:S(2)}) %collective-permute-start) | collective-permute-done | bytes 524320 | tf_op jit(solution)/shard_map/ppermute | solution.py:406
  6.4 1.9 %tail_cells.1 = f32[1,16,32,128]{3,2,1,0:T(8,128)S(1)} custom-call(f32[1,2,2,256,128]{4,3,2,1,0:T(8,128)S(1)} %collective-permute-done.incoming_ref, bf16[1,2,6,256,256]{4,3,2,1,0:T(8,128)(2,1)S(1)} %get-tuple-element.18.left_ref, bf16[1,2,6,256,256]{4,3,2,1,0:T(8,128)(2,1)S(1)} %get-tuple-element.19.right_ref, ...), custom_call_target="tpu_custom_call", output_to_operand_aliasing={{}: (5, {})} | custom-call | tf_op jit(solution)/shard_map/tail_cells/pallas_call | solution.py:330
  8.4 15.4 %all_to_all.4 = f32[1,16,32,128]{3,2,0,1:T(8,128)} all-to-all(f32[1,16,32,128]{3,2,0,1:T(8,128)S(1)} %bitcast.7), channel_id=1, replica_groups={{15,14,13,12,11,10,9,8,7,6,5,4,3,2,1,0},{31,30,29,28,27,26,25,24,23,22,..., dimensions={1} | all-to-all | bytes 524288 | tf_op jit(solution)/shard_map/all_to_all | solution.py:414
  23.7 1.9 %lag_sums.1 = f32[16,32,128]{2,1,0:T(8,128)} custom-call(f32[16,32,128]{2,1,0:T(8,128)} %bitcast.8), custom_call_target="tpu_custom_call" | custom-call | tf_op jit(solution)/shard_map/lag_sums/pallas_call | solution.py:382
Async XLA Ops:
  0.0 4.6 %collective-permute-start.1 = (f32[1,2,2,256,256]{4,3,2,1,0:T(8,128)}, f32[1,2,2,256,256]{4,3,2,1,0:T(8,128)S(1)}, u32[]{:S(2)}, u32[]{:S(2)}) collective-permute-start(f32[1,2,2,256,256]{4,3,2,1,0:T(8,128)} %g_hbm.1), channel_id=1, source_target_pairs={{0,16},{16,0},{1,17},{17,1},{2,18},{18,2},{3,19},{19,3},{4,20},{20... | collective-permute-start | bytes 3145736 | tf_op jit(solution)/shard_map/ppermute | solution.py:404
  4.5 2.0 %collective-permute-start = (f32[1,2,2,256,128]{4,3,2,1,0:T(8,128)S(1)}, f32[1,2,2,256,128]{4,3,2,1,0:T(8,128)S(1)}, u32[]{:S(2)}, u32[]{:S(2)}) collective-permute-start(f32[1,2,2,256,128]{4,3,2,1,0:T(8,128)S(1)} %get-tuple-element.13.inner_ref), channel_id=1, source_target_pairs={{0,16},{16,0},{1,17},{17,1},{2,18},{18,2},{3,19},{19,3},{4,20},{20... | collective-permute-start | bytes 1572872 | tf_op jit(solution)/shard_map/ppermute | solution.py:406

commit v12 on v11

--- a/solution.py
+++ b/solution.py
@@ -76,27 +76,44 @@
     return jnp.concatenate(rows, axis=0)
 
 
+def with_next_row(value):
+    return pltpu.roll(value, value.shape[0] - 1, 0)
+
+
+def with_row_before(value):
+    return pltpu.roll(value, 1, 0)
+
+
+def on_even_rows(shape):
+    return lax.broadcasted_iota(jnp.int32, shape, 0) % 2 == 0
+
+
 def pick_into(send_ref, e, cell, matrix_ref, kept_ref, keep, share_rows):
     nblk = matrix_ref.shape[-2] // BLOCK
+    owners = send_ref.shape[1]
     half = BLOCK // 2
-    lane = lax.broadcasted_iota(jnp.int32, (half, LANES), 1)
+    shape = (BLOCK, LANES)
+    even_row = on_even_rows(shape)
+    left_lane = lax.broadcasted_iota(jnp.int32, shape, 1) < BLOCK
     piece = min(half, share_rows)
     for k in range(keep):
         number = kept_ref[k]
-        top = (number // nblk) * BLOCK
+        top = pl.multiple_of((number // nblk) * BLOCK, BLOCK)
         across = (number % nblk) * BLOCK
         window = across // LANES
-        in_upper = jnp.full((half, LANES), across % LANES, jnp.int32) > 0
-        for part in range(2):
-            even = matrix_ref[part, window, pl.ds(top, half, 2), :]
-            odd = matrix_ref[part, window, pl.ds(top + 1, half, 2), :]
-            left = jnp.where(in_upper, pltpu.roll(even, BLOCK, 1), even)
-            right = jnp.where(in_upper, odd, pltpu.roll(odd, BLOCK, 1))
-            flat = jnp.where(lane < BLOCK, left, right)
-            first = (cell * keep + k) * half
-            for s in range(0, half, piece):
-                owner, inside = divmod(first + s, share_rows)
-                send_ref[e, send_ref.shape[1] - 1 - owner, pl.ds(part * share_rows + inside, piece), :] = flat[s:s + piece]
+        in_upper = jnp.full(shape, across % LANES, jnp.int32) > 0
+        re = matrix_ref[0, window, pl.ds(top, BLOCK), :]
+        im = matrix_ref[1, window, pl.ds(top, BLOCK), :]
+        first = jnp.where(even_row, re, with_row_before(im))
+        second = jnp.where(even_row, with_next_row(re), im)
+        moved = pltpu.roll(jnp.where(in_upper, first, second), BLOCK, 1)
+        left = jnp.where(in_upper, moved, first)
+        right = jnp.where(in_upper, second, moved)
+        flat = jnp.where(left_lane, left, right)
+        begin = (cell * keep + k) * half
+        for s in range(0, half, piece):
+            owner, inside = divmod(begin + s, share_rows)
+            send_ref[e, owners - 1 - owner, pl.ds(2 * inside, 2 * piece), :] = flat[2 * s:2 * (s + piece)]
 
 
 def head_kernel(g_hbm, s_hbm, b_hbm, pattern_hbm, lead_hbm,
@@ -344,31 +361,42 @@
     return (leaving, result[0]) if last else result
 
 
-def lag_kernel(here, in_ref, out_hbm, out_ref, sems):
+def lag_kernel(here, in_ref, out_hbm, swapped_ref, out_ref, sems):
     energies, double_rows, _ = in_ref.shape
-    rows = double_rows // 2
-    step = min(8, rows)
+    step = min(8, double_rows)
+    blocks = range(0, double_rows, step)
     scale = 1.0 / energies
     groups = sems.shape[0]
     width = LAGS // groups
-
-    def at(e, first):
-        place = (energies // here - 1 - e // here) * here + e % here
-        return in_ref[place, first:first + step]
+    even_row = on_even_rows((double_rows, LANES))
+    even_in_step = on_even_rows((step, LANES))
+    for e in range(energies):
+        value = in_ref[e]
+        swapped_ref[e] = jnp.where(even_row, with_next_row(value), with_row_before(value))
+
+    def place(e):
+        return (energies // here - 1 - e // here) * here + e % here
 
     copies = []
     for group in range(groups):
-        for lag in range(group * width, (group + 1) * width):
-            for first in range(0, rows, step):
-                real_sum = jnp.zeros((step, LANES), F32)
-                imag_sum = jnp.zeros((step, LANES), F32)
-                for e in range(energies - lag):
-                    late_re, late_im = at(e + lag, first), at(e + lag, rows + first)
-                    early_re, early_im = at(e, first), at(e, rows + first)
-                    real_sum += late_re * early_re + late_im * early_im
-                    imag_sum += late_im * early_re - late_re * early_im
-                out_ref[lag, pl.ds(2 * first, step, 2), :] = real_sum * scale
-                out_ref[lag, pl.ds(2 * first + 1, step, 2), :] = imag_sum * scale
+        lags = range(group * width, (group + 1) * width)
+        for pair in range(0, len(blocks), 2):
+            sums = {}
+            for e in range(energies - lags[0]):
+                for first in blocks[pair:pair + 2]:
+                    early = in_ref[place(e), first:first + step]
+                    early_swapped = swapped_ref[place(e), first:first + step]
+                    for lag in lags:
+                        if e + lag >= energies:
+                            continue
+                        late = in_ref[place(e + lag), first:first + step]
+                        straight, crossed = late * early, late * early_swapped
+                        if (lag, first) in sums:
+                            straight, crossed = sums[lag, first][0] + straight, sums[lag, first][1] + crossed
+                        sums[lag, first] = straight, crossed
+            for (lag, first), (straight, crossed) in sums.items():
+                both = jnp.where(even_in_step, straight + with_next_row(straight), crossed - with_row_before(crossed))
+                out_ref[lag, first:first + step] = both * scale
         part = pl.ds(group * width, width)
         copies.append(pltpu.make_async_copy(out_ref.at[part], out_hbm.at[part], sems.at[group]))
         copies[-1].start()
@@ -385,6 +413,7 @@
         in_specs=[pl.BlockSpec(memory_space=pltpu.VMEM)],
         out_specs=pl.BlockSpec(memory_space=pltpu.HBM),
         scratch_shapes=[
+            pltpu.VMEM((energies, double_rows, lanes), F32),
             pltpu.VMEM((LAGS, double_rows, lanes), F32),
             pltpu.SemaphoreType.DMA((4,)),
         ],

time: 26 us -> 26.1 us (level)
  no operation moved by 1% of the time
where the time goes in v12:
time: 26.1 us; the launch traced here: 25.7 us
  blocking collectives  15.4 us (59%)
  Pallas kernels  9.8 us (38%)
  waiting for transfers between devices  0.32 us (1%)
    all_to_all x1, blocking collectives, per_device(): lax.all_to_all(send, 'energy', split_axis=1, concat_axis=0, axis_index_gr...  15.4 us
    pallas_call x1, Pallas kernels, head(): pl.pallas_call(head_kernel, out_shape=(jax.ShapeDtypeStruct((energies,) +...  4.39 us
    pallas_call x1, Pallas kernels, lag_sums(): pl.pallas_call(functools.partial(lag_kernel, here), out_shape=jax.ShapeDt...  2 us
    pallas_call x1, Pallas kernels, tail(): pl.pallas_call(functools.partial(tail_kernel, keep, share_rows, hop, last...  1.91 us
    pallas_call x1, Pallas kernels, middle(): pl.pallas_call(functools.partial(middle_kernel, keep, share_rows), out_sh...  1.49 us
  transfers between devices with their start and end apart: 2, of which 1 were waited for; matrix products, arithmetic and copies ran while one was open for 0% of the time, Pallas kernels for 23%

profile of v12, /device:TPU:1, one launch (start us, length us, event | category | flops | bytes accessed | tf_op | source)
XLA Modules:
  0.0 25.7 jit_solution(13406853365156130307)
XLA Ops:
  0.0 0.1 collective-permute-start.1
  0.1 4.4 %head_cells.1 = (f32[1,2,2,256,128]{4,3,2,1,0:T(8,128)S(1)}, f32[1,2,2,2,256,128]{5,4,3,2,1,0:T(8,128)S(1)}, bf16[1,1,6,256,256]{4,3,2,1,0:T(8,128)(2,1)S(1)}, f...) custom-call(f32[1,2,2,256,256]{4,3,2,1,0:T(8,128)} %g_hbm.1, f32[1,2,2,256,256]{4,3,2,1,0:T(8,128)} %s_hbm.1, ...), custom_call_target="tpu_custom_call" | custom-call | tf_op jit(solution)/shard_map/head_cells/pallas_call | solution.py:212
  4.5 0.1 collective-permute-start
  4.6 0.0 collective-permute-done.1.before_ref
  4.6 1.5 %middle_cells.1 = (f32[1,16,32,128]{3,2,1,0:T(8,128)S(1)}, bf16[1,2,6,256,256]{4,3,2,1,0:T(8,128)(2,1)S(1)}, bf16[1,2,6,256,256]{4,3,2,1,0:T(8,128)(2,1)S(1)}) custom-call(f32[1,2,2,256,256]{4,3,2,1,0:T(8,128)S(1)} %collective-permute-done.1.before_ref, f32[1,2,2,256,128]{4,3,2,1,0:T(8,128)S(1)} %get-tuple-element.13.inner_ref, ...), custom_call_target="tpu_custom_call" | custom-call | flops 402653184 | bytes 262144 | tf_op jit(solution)/shard_map/middle_cells/pallas_call | solution.py:294
  6.1 0.3 %collective-permute-done.incoming_ref = f32[1,2,2,256,128]{4,3,2,1,0:T(8,128)S(1)} collective-permute-done((f32[1,2,2,256,128]{4,3,2,1,0:T(8,128)S(1)}, f32[1,2,2,256,128]{4,3,2,1,0:T(8,128)S(1)}, u32[]{:S(2)}, u32[]{:S(2)}) %collective-permute-start) | collective-permute-done | bytes 524320 | tf_op jit(solution)/shard_map/ppermute | solution.py:435
  6.4 1.9 %tail_cells.1 = f32[1,16,32,128]{3,2,1,0:T(8,128)S(1)} custom-call(f32[1,2,2,256,128]{4,3,2,1,0:T(8,128)S(1)} %collective-permute-done.incoming_ref, bf16[1,2,6,256,256]{4,3,2,1,0:T(8,128)(2,1)S(1)} %get-tuple-element.18.left_ref, bf16[1,2,6,256,256]{4,3,2,1,0:T(8,128)(2,1)S(1)} %get-tuple-element.19.right_ref, ...), custom_call_target="tpu_custom_call", output_to_operand_aliasing={{}: (5, {})} | custom-call | tf_op jit(solution)/shard_map/tail_cells/pallas_call | solution.py:347
  8.4 15.4 %all_to_all.4 = f32[1,16,32,128]{3,2,0,1:T(8,128)} all-to-all(f32[1,16,32,128]{3,2,0,1:T(8,128)S(1)} %bitcast.7), channel_id=1, replica_groups={{15,14,13,12,11,10,9,8,7,6,5,4,3,2,1,0},{31,30,29,28,27,26,25,24,23,22,..., dimensions={1} | all-to-all | bytes 524288 | tf_op jit(solution)/shard_map/all_to_all | solution.py:443
  23.7 2.0 %lag_sums.1 = f32[16,32,128]{2,1,0:T(8,128)} custom-call(f32[16,32,128]{2,1,0:T(8,128)} %bitcast.8), custom_call_target="tpu_custom_call" | custom-call | tf_op jit(solution)/shard_map/lag_sums/pallas_call | solution.py:410
Async XLA Ops:
  0.0 4.6 %collective-permute-start.1 = (f32[1,2,2,256,256]{4,3,2,1,0:T(8,128)}, f32[1,2,2,256,256]{4,3,2,1,0:T(8,128)S(1)}, u32[]{:S(2)}, u32[]{:S(2)}) collective-permute-start(f32[1,2,2,256,256]{4,3,2,1,0:T(8,128)} %g_hbm.1), channel_id=1, source_target_pairs={{0,16},{16,0},{1,17},{17,1},{2,18},{18,2},{3,19},{19,3},{4,20},{20... | collective-permute-start | bytes 3145736 | tf_op jit(solution)/shard_map/ppermute | solution.py:433
  4.5 2.0 %collective-permute-start = (f32[1,2,2,256,128]{4,3,2,1,0:T(8,128)S(1)}, f32[1,2,2,256,128]{4,3,2,1,0:T(8,128)S(1)}, u32[]{:S(2)}, u32[]{:S(2)}) collective-permute-start(f32[1,2,2,256,128]{4,3,2,1,0:T(8,128)S(1)} %get-tuple-element.13.inner_ref), channel_id=1, source_target_pairs={{0,16},{16,0},{1,17},{17,1},{2,18},{18,2},{3,19},{19,3},{4,20},{20... | collective-permute-start | bytes 1572872 | tf_op jit(solution)/shard_map/ppermute | solution.py:435

commit v13 on v11

--- a/solution.py
+++ b/solution.py
@@ -76,7 +76,17 @@
     return jnp.concatenate(rows, axis=0)
 
 
+def sending_order(owners):
+    inner = 1
+    while inner * inner < owners:
+        inner *= 2
+    if owners % inner:
+        inner = 1
+    return [start + n for n in range(inner)[::-1] for start in range(0, owners, inner)[::-1]]
+
+
 def pick_into(send_ref, e, cell, matrix_ref, kept_ref, keep, share_rows):
+    order = sending_order(send_ref.shape[1])
     nblk = matrix_ref.shape[-2] // BLOCK
     half = BLOCK // 2
     lane = lax.broadcasted_iota(jnp.int32, (half, LANES), 1)
@@ -96,7 +106,7 @@
             first = (cell * keep + k) * half
             for s in range(0, half, piece):
                 owner, inside = divmod(first + s, share_rows)
-                send_ref[e, send_ref.shape[1] - 1 - owner, pl.ds(part * share_rows + inside, piece), :] = flat[s:s + piece]
+                send_ref[e, order.index(owner), pl.ds(part * share_rows + inside, piece), :] = flat[s:s + piece]
 
 
 def head_kernel(g_hbm, s_hbm, b_hbm, pattern_hbm, lead_hbm,
@@ -352,8 +362,10 @@
     groups = sems.shape[0]
     width = LAGS // groups
 
+    order = sending_order(energies // here)
+
     def at(e, first):
-        place = (energies // here - 1 - e // here) * here + e % here
+        place = order.index(e // here) * here + e % here
         return in_ref[place, first:first + step]
 
     copies = []
@@ -410,8 +422,8 @@
             incoming = lax.ppermute(leaving, "chain", ring)
         last = hop == length - 2
         leaving, send = tail(keep, share_rows, hop, last, incoming, left, right, fresh, kept_blocks, leaving, send)
-    backwards = [list(range(owners))[::-1]]
-    owned = lax.all_to_all(send, "energy", split_axis=1, concat_axis=0, axis_index_groups=backwards, tiled=True)
+    groups = [sending_order(owners)]
+    owned = lax.all_to_all(send, "energy", split_axis=1, concat_axis=0, axis_index_groups=groups, tiled=True)
     return lag_sums(retarded.shape[0], owned.reshape((-1,) + owned.shape[2:]))
 
 

time: 26 us -> 26.2 us (level)
  no operation moved by 1% of the time
where the time goes in v13:
time: 26.2 us; the launch traced here: 25.8 us
  blocking collectives  15.5 us (59%)
  Pallas kernels  9.73 us (37%)
  waiting for transfers between devices  0.32 us (1%)
    all_to_all x1, blocking collectives, per_device(): lax.all_to_all(send, 'energy', split_axis=1, concat_axis=0, axis_index_gr...  15.5 us
    pallas_call x1, Pallas kernels, head(): pl.pallas_call(head_kernel, out_shape=(jax.ShapeDtypeStruct((energies,) +...  4.39 us
    pallas_call x1, Pallas kernels, tail(): pl.pallas_call(functools.partial(tail_kernel, keep, share_rows, hop, last...  1.94 us
    pallas_call x1, Pallas kernels, lag_sums(): pl.pallas_call(functools.partial(lag_kernel, here), out_shape=jax.ShapeDt...  1.91 us
    pallas_call x1, Pallas kernels, middle(): pl.pallas_call(functools.partial(middle_kernel, keep, share_rows), out_sh...  1.49 us
  transfers between devices with their start and end apart: 2, of which 1 were waited for; matrix products, arithmetic and copies ran while one was open for 0% of the time, Pallas kernels for 23%

profile of v13, /device:TPU:1, one launch (start us, length us, event | category | flops | bytes accessed | tf_op | source)
XLA Modules:
  0.0 25.8 jit_solution(4160842191927633314)
XLA Ops:
  0.0 0.1 collective-permute-start.1
  0.1 4.4 %head_cells.1 = (f32[1,2,2,256,128]{4,3,2,1,0:T(8,128)S(1)}, f32[1,2,2,2,256,128]{5,4,3,2,1,0:T(8,128)S(1)}, bf16[1,1,6,256,256]{4,3,2,1,0:T(8,128)(2,1)S(1)}, f...) custom-call(f32[1,2,2,256,256]{4,3,2,1,0:T(8,128)} %g_hbm.1, f32[1,2,2,256,256]{4,3,2,1,0:T(8,128)} %s_hbm.1, ...), custom_call_target="tpu_custom_call" | custom-call | tf_op jit(solution)/shard_map/head_cells/pallas_call | solution.py:205
  4.5 0.1 collective-permute-start
  4.6 0.0 collective-permute-done.1.before_ref
  4.6 1.5 %middle_cells.1 = (f32[1,16,32,128]{3,2,1,0:T(8,128)S(1)}, bf16[1,2,6,256,256]{4,3,2,1,0:T(8,128)(2,1)S(1)}, bf16[1,2,6,256,256]{4,3,2,1,0:T(8,128)(2,1)S(1)}) custom-call(f32[1,2,2,256,256]{4,3,2,1,0:T(8,128)S(1)} %collective-permute-done.1.before_ref, f32[1,2,2,256,128]{4,3,2,1,0:T(8,128)S(1)} %get-tuple-element.13.inner_ref, ...), custom_call_target="tpu_custom_call" | custom-call | flops 402653184 | bytes 262144 | tf_op jit(solution)/shard_map/middle_cells/pallas_call | solution.py:287
  6.1 0.3 %collective-permute-done.incoming_ref = f32[1,2,2,256,128]{4,3,2,1,0:T(8,128)S(1)} collective-permute-done((f32[1,2,2,256,128]{4,3,2,1,0:T(8,128)S(1)}, f32[1,2,2,256,128]{4,3,2,1,0:T(8,128)S(1)}, u32[]{:S(2)}, u32[]{:S(2)}) %collective-permute-start) | collective-permute-done | bytes 524320 | tf_op jit(solution)/shard_map/ppermute | solution.py:418
  6.4 1.9 %tail_cells.1 = f32[1,16,32,128]{3,2,1,0:T(8,128)S(1)} custom-call(f32[1,2,2,256,128]{4,3,2,1,0:T(8,128)S(1)} %collective-permute-done.incoming_ref, bf16[1,2,6,256,256]{4,3,2,1,0:T(8,128)(2,1)S(1)} %get-tuple-element.18.left_ref, bf16[1,2,6,256,256]{4,3,2,1,0:T(8,128)(2,1)S(1)} %get-tuple-element.19.right_ref, ...), custom_call_target="tpu_custom_call", output_to_operand_aliasing={{}: (5, {})} | custom-call | tf_op jit(solution)/shard_map/tail_cells/pallas_call | solution.py:340
  8.4 15.5 %all_to_all.4 = f32[1,16,32,128]{3,2,0,1:T(8,128)} all-to-all(f32[1,16,32,128]{3,2,0,1:T(8,128)S(1)} %bitcast.7), channel_id=1, replica_groups={{15,11,7,3,14,10,6,2,13,9,5,1,12,8,4,0},{31,27,23,19,30,26,22,18,29,25,..., dimensions={1} | all-to-all | bytes 524288 | tf_op jit(solution)/shard_map/all_to_all | solution.py:426
  23.9 1.9 %lag_sums.1 = f32[16,32,128]{2,1,0:T(8,128)} custom-call(f32[16,32,128]{2,1,0:T(8,128)} %bitcast.8), custom_call_target="tpu_custom_call" | custom-call | tf_op jit(solution)/shard_map/lag_sums/pallas_call | solution.py:394
Async XLA Ops:
  0.0 4.6 %collective-permute-start.1 = (f32[1,2,2,256,256]{4,3,2,1,0:T(8,128)}, f32[1,2,2,256,256]{4,3,2,1,0:T(8,128)S(1)}, u32[]{:S(2)}, u32[]{:S(2)}) collective-permute-start(f32[1,2,2,256,256]{4,3,2,1,0:T(8,128)} %g_hbm.1), channel_id=1, source_target_pairs={{0,16},{16,0},{1,17},{17,1},{2,18},{18,2},{3,19},{19,3},{4,20},{20... | collective-permute-start | bytes 3145736 | tf_op jit(solution)/shard_map/ppermute | solution.py:416
  4.5 2.0 %collective-permute-start = (f32[1,2,2,256,128]{4,3,2,1,0:T(8,128)S(1)}, f32[1,2,2,256,128]{4,3,2,1,0:T(8,128)S(1)}, u32[]{:S(2)}, u32[]{:S(2)}) collective-permute-start(f32[1,2,2,256,128]{4,3,2,1,0:T(8,128)S(1)} %get-tuple-element.13.inner_ref), channel_id=1, source_target_pairs={{0,16},{16,0},{1,17},{17,1},{2,18},{18,2},{3,19},{19,3},{4,20},{20... | collective-permute-start | bytes 1572872 | tf_op jit(solution)/shard_map/ppermute | solution.py:418

commit v14 on v11

--- a/solution.py
+++ b/solution.py
@@ -38,6 +38,13 @@
         tall = jnp.concatenate([right[n], right[n + 1], right[n]], axis=0)
         real.append(dot(wide, tall))
     return real[0] - real[1], real[2] - real[0] - real[1]
+
+
+def sandwich(left, inner, right):
+    rows = left[0].shape[0] // 2
+    halves = [product(tuple(part[n * rows:(n + 1) * rows] for part in left), inner) for n in range(2)]
+    done = [product(parts(half), right) for half in halves]
+    return tuple(jnp.concatenate(both, axis=0) for both in zip(*done))
 
 
 def put_parts(ref, values):
@@ -147,7 +154,7 @@
             bridge = bridge_of(i)
             bridge_left, bridge_right = parts(bridge), parts(adjoint(bridge))
             for e in range(energies):
-                entered = product(parts(product(bridge_left, parts(states[e]))), bridge_right)
+                entered = sandwich(bridge_left, parts(states[e]), bridge_right)
                 if e == 0:
                     g_copies[i].wait()
                     s_copies[i].wait()
@@ -156,7 +163,7 @@
                     put_state(inner_ref.at[e], inner)
                 else:
                     green = green_of(e, i)
-                    states[e] = product(parts(product(parts(green), parts(inner))), parts(adjoint(green)))
+                    states[e] = sandwich(parts(green), parts(inner), parts(adjoint(green)))
                     put_state(fresh_ref.at[e, i], states[e])
 
     @pl.when(position > 0)
@@ -176,9 +183,8 @@
                 if i < final:
                     put_parts(factor_ref.at[e, i], parts(product(green_left, parts(bridge))))
                 if i > 0:
-                    half = parts(product(parts(bridge), parts(states[e])))
-                    inner = plus(inner, product(half, parts(adjoint(bridge))))
-                states[e] = product(parts(product(green_left, parts(inner))), green_right)
+                    inner = plus(inner, sandwich(parts(bridge), parts(states[e]), parts(adjoint(bridge))))
+                states[e] = sandwich(green_left, parts(inner), green_right)
                 put_state(fresh_ref.at[e, i], states[e])
 
 
@@ -229,7 +235,7 @@
         for e in range(energies):
             green = green_ref[e, 0], green_ref[e, 1]
             inner = parts(get_state(inner_ref.at[e]))
-            put_state(state_ref.at[e], product(parts(product(parts(green), inner)), parts(adjoint(green))))
+            put_state(state_ref.at[e], sandwich(parts(green), inner, parts(adjoint(green))))
             if e == 0:
                 kept_copy.wait()
             for i in range(cells):
@@ -344,7 +350,7 @@
     return (leaving, result[0]) if last else result
 
 
-def lag_kernel(here, in_ref, out_hbm, out_ref, sems):
+def lag_kernel(here, in_ref, out_hbm, out_ref, mixed_ref, sems):
     energies, double_rows, _ = in_ref.shape
     rows = double_rows // 2
     step = min(8, rows)
@@ -356,17 +362,29 @@
         place = (energies // here - 1 - e // here) * here + e % here
         return in_ref[place, first:first + step]
 
+    for e in range(energies):
+        for first in range(0, rows, step):
+            re, im = at(e, first), at(e, rows + first)
+            mixed_ref[0, e, first:first + step] = re + im
+            mixed_ref[1, e, first:first + step] = re - im
+
+    def at_all(e, first, kind):
+        return mixed_ref[kind, e, first:first + step]
+
     copies = []
     for group in range(groups):
         for lag in range(group * width, (group + 1) * width):
             for first in range(0, rows, step):
-                real_sum = jnp.zeros((step, LANES), F32)
-                imag_sum = jnp.zeros((step, LANES), F32)
+                re_sum = jnp.zeros((step, LANES), F32)
+                im_sum = jnp.zeros((step, LANES), F32)
+                mixed_sum = jnp.zeros((step, LANES), F32)
                 for e in range(energies - lag):
                     late_re, late_im = at(e + lag, first), at(e + lag, rows + first)
                     early_re, early_im = at(e, first), at(e, rows + first)
-                    real_sum += late_re * early_re + late_im * early_im
-                    imag_sum += late_im * early_re - late_re * early_im
+                    re_sum += late_re * early_re
+                    im_sum += late_im * early_im
+                    mixed_sum += at_all(e + lag, first, 0) * at_all(e, first, 1)
+                real_sum, imag_sum = re_sum + im_sum, mixed_sum - re_sum + im_sum
                 out_ref[lag, pl.ds(2 * first, step, 2), :] = real_sum * scale
                 out_ref[lag, pl.ds(2 * first + 1, step, 2), :] = imag_sum * scale
         part = pl.ds(group * width, width)
@@ -386,6 +404,7 @@
         out_specs=pl.BlockSpec(memory_space=pltpu.HBM),
         scratch_shapes=[
             pltpu.VMEM((LAGS, double_rows, lanes), F32),
+            pltpu.VMEM((2, energies, rows, lanes), F32),
             pltpu.SemaphoreType.DMA((4,)),
         ],
         name="lag_sums",

time: 26 us -> 26 us (level)
  no operation moved by 1% of the time
where the time goes in v14:
time: 26 us; the launch traced here: 25.6 us
  blocking collectives  15.3 us (59%)
  Pallas kernels  9.69 us (37%)
  waiting for transfers between devices  0.3 us (1%)
    all_to_all x1, blocking collectives, per_device(): lax.all_to_all(send, 'energy', split_axis=1, concat_axis=0, axis_index_gr...  15.3 us
    pallas_call x1, Pallas kernels, head(): pl.pallas_call(head_kernel, out_shape=(jax.ShapeDtypeStruct((energies,) +...  4.38 us
    pallas_call x1, Pallas kernels, tail(): pl.pallas_call(functools.partial(tail_kernel, keep, share_rows, hop, last...  1.95 us
    pallas_call x1, Pallas kernels, lag_sums(): pl.pallas_call(functools.partial(lag_kernel, here), out_shape=jax.ShapeDt...  1.87 us
    pallas_call x1, Pallas kernels, middle(): pl.pallas_call(functools.partial(middle_kernel, keep, share_rows), out_sh...  1.49 us
  transfers between devices with their start and end apart: 2, of which 1 were waited for; matrix products, arithmetic and copies ran while one was open for 0% of the time, Pallas kernels for 23%

profile of v14, /device:TPU:1, one launch (start us, length us, event | category | flops | bytes accessed | tf_op | source)
XLA Modules:
  0.0 25.6 jit_solution(4102711594463111598)
XLA Ops:
  0.0 0.1 collective-permute-start.1
  0.1 4.4 %head_cells.1 = (f32[1,2,2,256,128]{4,3,2,1,0:T(8,128)S(1)}, f32[1,2,2,2,256,128]{5,4,3,2,1,0:T(8,128)S(1)}, bf16[1,1,6,256,256]{4,3,2,1,0:T(8,128)(2,1)S(1)}, f...) custom-call(f32[1,2,2,256,256]{4,3,2,1,0:T(8,128)} %g_hbm.1, f32[1,2,2,256,256]{4,3,2,1,0:T(8,128)} %s_hbm.1, ...), custom_call_target="tpu_custom_call" | custom-call | tf_op jit(solution)/shard_map/head_cells/pallas_call | solution.py:201
  4.4 0.2 collective-permute-start
  4.6 0.0 collective-permute-done.1.before_ref
  4.6 1.5 %middle_cells.1 = (f32[1,16,32,128]{3,2,1,0:T(8,128)S(1)}, bf16[1,2,6,256,256]{4,3,2,1,0:T(8,128)(2,1)S(1)}, bf16[1,2,6,256,256]{4,3,2,1,0:T(8,128)(2,1)S(1)}) custom-call(f32[1,2,2,256,256]{4,3,2,1,0:T(8,128)S(1)} %collective-permute-done.1.before_ref, f32[1,2,2,256,128]{4,3,2,1,0:T(8,128)S(1)} %get-tuple-element.13.inner_ref, ...), custom_call_target="tpu_custom_call" | custom-call | flops 402653184 | bytes 262144 | tf_op jit(solution)/shard_map/middle_cells/pallas_call | solution.py:283
  6.1 0.3 %collective-permute-done.incoming_ref = f32[1,2,2,256,128]{4,3,2,1,0:T(8,128)S(1)} collective-permute-done((f32[1,2,2,256,128]{4,3,2,1,0:T(8,128)S(1)}, f32[1,2,2,256,128]{4,3,2,1,0:T(8,128)S(1)}, u32[]{:S(2)}, u32[]{:S(2)}) %collective-permute-start) | collective-permute-done | bytes 524320 | tf_op jit(solution)/shard_map/ppermute | solution.py:425
  6.4 1.9 %tail_cells.1 = f32[1,16,32,128]{3,2,1,0:T(8,128)S(1)} custom-call(f32[1,2,2,256,128]{4,3,2,1,0:T(8,128)S(1)} %collective-permute-done.incoming_ref, bf16[1,2,6,256,256]{4,3,2,1,0:T(8,128)(2,1)S(1)} %get-tuple-element.18.left_ref, bf16[1,2,6,256,256]{4,3,2,1,0:T(8,128)(2,1)S(1)} %get-tuple-element.19.right_ref, ...), custom_call_target="tpu_custom_call", output_to_operand_aliasing={{}: (5, {})} | custom-call | tf_op jit(solution)/shard_map/tail_cells/pallas_call | solution.py:336
  8.4 15.3 %all_to_all.4 = f32[1,16,32,128]{3,2,0,1:T(8,128)} all-to-all(f32[1,16,32,128]{3,2,0,1:T(8,128)S(1)} %bitcast.7), channel_id=1, replica_groups={{15,14,13,12,11,10,9,8,7,6,5,4,3,2,1,0},{31,30,29,28,27,26,25,24,23,22,..., dimensions={1} | all-to-all | bytes 524288 | tf_op jit(solution)/shard_map/all_to_all | solution.py:433
  23.7 1.9 %lag_sums.1 = f32[16,32,128]{2,1,0:T(8,128)} custom-call(f32[16,32,128]{2,1,0:T(8,128)} %bitcast.8), custom_call_target="tpu_custom_call" | custom-call | tf_op jit(solution)/shard_map/lag_sums/pallas_call | solution.py:400
Async XLA Ops:
  0.0 4.6 %collective-permute-start.1 = (f32[1,2,2,256,256]{4,3,2,1,0:T(8,128)}, f32[1,2,2,256,256]{4,3,2,1,0:T(8,128)S(1)}, u32[]{:S(2)}, u32[]{:S(2)}) collective-permute-start(f32[1,2,2,256,256]{4,3,2,1,0:T(8,128)} %g_hbm.1), channel_id=1, source_target_pairs={{0,16},{16,0},{1,17},{17,1},{2,18},{18,2},{3,19},{19,3},{4,20},{20... | collective-permute-start | bytes 3145736 | tf_op jit(solution)/shard_map/ppermute | solution.py:423
  4.4 2.0 %collective-permute-start = (f32[1,2,2,256,128]{4,3,2,1,0:T(8,128)S(1)}, f32[1,2,2,256,128]{4,3,2,1,0:T(8,128)S(1)}, u32[]{:S(2)}, u32[]{:S(2)}) collective-permute-start(f32[1,2,2,256,128]{4,3,2,1,0:T(8,128)S(1)} %get-tuple-element.13.inner_ref), channel_id=1, source_target_pairs={{0,16},{16,0},{1,17},{17,1},{2,18},{18,2},{3,19},{19,3},{4,20},{20... | collective-permute-start | bytes 1572872 | tf_op jit(solution)/shard_map/ppermute | solution.py:425

commit v15 on v14

--- a/solution.py
+++ b/solution.py
@@ -108,7 +108,7 @@
 
 def head_kernel(g_hbm, s_hbm, b_hbm, pattern_hbm, lead_hbm,
                 inner_ref, fresh_ref, factor_ref, green_ref, bridge_ref,
-                pattern_ref, g_ref, s_ref, b_ref, lead_ref, sems):
+                pattern_ref, s_ref, b_ref, lead_ref, sems):
     energies, cells, _, size, _ = s_ref.shape
     position = lax.axis_index("chain")
     final = cells - 1
@@ -116,12 +116,9 @@
     def fetch(slot, source, target):
         return pltpu.make_async_copy(source, target, sems.at[slot])
 
-    def g_place(i):
-        return green_ref if i == final else g_ref.at[:, i]
-
     lead_copy = fetch(0, lead_hbm, lead_ref)
     b_copies = [fetch(1 + i, b_hbm.at[i], b_ref.at[i]) for i in range(cells)]
-    g_copies = [fetch(1 + cells + i, g_hbm.at[:, i], g_place(i)) for i in range(cells)]
+    g_copies = [fetch(1 + cells + i, g_hbm.at[:, i], green_ref.at[:, i]) for i in range(cells)]
     s_copies = [fetch(1 + 2 * cells + i, s_hbm.at[:, i], s_ref.at[:, i]) for i in range(cells)]
     pattern_copy = fetch(1 + 3 * cells, pattern_hbm, pattern_ref)
     pattern_copy.start()
@@ -141,9 +138,7 @@
         return b_ref[i, 0] * mask, b_ref[i, 1] * mask
 
     def green_of(e, i):
-        if i == final:
-            return green_ref[e, 0], green_ref[e, 1]
-        return g_ref[e, i, 0], g_ref[e, i, 1]
+        return green_ref[e, i, 0], green_ref[e, i, 1]
 
     @pl.when(position == 0)
     def _():
@@ -151,24 +146,30 @@
         states = [(lead_ref[e, 0], lead_ref[e, 1]) for e in range(energies)]
         for i in range(cells):
             b_copies[i].wait()
-            bridge = bridge_of(i)
-            bridge_left, bridge_right = parts(bridge), parts(adjoint(bridge))
+            bridge = parts(bridge_of(i))
+            if i == 0 or i < final:
+                bridge_right = parts(adjoint(bridge_of(i)))
             for e in range(energies):
-                entered = sandwich(bridge_left, parts(states[e]), bridge_right)
+                if i == 0 or i < final:
+                    entered = sandwich(bridge, parts(states[e]), bridge_right)
+                else:
+                    across = product(bridge, parts(green_of(e, i - 1)))
+                    entered = sandwich(parts(across), parts(states[e]), parts(adjoint(across)))
                 if e == 0:
                     g_copies[i].wait()
                     s_copies[i].wait()
                 inner = plus((s_ref[e, i, 0], s_ref[e, i, 1]), entered)
                 if i == final:
                     put_state(inner_ref.at[e], inner)
-                else:
+                    continue
+                states[e] = inner
+                if i < final - 1:
                     green = green_of(e, i)
                     states[e] = sandwich(parts(green), parts(inner), parts(adjoint(green)))
-                    put_state(fresh_ref.at[e, i], states[e])
+                put_state(fresh_ref.at[e, i], states[e])
 
     @pl.when(position > 0)
     def _():
-        states = [None] * energies
         for i in range(cells):
             b_copies[i].wait()
             g_copies[i].wait()
@@ -178,14 +179,11 @@
                 bridge_ref[0], bridge_ref[1] = bridge
             for e in range(energies):
                 green = green_of(e, i)
-                green_left, green_right = parts(green), parts(adjoint(green))
-                inner = s_ref[e, i, 0], s_ref[e, i, 1]
+                green_left = parts(green)
                 if i < final:
-                    put_parts(factor_ref.at[e, i], parts(product(green_left, parts(bridge))))
-                if i > 0:
-                    inner = plus(inner, sandwich(parts(bridge), parts(states[e]), parts(adjoint(bridge))))
-                states[e] = sandwich(green_left, parts(inner), green_right)
-                put_state(fresh_ref.at[e, i], states[e])
+                    factor_ref[e, i, 0], factor_ref[e, i, 1] = product(green_left, parts(bridge))
+                inner = parts((s_ref[e, i, 0], s_ref[e, i, 1]))
+                put_state(fresh_ref.at[e, i], sandwich(green_left, inner, parts(adjoint(green))))
 
 
 def in_hbm(value):
@@ -203,15 +201,14 @@
         out_shape=(
             jax.ShapeDtypeStruct((energies,) + state_shape, F32),
             jax.ShapeDtypeStruct((energies, cells) + state_shape, F32),
-            jax.ShapeDtypeStruct((energies, others, 6, size, size), BF16),
-            jax.ShapeDtypeStruct((energies, 2, size, size), F32),
+            jax.ShapeDtypeStruct((energies, others, 2, size, size), F32),
+            jax.ShapeDtypeStruct(retarded.shape, F32),
             jax.ShapeDtypeStruct((2, size, size), F32),
         ),
         in_specs=[hbm] * 5,
         out_specs=(vmem,) * 5,
         scratch_shapes=[
             pltpu.SMEM(pattern.shape, jnp.int32),
-            pltpu.VMEM((energies, others, 2, size, size), F32),
             pltpu.VMEM(lesser_sigma.shape, F32),
             pltpu.VMEM(coupling.shape, F32),
             pltpu.VMEM(lead.shape, F32),
@@ -233,45 +230,39 @@
     @pl.when(position == 0)
     def _():
         for e in range(energies):
-            green = green_ref[e, 0], green_ref[e, 1]
-            inner = parts(get_state(inner_ref.at[e]))
-            put_state(state_ref.at[e], sandwich(parts(green), inner, parts(adjoint(green))))
-            if e == 0:
-                kept_copy.wait()
             for i in range(cells):
-                matrix_ref = state_ref.at[e] if i == final else fresh_ref.at[e, i]
+                matrix_ref = fresh_ref.at[e, i]
+                if i >= final - 1:
+                    green = green_ref[e, i, 0], green_ref[e, i, 1]
+                    inner = get_state(inner_ref.at[e] if i == final else matrix_ref)
+                    matrix_ref = state_ref.at[e, i - max(final - 1, 0)]
+                    put_state(matrix_ref, sandwich(parts(green), parts(inner), parts(adjoint(green))))
+                if i == 0 and e == 0:
+                    kept_copy.wait()
                 pick_into(send_ref, e, i, matrix_ref, kept_ref, keep, share_rows)
 
-    def chain_of_factors(with_before):
+    def factors(with_before):
         for e in range(energies):
-            last_factor = product(parts((green_ref[e, 0], green_ref[e, 1])), parts((bridge_ref[0], bridge_ref[1])))
-            joined = None
-            if with_before:
-                joined = before_ref[e, final, 0], before_ref[e, final, 1]
             for i in range(cells):
-                if joined is not None:
-                    factor = parts(last_factor) if i == final else get_parts(factor_ref.at[e, i])
-                    joined = product(factor, parts(joined))
-                    put_parts(left_ref.at[e, i], parts(joined))
-                    put_parts(right_ref.at[e, i], parts(adjoint(joined)))
-                    continue
-                if i == final:
-                    joined = last_factor
+                if i < final:
+                    factor = factor_ref[e, i, 0], factor_ref[e, i, 1]
                 else:
-                    whole = get_parts(factor_ref.at[e, i])
-                    joined = tuple(whole[n].astype(F32) + whole[n + 1].astype(F32) for n in (0, 2))
-                put_parts(left_ref.at[e, i], parts(joined))
-                put_parts(right_ref.at[e, i], parts(adjoint(joined)))
+                    green = parts((green_ref[e, i, 0], green_ref[e, i, 1]))
+                    factor = product(green, parts((bridge_ref[0], bridge_ref[1])))
+                if i == 0 and with_before:
+                    factor = product(parts(factor), parts((before_ref[e, final, 0], before_ref[e, final, 1])))
+                put_parts(left_ref.at[e, i], parts(factor))
+                put_parts(right_ref.at[e, i], parts(adjoint(factor)))
 
     @pl.when(position == 1)
     def _():
-        chain_of_factors(True)
+        factors(True)
         kept_copy.wait()
 
     if lax.axis_size("chain") > 2:
         @pl.when(position > 1)
         def _():
-            chain_of_factors(False)
+            factors(False)
             kept_copy.wait()
 
 
@@ -291,7 +282,7 @@
         out_specs=(vmem,) * 3,
         scratch_shapes=[
             pltpu.SMEM(kept_blocks.shape, jnp.int32),
-            pltpu.VMEM(inner.shape, F32),
+            pltpu.VMEM((energies, 2) + inner.shape[1:], F32),
             pltpu.SemaphoreType.DMA,
         ],
         compiler_params=pltpu.CompilerParams(vmem_limit_bytes=32 << 20),
@@ -314,13 +305,11 @@
         kept_copy = pltpu.make_async_copy(kept_hbm, kept_ref, sem)
         kept_copy.start()
         for e in range(energies):
-            state = parts(get_state(incoming_ref.at[e]))
-            halves = []
+            state = get_state(incoming_ref.at[e])
             for i in range(cells):
-                halves.append(parts(product(get_parts(left_ref.at[e, i]), state)))
-            for i in range(cells):
-                grown = product(halves[i], get_parts(right_ref.at[e, i]))
-                put_state(state_ref.at[e, i], plus(get_state(fresh_ref.at[e, i]), grown))
+                grown = sandwich(get_parts(left_ref.at[e, i]), parts(state), get_parts(right_ref.at[e, i]))
+                state = plus(get_state(fresh_ref.at[e, i]), grown)
+                put_state(state_ref.at[e, i], state)
                 if i == 0 and e == 0:
                     kept_copy.wait()
                 pick_into(send_ref, e, i, state_ref.at[e, i], kept_ref, keep, share_rows)

time: 26 us -> 25.9 us (level)
  the two profiles are of different devices: /device:TPU:1 before, /device:TPU:0 now
where the time goes in v15:
time: 25.9 us; the launch traced here: 25.7 us
  blocking collectives  17.6 us (68%)
  Pallas kernels  7.55 us (29%)
  starting transfers between devices  0.52 us (2%)
    all_to_all x1, blocking collectives, per_device(): lax.all_to_all(send, 'energy', split_axis=1, concat_axis=0, axis_index_gr...  17.6 us
    pallas_call x1, Pallas kernels, head(): pl.pallas_call(head_kernel, out_shape=(jax.ShapeDtypeStruct((energies,) +...  3.65 us
    pallas_call x1, Pallas kernels, middle(): pl.pallas_call(functools.partial(middle_kernel, keep, share_rows), out_sh...  2 us
    pallas_call x1, Pallas kernels, lag_sums(): pl.pallas_call(functools.partial(lag_kernel, here), out_shape=jax.ShapeDt...  1.87 us
  transfers between devices with their start and end apart: 2, of which 0 were waited for; matrix products, arithmetic and copies ran while one was open for 0% of the time, Pallas kernels for 22%

profile of v15, /device:TPU:0, one launch (start us, length us, event | category | flops | bytes accessed | tf_op | source)
XLA Modules:
  0.0 25.7 jit_solution(4717858869955117245)
XLA Ops:
  0.0 0.5 %collective-permute-start.1 = (f32[1,2,2,256,256]{4,3,2,1,0:T(8,128)}, f32[1,2,2,256,256]{4,3,2,1,0:T(8,128)S(1)}, u32[]{:S(2)}, u32[]{:S(2)}) collective-permute-start(f32[1,2,2,256,256]{4,3,2,1,0:T(8,128)} %g_hbm.1), channel_id=1, source_target_pairs={{0,16},{16,0},{1,17},{17,1},{2,18},{18,2},{3,19},{19,3},{4,20},{20... | collective-permute-start | bytes 3145736 | tf_op jit(solution)/shard_map/ppermute | solution.py:412
  0.5 3.7 %head_cells.1 = (f32[1,2,2,256,128]{4,3,2,1,0:T(8,128)S(1)}, f32[1,2,2,2,256,128]{5,4,3,2,1,0:T(8,128)S(1)}, f32[1,1,2,256,256]{4,3,2,1,0:T(8,128)S(1)}, f32[1,2...) custom-call(f32[1,2,2,256,256]{4,3,2,1,0:T(8,128)} %g_hbm.1, f32[1,2,2,256,256]{4,3,2,1,0:T(8,128)} %s_hbm.1, ...), custom_call_target="tpu_custom_call" | custom-call | tf_op jit(solution)/shard_map/head_cells/pallas_call | solution.py:199
  4.1 0.1 collective-permute-start
  4.2 0.0 collective-permute-done.1.before_ref
  4.2 2.0 %middle_cells.1 = (f32[1,16,32,128]{3,2,1,0:T(8,128)S(1)}, bf16[1,2,6,256,256]{4,3,2,1,0:T(8,128)(2,1)S(1)}, bf16[1,2,6,256,256]{4,3,2,1,0:T(8,128)(2,1)S(1)}) custom-call(f32[1,2,2,256,256]{4,3,2,1,0:T(8,128)S(1)} %collective-permute-done.1.before_ref, f32[1,2,2,256,128]{4,3,2,1,0:T(8,128)S(1)} %get-tuple-element.13.inner_ref, ...), custom_call_target="tpu_custom_call" | custom-call | flops 402653184 | bytes 262144 | tf_op jit(solution)/shard_map/middle_cells/pallas_call | solution.py:274
  6.2 0.0 collective-permute-done.incoming_ref
  6.3 17.6 %all_to_all.4 = f32[1,16,32,128]{3,2,0,1:T(8,128)} all-to-all(f32[1,16,32,128]{3,2,0,1:T(8,128)S(1)} %bitcast.7), channel_id=1, replica_groups={{15,14,13,12,11,10,9,8,7,6,5,4,3,2,1,0},{31,30,29,28,27,26,25,24,23,22,..., dimensions={1} | all-to-all | bytes 524288 | tf_op jit(solution)/shard_map/all_to_all | solution.py:422
  23.8 1.9 %lag_sums.1 = f32[16,32,128]{2,1,0:T(8,128)} custom-call(f32[16,32,128]{2,1,0:T(8,128)} %bitcast.8), custom_call_target="tpu_custom_call" | custom-call | tf_op jit(solution)/shard_map/lag_sums/pallas_call | solution.py:389
  (1 shorter events, 0.0 us)
Async XLA Ops:
  0.0 4.2 %collective-permute-start.1 = (f32[1,2,2,256,256]{4,3,2,1,0:T(8,128)}, f32[1,2,2,256,256]{4,3,2,1,0:T(8,128)S(1)}, u32[]{:S(2)}, u32[]{:S(2)}) collective-permute-start(f32[1,2,2,256,256]{4,3,2,1,0:T(8,128)} %g_hbm.1), channel_id=1, source_target_pairs={{0,16},{16,0},{1,17},{17,1},{2,18},{18,2},{3,19},{19,3},{4,20},{20... | collective-permute-start | bytes 3145736 | tf_op jit(solution)/shard_map/ppermute | solution.py:412
  4.1 2.1 %collective-permute-start = (f32[1,2,2,256,128]{4,3,2,1,0:T(8,128)S(1)}, f32[1,2,2,256,128]{4,3,2,1,0:T(8,128)S(1)}, u32[]{:S(2)}, u32[]{:S(2)}) collective-permute-start(f32[1,2,2,256,128]{4,3,2,1,0:T(8,128)S(1)} %get-tuple-element.13.inner_ref), channel_id=1, source_target_pairs={{0,16},{16,0},{1,17},{17,1},{2,18},{18,2},{3,19},{19,3},{4,20},{20... | collective-permute-start | bytes 1572872 | tf_op jit(solution)/shard_map/ppermute | solution.py:414

commit v16 on v15

--- a/solution.py
+++ b/solution.py
@@ -146,27 +146,20 @@
         states = [(lead_ref[e, 0], lead_ref[e, 1]) for e in range(energies)]
         for i in range(cells):
             b_copies[i].wait()
-            bridge = parts(bridge_of(i))
-            if i == 0 or i < final:
-                bridge_right = parts(adjoint(bridge_of(i)))
+            bridge = bridge_of(i)
+            bridge_left, bridge_right = parts(bridge), parts(adjoint(bridge))
             for e in range(energies):
-                if i == 0 or i < final:
-                    entered = sandwich(bridge, parts(states[e]), bridge_right)
-                else:
-                    across = product(bridge, parts(green_of(e, i - 1)))
-                    entered = sandwich(parts(across), parts(states[e]), parts(adjoint(across)))
+                entered = sandwich(bridge_left, parts(states[e]), bridge_right)
                 if e == 0:
                     g_copies[i].wait()
                     s_copies[i].wait()
                 inner = plus((s_ref[e, i, 0], s_ref[e, i, 1]), entered)
                 if i == final:
                     put_state(inner_ref.at[e], inner)
-                    continue
-                states[e] = inner
-                if i < final - 1:
+                else:
                     green = green_of(e, i)
                     states[e] = sandwich(parts(green), parts(inner), parts(adjoint(green)))
-                put_state(fresh_ref.at[e, i], states[e])
+                    put_state(fresh_ref.at[e, i], states[e])
 
     @pl.when(position > 0)
     def _():
@@ -230,14 +223,14 @@
     @pl.when(position == 0)
     def _():
         for e in range(energies):
-            for i in range(cells):
+            for i in range(cells)[::-1]:
                 matrix_ref = fresh_ref.at[e, i]
-                if i >= final - 1:
+                if i == final:
                     green = green_ref[e, i, 0], green_ref[e, i, 1]
-                    inner = get_state(inner_ref.at[e] if i == final else matrix_ref)
-                    matrix_ref = state_ref.at[e, i - max(final - 1, 0)]
-                    put_state(matrix_ref, sandwich(parts(green), parts(inner), parts(adjoint(green))))
-                if i == 0 and e == 0:
+                    inner = parts(get_state(inner_ref.at[e]))
+                    matrix_ref = state_ref.at[e]
+                    put_state(matrix_ref, sandwich(parts(green), inner, parts(adjoint(green))))
+                if i == final and e == 0:
                     kept_copy.wait()
                 pick_into(send_ref, e, i, matrix_ref, kept_ref, keep, share_rows)
 
@@ -282,7 +275,7 @@
         out_specs=(vmem,) * 3,
         scratch_shapes=[
             pltpu.SMEM(kept_blocks.shape, jnp.int32),
-            pltpu.VMEM((energies, 2) + inner.shape[1:], F32),
+            pltpu.VMEM(inner.shape, F32),
             pltpu.SemaphoreType.DMA,
         ],
         compiler_params=pltpu.CompilerParams(vmem_limit_bytes=32 << 20),

time: 25.9 us -> 25.5 us (0.985)
  the two profiles are of different devices: /device:TPU:0 before, /device:TPU:1 now
where the time goes in v16:
time: 25.5 us; the launch traced here: 25.1 us
  blocking collectives  15.2 us (60%)
  Pallas kernels  8.39 us (33%)
  starting transfers between devices  1.05 us (4%)
  waiting for transfers between devices  0.41 us (2%)
    all_to_all x1, blocking collectives, per_device(): lax.all_to_all(send, 'energy', split_axis=1, concat_axis=0, axis_index_gr...  15.2 us
    pallas_call x1, Pallas kernels, head(): pl.pallas_call(head_kernel, out_shape=(jax.ShapeDtypeStruct((energies,) +...  3.55 us
    pallas_call x1, Pallas kernels, lag_sums(): pl.pallas_call(functools.partial(lag_kernel, here), out_shape=jax.ShapeDt...  1.87 us
    pallas_call x1, Pallas kernels, tail(): pl.pallas_call(functools.partial(tail_kernel, keep, share_rows, hop, last...  1.85 us
    pallas_call x1, Pallas kernels, middle(): pl.pallas_call(functools.partial(middle_kernel, keep, share_rows), out_sh...  1.12 us
    ppermute x1, starting transfers between devices, per_device(): incoming = lax.ppermute(leaving, 'chain', ring)  0.99 us
  transfers between devices with their start and end apart: 2, of which 1 were waited for; matrix products, arithmetic and copies ran while one was open for 0% of the time, Pallas kernels for 19%

profile of v16, /device:TPU:1, one launch (start us, length us, event | category | flops | bytes accessed | tf_op | source)
XLA Modules:
  0.0 25.1 jit_solution(17980262209458531781)
XLA Ops:
  0.0 0.1 collective-permute-start.1
  0.1 3.5 %head_cells.1 = (f32[1,2,2,256,128]{4,3,2,1,0:T(8,128)S(1)}, f32[1,2,2,2,256,128]{5,4,3,2,1,0:T(8,128)S(1)}, f32[1,1,2,256,256]{4,3,2,1,0:T(8,128)S(1)}, f32[1,2...) custom-call(f32[1,2,2,256,256]{4,3,2,1,0:T(8,128)} %g_hbm.1, f32[1,2,2,256,256]{4,3,2,1,0:T(8,128)} %s_hbm.1, ...), custom_call_target="tpu_custom_call" | custom-call | tf_op jit(solution)/shard_map/head_cells/pallas_call | solution.py:192
  3.6 1.0 %collective-permute-start = (f32[1,2,2,256,128]{4,3,2,1,0:T(8,128)S(1)}, f32[1,2,2,256,128]{4,3,2,1,0:T(8,128)S(1)}, u32[]{:S(2)}, u32[]{:S(2)}) collective-permute-start(f32[1,2,2,256,128]{4,3,2,1,0:T(8,128)S(1)} %get-tuple-element.13.inner_ref), channel_id=1, source_target_pairs={{0,16},{16,0},{1,17},{17,1},{2,18},{18,2},{3,19},{19,3},{4,20},{20... | collective-permute-start | bytes 1572872 | tf_op jit(solution)/shard_map/ppermute | solution.py:407
  4.6 0.0 collective-permute-done.1.before_ref
  4.6 1.1 %middle_cells.1 = (f32[1,16,32,128]{3,2,1,0:T(8,128)S(1)}, bf16[1,2,6,256,256]{4,3,2,1,0:T(8,128)(2,1)S(1)}, bf16[1,2,6,256,256]{4,3,2,1,0:T(8,128)(2,1)S(1)}) custom-call(f32[1,2,2,256,256]{4,3,2,1,0:T(8,128)S(1)} %collective-permute-done.1.before_ref, f32[1,2,2,256,128]{4,3,2,1,0:T(8,128)S(1)} %get-tuple-element.13.inner_ref, ...), custom_call_target="tpu_custom_call" | custom-call | flops 402653184 | bytes 262144 | tf_op jit(solution)/shard_map/middle_cells/pallas_call | solution.py:267
  5.7 0.4 %collective-permute-done.incoming_ref = f32[1,2,2,256,128]{4,3,2,1,0:T(8,128)S(1)} collective-permute-done((f32[1,2,2,256,128]{4,3,2,1,0:T(8,128)S(1)}, f32[1,2,2,256,128]{4,3,2,1,0:T(8,128)S(1)}, u32[]{:S(2)}, u32[]{:S(2)}) %collective-permute-start) | collective-permute-done | bytes 524320 | tf_op jit(solution)/shard_map/ppermute | solution.py:407
  6.1 1.9 %tail_cells.1 = f32[1,16,32,128]{3,2,1,0:T(8,128)S(1)} custom-call(f32[1,2,2,256,128]{4,3,2,1,0:T(8,128)S(1)} %collective-permute-done.incoming_ref, bf16[1,2,6,256,256]{4,3,2,1,0:T(8,128)(2,1)S(1)} %get-tuple-element.18.left_ref, bf16[1,2,6,256,256]{4,3,2,1,0:T(8,128)(2,1)S(1)} %get-tuple-element.19.right_ref, ...), custom_call_target="tpu_custom_call", output_to_operand_aliasing={{}: (5, {})} | custom-call | tf_op jit(solution)/shard_map/tail_cells/pallas_call | solution.py:318
  8.0 15.2 %all_to_all.4 = f32[1,16,32,128]{3,2,0,1:T(8,128)} all-to-all(f32[1,16,32,128]{3,2,0,1:T(8,128)S(1)} %bitcast.7), channel_id=1, replica_groups={{15,14,13,12,11,10,9,8,7,6,5,4,3,2,1,0},{31,30,29,28,27,26,25,24,23,22,..., dimensions={1} | all-to-all | bytes 524288 | tf_op jit(solution)/shard_map/all_to_all | solution.py:415
  23.2 1.9 %lag_sums.1 = f32[16,32,128]{2,1,0:T(8,128)} custom-call(f32[16,32,128]{2,1,0:T(8,128)} %bitcast.8), custom_call_target="tpu_custom_call" | custom-call | tf_op jit(solution)/shard_map/lag_sums/pallas_call | solution.py:382
Async XLA Ops:
  0.0 4.6 %collective-permute-start.1 = (f32[1,2,2,256,256]{4,3,2,1,0:T(8,128)}, f32[1,2,2,256,256]{4,3,2,1,0:T(8,128)S(1)}, u32[]{:S(2)}, u32[]{:S(2)}) collective-permute-start(f32[1,2,2,256,256]{4,3,2,1,0:T(8,128)} %g_hbm.1), channel_id=1, source_target_pairs={{0,16},{16,0},{1,17},{17,1},{2,18},{18,2},{3,19},{19,3},{4,20},{20... | collective-permute-start | bytes 3145736 | tf_op jit(solution)/shard_map/ppermute | solution.py:405
  3.6 2.5 %collective-permute-start = (f32[1,2,2,256,128]{4,3,2,1,0:T(8,128)S(1)}, f32[1,2,2,256,128]{4,3,2,1,0:T(8,128)S(1)}, u32[]{:S(2)}, u32[]{:S(2)}) collective-permute-start(f32[1,2,2,256,128]{4,3,2,1,0:T(8,128)S(1)} %get-tuple-element.13.inner_ref), channel_id=1, source_target_pairs={{0,16},{16,0},{1,17},{17,1},{2,18},{18,2},{3,19},{19,3},{4,20},{20... | collective-permute-start | bytes 1572872 | tf_op jit(solution)/shard_map/ppermute | solution.py:407

commit v17 on v16

--- a/solution.py
+++ b/solution.py
@@ -71,16 +71,16 @@
     return tuple(jnp.concatenate([state_ref[part, group] for group in groups], axis=1) for part in range(2))
 
 
-def block_mask(pattern_ref, cell, size):
+def row_masks(pattern_ref, cell, size):
     nblk = size // BLOCK
-    column = lax.broadcasted_iota(jnp.int32, (BLOCK, size), 1) // BLOCK
+    column = lax.broadcasted_iota(jnp.int32, (1, size), 1) // BLOCK
     rows = []
     for r in range(nblk):
-        row = jnp.zeros((BLOCK, size), F32)
+        row = jnp.zeros((1, size), F32)
         for c in range(nblk):
             row = jnp.where(column == c, pattern_ref[cell, r, c].astype(F32), row)
         rows.append(row)
-    return jnp.concatenate(rows, axis=0)
+    return rows
 
 
 def pick_into(send_ref, e, cell, matrix_ref, kept_ref, keep, share_rows):
@@ -134,8 +134,11 @@
     pattern_copy.wait()
 
     def bridge_of(i):
-        mask = block_mask(pattern_ref, i, size)
-        return b_ref[i, 0] * mask, b_ref[i, 1] * mask
+        rows = row_masks(pattern_ref, i, size)
+        return tuple(
+            jnp.concatenate([b_ref[i, part, r * BLOCK:(r + 1) * BLOCK] * row for r, row in enumerate(rows)], axis=0)
+            for part in range(2)
+        )
 
     def green_of(e, i):
         return green_ref[e, i, 0], green_ref[e, i, 1]

time: 25.5 us -> 25.5 us (level)
  no operation moved by 1% of the time
where the time goes in v17:
time: 25.5 us; the launch traced here: 25.1 us
  blocking collectives  15.2 us (60%)
  Pallas kernels  8.39 us (33%)
  starting transfers between devices  1.05 us (4%)
  waiting for transfers between devices  0.41 us (2%)
    all_to_all x1, blocking collectives, per_device(): lax.all_to_all(send, 'energy', split_axis=1, concat_axis=0, axis_index_gr...  15.2 us
    pallas_call x1, Pallas kernels, head(): pl.pallas_call(head_kernel, out_shape=(jax.ShapeDtypeStruct((energies,) +...  3.55 us
    pallas_call x1, Pallas kernels, lag_sums(): pl.pallas_call(functools.partial(lag_kernel, here), out_shape=jax.ShapeDt...  1.87 us
    pallas_call x1, Pallas kernels, tail(): pl.pallas_call(functools.partial(tail_kernel, keep, share_rows, hop, last...  1.85 us
    pallas_call x1, Pallas kernels, middle(): pl.pallas_call(functools.partial(middle_kernel, keep, share_rows), out_sh...  1.12 us
    ppermute x1, starting transfers between devices, per_device(): incoming = lax.ppermute(leaving, 'chain', ring)  0.99 us
  transfers between devices with their start and end apart: 2, of which 1 were waited for; matrix products, arithmetic and copies ran while one was open for 0% of the time, Pallas kernels for 19%

profile of v17, /device:TPU:1, one launch (start us, length us, event | category | flops | bytes accessed | tf_op | source)
XLA Modules:
  0.0 25.1 jit_solution(14218529402583427227)
XLA Ops:
  0.0 0.1 collective-permute-start.1
  0.1 3.5 %head_cells.1 = (f32[1,2,2,256,128]{4,3,2,1,0:T(8,128)S(1)}, f32[1,2,2,2,256,128]{5,4,3,2,1,0:T(8,128)S(1)}, f32[1,1,2,256,256]{4,3,2,1,0:T(8,128)S(1)}, f32[1,2...) custom-call(f32[1,2,2,256,256]{4,3,2,1,0:T(8,128)} %g_hbm.1, f32[1,2,2,256,256]{4,3,2,1,0:T(8,128)} %s_hbm.1, ...), custom_call_target="tpu_custom_call" | custom-call | tf_op jit(solution)/shard_map/head_cells/pallas_call | solution.py:195
  3.6 1.0 %collective-permute-start = (f32[1,2,2,256,128]{4,3,2,1,0:T(8,128)S(1)}, f32[1,2,2,256,128]{4,3,2,1,0:T(8,128)S(1)}, u32[]{:S(2)}, u32[]{:S(2)}) collective-permute-start(f32[1,2,2,256,128]{4,3,2,1,0:T(8,128)S(1)} %get-tuple-element.13.inner_ref), channel_id=1, source_target_pairs={{0,16},{16,0},{1,17},{17,1},{2,18},{18,2},{3,19},{19,3},{4,20},{20... | collective-permute-start | bytes 1572872 | tf_op jit(solution)/shard_map/ppermute | solution.py:410
  4.6 0.0 collective-permute-done.1.before_ref
  4.6 1.1 %middle_cells.1 = (f32[1,16,32,128]{3,2,1,0:T(8,128)S(1)}, bf16[1,2,6,256,256]{4,3,2,1,0:T(8,128)(2,1)S(1)}, bf16[1,2,6,256,256]{4,3,2,1,0:T(8,128)(2,1)S(1)}) custom-call(f32[1,2,2,256,256]{4,3,2,1,0:T(8,128)S(1)} %collective-permute-done.1.before_ref, f32[1,2,2,256,128]{4,3,2,1,0:T(8,128)S(1)} %get-tuple-element.13.inner_ref, ...), custom_call_target="tpu_custom_call" | custom-call | flops 402653184 | bytes 262144 | tf_op jit(solution)/shard_map/middle_cells/pallas_call | solution.py:270
  5.7 0.4 %collective-permute-done.incoming_ref = f32[1,2,2,256,128]{4,3,2,1,0:T(8,128)S(1)} collective-permute-done((f32[1,2,2,256,128]{4,3,2,1,0:T(8,128)S(1)}, f32[1,2,2,256,128]{4,3,2,1,0:T(8,128)S(1)}, u32[]{:S(2)}, u32[]{:S(2)}) %collective-permute-start) | collective-permute-done | bytes 524320 | tf_op jit(solution)/shard_map/ppermute | solution.py:410
  6.1 1.9 %tail_cells.1 = f32[1,16,32,128]{3,2,1,0:T(8,128)S(1)} custom-call(f32[1,2,2,256,128]{4,3,2,1,0:T(8,128)S(1)} %collective-permute-done.incoming_ref, bf16[1,2,6,256,256]{4,3,2,1,0:T(8,128)(2,1)S(1)} %get-tuple-element.18.left_ref, bf16[1,2,6,256,256]{4,3,2,1,0:T(8,128)(2,1)S(1)} %get-tuple-element.19.right_ref, ...), custom_call_target="tpu_custom_call", output_to_operand_aliasing={{}: (5, {})} | custom-call | tf_op jit(solution)/shard_map/tail_cells/pallas_call | solution.py:321
  8.0 15.2 %all_to_all.4 = f32[1,16,32,128]{3,2,0,1:T(8,128)} all-to-all(f32[1,16,32,128]{3,2,0,1:T(8,128)S(1)} %bitcast.7), channel_id=1, replica_groups={{15,14,13,12,11,10,9,8,7,6,5,4,3,2,1,0},{31,30,29,28,27,26,25,24,23,22,..., dimensions={1} | all-to-all | bytes 524288 | tf_op jit(solution)/shard_map/all_to_all | solution.py:418
  23.2 1.9 %lag_sums.1 = f32[16,32,128]{2,1,0:T(8,128)} custom-call(f32[16,32,128]{2,1,0:T(8,128)} %bitcast.8), custom_call_target="tpu_custom_call" | custom-call | tf_op jit(solution)/shard_map/lag_sums/pallas_call | solution.py:385
Async XLA Ops:
  0.0 4.6 %collective-permute-start.1 = (f32[1,2,2,256,256]{4,3,2,1,0:T(8,128)}, f32[1,2,2,256,256]{4,3,2,1,0:T(8,128)S(1)}, u32[]{:S(2)}, u32[]{:S(2)}) collective-permute-start(f32[1,2,2,256,256]{4,3,2,1,0:T(8,128)} %g_hbm.1), channel_id=1, source_target_pairs={{0,16},{16,0},{1,17},{17,1},{2,18},{18,2},{3,19},{19,3},{4,20},{20... | collective-permute-start | bytes 3145736 | tf_op jit(solution)/shard_map/ppermute | solution.py:408
  3.6 2.5 %collective-permute-start = (f32[1,2,2,256,128]{4,3,2,1,0:T(8,128)S(1)}, f32[1,2,2,256,128]{4,3,2,1,0:T(8,128)S(1)}, u32[]{:S(2)}, u32[]{:S(2)}) collective-permute-start(f32[1,2,2,256,128]{4,3,2,1,0:T(8,128)S(1)} %get-tuple-element.13.inner_ref), channel_id=1, source_target_pairs={{0,16},{16,0},{1,17},{17,1},{2,18},{18,2},{3,19},{19,3},{4,20},{20... | collective-permute-start | bytes 1572872 | tf_op jit(solution)/shard_map/ppermute | solution.py:410

commit v18 on v16

--- a/solution.py
+++ b/solution.py
@@ -387,7 +387,7 @@
         scratch_shapes=[
             pltpu.VMEM((LAGS, double_rows, lanes), F32),
             pltpu.VMEM((2, energies, rows, lanes), F32),
-            pltpu.SemaphoreType.DMA((4,)),
+            pltpu.SemaphoreType.DMA((8,)),
         ],
         name="lag_sums",
     )(owned)

time: 25.5 us -> 25.5 us (level)
  no operation moved by 1% of the time
where the time goes in v18:
time: 25.5 us; the launch traced here: 25.1 us
  blocking collectives  15.2 us (60%)
  Pallas kernels  8.41 us (33%)
  starting transfers between devices  1.05 us (4%)
  waiting for transfers between devices  0.41 us (2%)
    all_to_all x1, blocking collectives, per_device(): lax.all_to_all(send, 'energy', split_axis=1, concat_axis=0, axis_index_gr...  15.2 us
    pallas_call x1, Pallas kernels, head(): pl.pallas_call(head_kernel, out_shape=(jax.ShapeDtypeStruct((energies,) +...  3.55 us
    pallas_call x1, Pallas kernels, lag_sums(): pl.pallas_call(functools.partial(lag_kernel, here), out_shape=jax.ShapeDt...  1.89 us
    pallas_call x1, Pallas kernels, tail(): pl.pallas_call(functools.partial(tail_kernel, keep, share_rows, hop, last...  1.85 us
    pallas_call x1, Pallas kernels, middle(): pl.pallas_call(functools.partial(middle_kernel, keep, share_rows), out_sh...  1.12 us
    ppermute x1, starting transfers between devices, per_device(): incoming = lax.ppermute(leaving, 'chain', ring)  0.99 us
  transfers between devices with their start and end apart: 2, of which 1 were waited for; matrix products, arithmetic and copies ran while one was open for 0% of the time, Pallas kernels for 19%

profile of v18, /device:TPU:1, one launch (start us, length us, event | category | flops | bytes accessed | tf_op | source)
XLA Modules:
  0.0 25.1 jit_solution(1992054539088901669)
XLA Ops:
  0.0 0.1 collective-permute-start.1
  0.1 3.5 %head_cells.1 = (f32[1,2,2,256,128]{4,3,2,1,0:T(8,128)S(1)}, f32[1,2,2,2,256,128]{5,4,3,2,1,0:T(8,128)S(1)}, f32[1,1,2,256,256]{4,3,2,1,0:T(8,128)S(1)}, f32[1,2...) custom-call(f32[1,2,2,256,256]{4,3,2,1,0:T(8,128)} %g_hbm.1, f32[1,2,2,256,256]{4,3,2,1,0:T(8,128)} %s_hbm.1, ...), custom_call_target="tpu_custom_call" | custom-call | tf_op jit(solution)/shard_map/head_cells/pallas_call | solution.py:192
  3.6 1.0 %collective-permute-start = (f32[1,2,2,256,128]{4,3,2,1,0:T(8,128)S(1)}, f32[1,2,2,256,128]{4,3,2,1,0:T(8,128)S(1)}, u32[]{:S(2)}, u32[]{:S(2)}) collective-permute-start(f32[1,2,2,256,128]{4,3,2,1,0:T(8,128)S(1)} %get-tuple-element.13.inner_ref), channel_id=1, source_target_pairs={{0,16},{16,0},{1,17},{17,1},{2,18},{18,2},{3,19},{19,3},{4,20},{20... | collective-permute-start | bytes 1572872 | tf_op jit(solution)/shard_map/ppermute | solution.py:407
  4.6 0.0 collective-permute-done.1.before_ref
  4.6 1.1 %middle_cells.1 = (f32[1,16,32,128]{3,2,1,0:T(8,128)S(1)}, bf16[1,2,6,256,256]{4,3,2,1,0:T(8,128)(2,1)S(1)}, bf16[1,2,6,256,256]{4,3,2,1,0:T(8,128)(2,1)S(1)}) custom-call(f32[1,2,2,256,256]{4,3,2,1,0:T(8,128)S(1)} %collective-permute-done.1.before_ref, f32[1,2,2,256,128]{4,3,2,1,0:T(8,128)S(1)} %get-tuple-element.13.inner_ref, ...), custom_call_target="tpu_custom_call" | custom-call | flops 402653184 | bytes 262144 | tf_op jit(solution)/shard_map/middle_cells/pallas_call | solution.py:267
  5.7 0.4 %collective-permute-done.incoming_ref = f32[1,2,2,256,128]{4,3,2,1,0:T(8,128)S(1)} collective-permute-done((f32[1,2,2,256,128]{4,3,2,1,0:T(8,128)S(1)}, f32[1,2,2,256,128]{4,3,2,1,0:T(8,128)S(1)}, u32[]{:S(2)}, u32[]{:S(2)}) %collective-permute-start) | collective-permute-done | bytes 524320 | tf_op jit(solution)/shard_map/ppermute | solution.py:407
  6.1 1.9 %tail_cells.1 = f32[1,16,32,128]{3,2,1,0:T(8,128)S(1)} custom-call(f32[1,2,2,256,128]{4,3,2,1,0:T(8,128)S(1)} %collective-permute-done.incoming_ref, bf16[1,2,6,256,256]{4,3,2,1,0:T(8,128)(2,1)S(1)} %get-tuple-element.18.left_ref, bf16[1,2,6,256,256]{4,3,2,1,0:T(8,128)(2,1)S(1)} %get-tuple-element.19.right_ref, ...), custom_call_target="tpu_custom_call", output_to_operand_aliasing={{}: (5, {})} | custom-call | tf_op jit(solution)/shard_map/tail_cells/pallas_call | solution.py:318
  8.0 15.2 %all_to_all.4 = f32[1,16,32,128]{3,2,0,1:T(8,128)} all-to-all(f32[1,16,32,128]{3,2,0,1:T(8,128)S(1)} %bitcast.7), channel_id=1, replica_groups={{15,14,13,12,11,10,9,8,7,6,5,4,3,2,1,0},{31,30,29,28,27,26,25,24,23,22,..., dimensions={1} | all-to-all | bytes 524288 | tf_op jit(solution)/shard_map/all_to_all | solution.py:415
  23.2 1.9 %lag_sums.1 = f32[16,32,128]{2,1,0:T(8,128)} custom-call(f32[16,32,128]{2,1,0:T(8,128)} %bitcast.8), custom_call_target="tpu_custom_call" | custom-call | tf_op jit(solution)/shard_map/lag_sums/pallas_call | solution.py:382
Async XLA Ops:
  0.0 4.6 %collective-permute-start.1 = (f32[1,2,2,256,256]{4,3,2,1,0:T(8,128)}, f32[1,2,2,256,256]{4,3,2,1,0:T(8,128)S(1)}, u32[]{:S(2)}, u32[]{:S(2)}) collective-permute-start(f32[1,2,2,256,256]{4,3,2,1,0:T(8,128)} %g_hbm.1), channel_id=1, source_target_pairs={{0,16},{16,0},{1,17},{17,1},{2,18},{18,2},{3,19},{19,3},{4,20},{20... | collective-permute-start | bytes 3145736 | tf_op jit(solution)/shard_map/ppermute | solution.py:405
  3.6 2.5 %collective-permute-start = (f32[1,2,2,256,128]{4,3,2,1,0:T(8,128)S(1)}, f32[1,2,2,256,128]{4,3,2,1,0:T(8,128)S(1)}, u32[]{:S(2)}, u32[]{:S(2)}) collective-permute-start(f32[1,2,2,256,128]{4,3,2,1,0:T(8,128)S(1)} %get-tuple-element.13.inner_ref), channel_id=1, source_target_pairs={{0,16},{16,0},{1,17},{17,1},{2,18},{18,2},{3,19},{19,3},{4,20},{20... | collective-permute-start | bytes 1572872 | tf_op jit(solution)/shard_map/ppermute | solution.py:407
